TPU v7x, 128 devices: a whole 4x4x4 slice. The times are simulated.
128 devices in a mesh: rows: 4 (over y), cols: 32 (over x, z, core).
Axes of the slice: x: 4, y: 4, z: 4, core: 2. Of those that a mesh axis runs over, the one named last changes fastest.
Arguments:
- object_field: bfloat16 [2, 4096, 4096], P(None, 'rows', 'cols'), may hold values from -6 to 6
- probe_mode_stack: float32 [2, 4, 256, 256], replicated, may hold values from -6 to 6
- measured: bfloat16 [4, 256, 256, 256], P('rows', 'cols'), may hold values from 0.25 to 3
- corner_row: int32 [4, 256], P('rows', 'cols'), may hold values from 0 to 4095, as said below
- corner_col: int32 [4, 256], P('rows', 'cols'), may hold values from 0 to 4095, as said below
- count: int32 [4, 32], P('rows', 'cols'), may hold values from 1 to 8, as said below
Outputs:
- object_grad: float32 [2, 4096, 4096], P(None, 'rows', 'cols')
- probe_grad: float32 [2, 4, 256, 256], replicated
Inputs may be any that keep to these rules, and one draw needn't show every extreme that they name: `corner_row`: the corner of slot s of tile (a, b) lies in that tile: rows a * 1024 to (a + 1) * 1024 - 1, columns b * 128 to (b + 1) * 128 - 1. `corner_col`: same tile as corner_row. `count`: some tile has all 8 slots live.
All inputs are finite; a program needn't handle non-finite values.
Results may differ from a plain program's by a relative error of at most 0.004.
Values may be sent and summed in bfloat16 or wider, within the bound.
No kernel may reach another device: no remote copies, remote signals or barrier semaphores. Data moves between devices by JAX's collectives and lax.ppermute only.
A program may use at most 64 MiB of HBM per device.

v0:
```python
import functools

import jax
import jax.numpy as jnp
import ml_dtypes
import numpy as np
from jax import lax
from jax.experimental import pallas as pl
from jax.experimental.pallas import tpu as pltpu
from jax.sharding import PartitionSpec as P

F32 = jnp.float32
BF16 = jnp.bfloat16
LANES = 128
CHUNK = 16
BLOCK = 64


def dft_tables(win):
    half = win // 2
    k = np.arange(win)[:, None]
    j = np.arange(win)[None, :]
    angle = (k * j % win).astype(np.float64) * (2.0 * np.pi / win)
    re = np.cos(angle) / np.sqrt(win)
    im = -np.sin(angle) / np.sqrt(win)
    tables = []
    for parity in range(2):
        cr = re[parity::2, :half]
        ci = im[parity::2, :half]
        tables.append(np.block([[cr, -ci], [ci, cr]]))
    forward = np.stack(tables)
    backward = np.stack([t.T for t in tables])
    order = np.concatenate([np.arange(0, win, 2), np.arange(1, win, 2)])
    permute = np.zeros((win, win))
    permute[np.arange(win), order] = 1.0
    both = np.stack([permute, permute.T])
    cast = lambda a: a.astype(ml_dtypes.bfloat16)
    return cast(forward), cast(backward), cast(both)


def slots_kernel(
    info, fwd, bwd, probe, meas, own, own_low, nxt, nxt_low, sec, sec_low,
    g_own, g_next, g_next_low, g_sec, acc_keep, acc_send,
    ext, mid, acc, owin, xs, hb, gb, kb,
):
    slots = meas.shape[0]
    live = info[2 * slots]
    core = info[2 * slots + 1]
    modes = probe.shape[1]
    win = probe.shape[2]
    half = win // 2
    blocks = win // BLOCK
    tile_rows = own.shape[1]
    sums = (g_own, mid, g_sec)

    for c in range(2):
        for t, (top, bottom) in enumerate(((own, own_low), (nxt, nxt_low), (sec, sec_low))):
            ext[c, t, :tile_rows, :] = top[c].astype(F32)
            ext[c, t, tile_rows:, :] = bottom[c].astype(F32)
    for ref in sums + (acc,):
        ref[...] = jnp.zeros_like(ref)

    sides = (slice(0, LANES), slice(LANES, 2 * LANES))
    lane = lax.broadcasted_iota(jnp.int32, (CHUNK, LANES), 1)

    def pair_of_slots(pair, _):
        whole = 2 * pair + 1 < live
        slot = (2 * pair, jnp.where(whole, 2 * pair + 1, 2 * pair))
        weight = (None, jnp.where(whole, 1.0, 0.0).astype(F32))
        row = [info[s] for s in slot]
        col = [info[slots + s] for s in slot]
        left_shift = [lax.rem(LANES - c, LANES) for c in col]
        keep_left = [lane < LANES - c for c in col]
        keep_right = [lane >= c for c in col]

        for q in range(2):
            for at in range(0, win, CHUNK):
                for c in range(2):
                    parts = [
                        pltpu.roll(ext[c, t, pl.ds(row[q] + at, CHUNK), :], left_shift[q], 1) for t in range(3)
                    ]
                    for h in range(2):
                        owin[q, c, h, at : at + CHUNK, :] = jnp.where(keep_left[q], parts[h], parts[h + 1])

        for m in range(modes):
            for at in range(0, half, CHUNK):
                for h in range(2):
                    psi = ([], [])
                    for rows in (slice(at, at + CHUNK), slice(half + at, half + at + CHUNK)):
                        p_re = probe[0, m, rows, sides[h]]
                        p_im = probe[1, m, rows, sides[h]]
                        for q in range(2):
                            o_re = owin[q, 0, h, rows, :]
                            o_im = owin[q, 1, h, rows, :]
                            psi[q].append((p_re * o_re - p_im * o_im, p_re * o_im + p_im * o_re))
                    for q in range(2):
                        for c in range(2):
                            rows = slice(c * half + at, c * half + at + CHUNK)
                            xs[q, m, 0, rows, sides[h]] = (psi[q][0][c] + psi[q][1][c]).astype(BF16)
                            xs[q, m, 1, rows, sides[h]] = (psi[q][0][c] - psi[q][1][c]).astype(BF16)
            for q in range(2):
                for rp in range(2):
                    v = jnp.dot(fwd[rp], xs[q, m, rp], preferred_element_type=F32)
                    v = (
                        (v[:, :half] + v[:, half:]).astype(BF16),
                        (v[:, :half] - v[:, half:]).astype(BF16),
                    )
                    for pc in range(2):
                        for at in range(0, half, BLOCK):
                            for c in range(2):
                                hb[
                                    q, pc, (rp * half + at) // BLOCK, m * BLOCK : (m + 1) * BLOCK, sides[c]
                                ] = v[pc][c * half + at : c * half + at + BLOCK]

        for rb in range(blocks):
            for pc in range(2):
                for q in range(2):
                    field = jnp.dot(hb[q, pc, rb], bwd[pc], preferred_element_type=F32)
                    for at in range(0, BLOCK, CHUNK):
                        part = [field[m * BLOCK + at : m * BLOCK + at + CHUNK] for m in range(modes)]
                        total = 1.0
                        for f in part:
                            total = total + (f[:, :half] * f[:, :half] + f[:, half:] * f[:, half:])
                        f_row = rb * BLOCK + at
                        factor = 1.0 - meas[slot[q], f_row : f_row + CHUNK, sides[pc]].astype(F32) * lax.rsqrt(total)
                        if q == 1:
                            factor = factor * weight[q]
                        rp, f_row = divmod(f_row, half)
                        for m in range(modes):
                            for c in range(2):
                                gb[q, m, rp, c * half + f_row : c * half + f_row + CHUNK, sides[pc]] = (
                                    part[m][:, sides[c]] * factor
                                ).astype(BF16)

        for m in range(modes):
            for q in range(2):
                v0 = jnp.dot(bwd[0], gb[q, m, 0], preferred_element_type=F32)
                v1 = jnp.dot(bwd[1], gb[q, m, 1], preferred_element_type=F32)
                for side, v in enumerate(((v0 + v1).astype(BF16), (v0 - v1).astype(BF16))):
                    for at in range(0, half, BLOCK):
                        for pc in range(2):
                            for c in range(2):
                                kb[
                                    q, pc, (side * half + at) // BLOCK, m * BLOCK : (m + 1) * BLOCK, sides[c]
                                ] = v[c * half + at : c * half + at + BLOCK, sides[pc]]

        for rb in range(blocks):
            w = [
                [jnp.dot(kb[q, pc, rb], fwd[pc], preferred_element_type=F32) for pc in range(2)]
                for q in range(2)
            ]
            for at in range(0, BLOCK, CHUNK):
                rows = slice(rb * BLOCK + at, rb * BLOCK + at + CHUNK)
                g = [[[None, None], [None, None]] for q in range(2)]
                for h in range(2):
                    o = [[owin[q, c, h, rows, :] for c in range(2)] for q in range(2)]
                    for m in range(modes):
                        p_re = probe[0, m, rows, sides[h]]
                        p_im = probe[1, m, rows, sides[h]]
                        terms = []
                        for q in range(2):
                            w0, w1 = (v[m * BLOCK + at : m * BLOCK + at + CHUNK] for v in w[q])
                            chi = w0 + w1 if h == 0 else w0 - w1
                            c_re = chi[:, :half]
                            c_im = chi[:, half:]
                            t_re = p_re * c_re + p_im * c_im
                            t_im = p_re * c_im - p_im * c_re
                            g[q][0][h] = t_re if m == 0 else g[q][0][h] + t_re
                            g[q][1][h] = t_im if m == 0 else g[q][1][h] + t_im
                            o_re, o_im = o[q]
                            terms.append((o_re * c_re + o_im * c_im, o_re * c_im - o_im * c_re))
                        for c in range(2):
                            acc[c, m, rows, sides[h]] += terms[0][c] + terms[1][c]
                for q in range(2):
                    for c in range(2):
                        left = pltpu.roll(g[q][c][0], col[q], 1)
                        right = pltpu.roll(g[q][c][1], col[q], 1)
                        zero = jnp.zeros_like(left)
                        spread = (
                            jnp.where(keep_right[q], left, zero),
                            jnp.where(keep_right[q], right, left),
                            jnp.where(keep_right[q], zero, right),
                        )
                        for t in range(3):
                            sums[t][c, pl.ds(row[q] + rows.start, CHUNK), :] += spread[t]
        return 0

    lax.fori_loop(0, lax.div(live + 1, 2), pair_of_slots, 0)

    g_next[...] = mid[:, :tile_rows, :].astype(BF16)
    g_next_low[...] = mid[:, tile_rows:, :].astype(BF16)
    for m in range(modes):
        for at in range(0, win, 8):
            for h in range(2):
                to = (m * win + at) * 2 + 8 * h
                acc_keep[to : to + 8, :] = acc[core, m, at : at + 8, h * LANES : (h + 1) * LANES]
            pair = acc[1 - core, m, at : at + 8, :]
            to = (m * win + at) * 2
            acc_send[to : to + 16, :] = jnp.concatenate([pair[:, :LANES], pair[:, LANES:]], axis=0).astype(BF16)


def prepare_kernel(fwd, bwd, perm, probe, meas, fwd_out, bwd_out, probe_out, meas_out, swaps, raw, sems):
    copies = [
        pltpu.make_async_copy(source, target, sems.at[i])
        for i, (source, target) in enumerate(
            ((perm, swaps), (meas.at[0], raw), (probe, probe_out), (fwd, fwd_out), (bwd, bwd_out))
        )
    ]
    for copy in copies:
        copy.start()
    copies[0].wait()
    copies[1].wait()
    for s in range(raw.shape[0]):
        rows_done = jnp.dot(swaps[0], raw[s], preferred_element_type=F32).astype(BF16)
        meas_out[s] = jnp.dot(rows_done, swaps[1], preferred_element_type=F32).astype(BF16)
    for copy in copies[2:]:
        copy.wait()


def prepare(probe, measured):
    slots, win = measured.shape[1:3]
    fwd, bwd, perm = dft_tables(win)
    return pl.pallas_call(
        prepare_kernel,
        in_specs=[pl.BlockSpec(memory_space=pltpu.HBM)] * 5,
        out_specs=[pl.BlockSpec(memory_space=pltpu.VMEM)] * 4,
        out_shape=[
            jax.ShapeDtypeStruct(fwd.shape, BF16),
            jax.ShapeDtypeStruct(bwd.shape, BF16),
            jax.ShapeDtypeStruct(probe.shape, F32),
            jax.ShapeDtypeStruct(measured.shape[1:], BF16),
        ],
        scratch_shapes=[
            pltpu.VMEM(perm.shape, BF16),
            pltpu.VMEM(measured.shape[1:], BF16),
            pltpu.SemaphoreType.DMA((5,)),
        ],
        cost_estimate=pl.CostEstimate(flops=4 * slots * win**3, bytes_accessed=8 << 20, transcendentals=0),
        compiler_params=pltpu.CompilerParams(vmem_limit_bytes=8 * 1024 * 1024),
        name="prepare",
    )(jnp.asarray(fwd), jnp.asarray(bwd), jnp.asarray(perm), probe, measured)


def run_slots(info, fwd, bwd, probe, measured, own, own_low, nxt, nxt_low, sec, sec_low):
    tile_rows, tile_cols = own.shape[1:]
    modes, win = probe.shape[1:3]
    tall = (2, tile_rows + win, tile_cols)
    flat = (2 * modes * win, LANES)
    blocks = (2, win // BLOCK, modes * BLOCK, win)
    vmem = pl.BlockSpec(memory_space=pltpu.VMEM)
    return pl.pallas_call(
        slots_kernel,
        in_specs=[pl.BlockSpec(memory_space=pltpu.SMEM)] + [vmem] * 10,
        out_specs=[vmem] * 6,
        out_shape=[
            jax.ShapeDtypeStruct(tall, F32),
            jax.ShapeDtypeStruct(own.shape, BF16),
            jax.ShapeDtypeStruct(own_low.shape, BF16),
            jax.ShapeDtypeStruct(tall, F32),
            jax.ShapeDtypeStruct(flat, F32),
            jax.ShapeDtypeStruct(flat, BF16),
        ],
        scratch_shapes=[
            pltpu.VMEM((2, 3) + tall[1:], F32),
            pltpu.VMEM(tall, F32),
            pltpu.VMEM((2, modes, win, win), F32),
            pltpu.VMEM((2, 2, 2, win, LANES), F32),
            pltpu.VMEM((2, modes, 2, win, win), BF16),
            pltpu.VMEM((2,) + blocks, BF16),
            pltpu.VMEM((2, modes, 2, win, win), BF16),
            pltpu.VMEM((2,) + blocks, BF16),
        ],
        compiler_params=pltpu.CompilerParams(vmem_limit_bytes=32 * 1024 * 1024),
        name="slots",
    )(info, fwd, bwd, probe, measured, own, own_low, nxt, nxt_low, sec, sec_low)


def moved(value, target):
    n_rows = lax.axis_size("rows")
    n_cols = lax.axis_size("cols")
    pairs = []
    for a in range(n_rows):
        for b in range(n_cols):
            to_a, to_b = target(a, b)
            if 0 <= to_a < n_rows and 0 <= to_b < n_cols:
                pairs.append((a * n_cols + b, to_a * n_cols + to_b))
    return lax.ppermute(value, ("rows", "cols"), pairs)


def swap_cores(value):
    return moved(value, lambda a, b: (a, b ^ 1))


def local(object_field, probe_mode_stack, measured, corner_row, corner_col, count):
    tile_rows, tile_cols = object_field.shape[1:]
    modes, win = probe_mode_stack.shape[1:3]
    slot_count = measured.shape[1]
    devices = lax.axis_size("rows") * lax.axis_size("cols")
    col_at = lax.axis_index("cols")
    core = lax.rem(col_at, 2)

    top = object_field[:, :win, :]
    sec = moved(object_field, lambda a, b: (a, b - 2))
    sec_low = moved(top, lambda a, b: (a - 1, b - 2))
    own_low = moved(top, lambda a, b: (a - 1, b))
    prepared, sec = lax.optimization_barrier((prepare(probe_mode_stack, measured), sec))
    nxt_low = swap_cores(jnp.where(core == 0, sec_low, own_low))
    nxt = swap_cores(jnp.where(core == 0, sec, object_field))
    info = jnp.concatenate(
        [
            corner_row[0] - lax.axis_index("rows") * tile_rows,
            corner_col[0] - col_at * tile_cols,
            count[0],
            core[None],
        ]
    )
    g_own, g_next, g_next_low, g_sec, acc_keep, acc_send = run_slots(
        info, *prepared, object_field, own_low, nxt, nxt_low, sec, sec_low
    )

    acc_got = swap_cores(acc_send)
    near = swap_cores(g_next)
    chip_sum = (acc_keep + acc_got.astype(F32)).astype(BF16)
    chip_sum, near, near_low = lax.optimization_barrier((chip_sum, near, g_next_low))
    near = jnp.concatenate([near, swap_cores(near_low)], axis=1).astype(F32)
    none = jnp.zeros_like(near)
    outward = (g_sec + jnp.where(core == 0, near, none)).astype(BF16)
    far = moved(outward, lambda a, b: (a, b + 2))
    total = g_own + jnp.where(core == 1, near, none) + far.astype(F32)
    rim = moved(total[:, tile_rows:].astype(BF16), lambda a, b: (a + 1, b))

    groups = [[i for i in range(devices) if i % 2 == c] for c in range(2)]
    exchange = functools.partial(
        lax.all_to_all, axis_name=("rows", "cols"), split_axis=0, concat_axis=0,
        axis_index_groups=groups, tiled=True,
    )
    share = exchange(chip_sum.reshape(devices // 2, -1, LANES))
    scale = 1.0 / jnp.sqrt(jnp.float32(devices * slot_count))
    share = (jnp.sum(share.astype(F32), axis=0) * scale).astype(BF16)
    mine = exchange(jnp.broadcast_to(share[None], (devices // 2,) + share.shape))
    mine, rim = lax.optimization_barrier((mine, rim))
    mine = mine.reshape(-1, LANES)
    part = lax.broadcasted_iota(jnp.int32, (2,) + mine.shape, 0)
    probe_grad = jnp.where(part == core, mine[None], swap_cores(mine)[None]).astype(F32)
    probe_grad = probe_grad.reshape(2, modes, win // 8, 2, 8, LANES).transpose(0, 1, 2, 4, 3, 5)
    probe_grad = probe_grad.reshape(2, modes, win, win)

    object_grad = total[:, :tile_rows] + jnp.pad(rim.astype(F32), ((0, 0), (0, tile_rows - win), (0, 0)))
    return (object_grad, probe_grad)


def solution(mesh):
    placed = (
        P(None, "rows", "cols"),
        P(),
        P("rows", "cols", None, None),
        P("rows", "cols"),
        P("rows", "cols"),
        P("rows", "cols"),
    )
    return jax.shard_map(
        local, mesh=mesh, in_specs=placed, out_specs=(P(None, "rows", "cols"), P()), check_vma=False
    )
```

profile of v0, /device:TPU:1, one launch (start us, length us, event | category | flops | bytes accessed | tf_op | source)
XLA Modules:
  0.0 96.4 jit_solution(2580299578002281030)
XLA Ops:
  0.6 1.3 %collective-permute-start = (bf16[2,1024,128]{2,1,0:T(8,128)(2,1)}, bf16[2,1024,128]{2,1,0:T(8,128)(2,1)S(1)}, u32[]{:S(2)}, u32[]{:S(2)}) collective-permute-start(bf16[2,1024,128]{2,1,0:T(8,128)(2,1)} %own.1), channel_id=1, source_target_pairs={{2,0},{3,1},{4,2},{5,3},{6,4},{7,5},{8,6},{9,7},{10,8},{11,9},{12,... | collective-permute-start | bytes 1572872 | tf_op jit(solution)/shard_map/ppermute | solution.py:287
  1.9 0.9 slice.10
  2.9 1.3 %collective-permute-start.1 = (bf16[2,256,128]{2,1,0:T(8,128)(2,1)S(1)}, bf16[2,256,128]{2,1,0:T(8,128)(2,1)S(1)}, u32[]{:S(2)}, u32[]{:S(2)}) collective-permute-start(bf16[2,256,128]{2,1,0:T(8,128)(2,1)S(1)} %slice.10), channel_id=1, source_target_pairs={{32,0},{33,1},{34,2},{35,3},{36,4},{37,5},{38,6},{39,7},{40,8},{41... | collective-permute-start | bytes 393224 | tf_op jit(solution)/shard_map/ppermute | solution.py:287
  4.2 1.3 %collective-permute-start.3 = (bf16[2,256,128]{2,1,0:T(8,128)(2,1)S(1)}, bf16[2,256,128]{2,1,0:T(8,128)(2,1)S(1)}, u32[]{:S(2)}, u32[]{:S(2)}) collective-permute-start(bf16[2,256,128]{2,1,0:T(8,128)(2,1)S(1)} %slice.10), channel_id=1, source_target_pairs={{34,0},{35,1},{36,2},{37,3},{38,4},{39,5},{40,6},{41,7},{42,8},{43... | collective-permute-start | bytes 393224 | tf_op jit(solution)/shard_map/ppermute | solution.py:287
  5.5 0.0 copy-start.1
  5.5 1.6 %copy-done.1 = f32[2,4,256,256]{3,2,1,0:T(8,128)S(1)} copy-done((f32[2,4,256,256]{3,2,1,0:T(8,128)S(1)}, f32[2,4,256,256]{3,2,1,0:T(8,128)}, u32[]{:S(2)}) %copy-start.1) | copy-done | bytes 2097176
  7.1 0.0 copy-start.2
  7.1 1.2 %copy-done.2 = bf16[1,8,256,256]{3,2,1,0:T(8,128)(2,1)S(1)} copy-done((bf16[1,8,256,256]{3,2,1,0:T(8,128)(2,1)S(1)}, bf16[1,8,256,256]{3,2,1,0:T(8,128)(2,1)}, u32[]{:S(2)}) %copy-start.2) | copy-done | bytes 1048600
  8.3 0.0 copy-start.3
  8.3 0.9 copy-done.3
  9.2 0.0 copy-start.4
  9.2 0.9 copy-done.4
  10.2 0.0 copy-start.5
  10.2 0.9 copy-done.5
  11.1 0.0 copy-start
  11.1 1.1 %prepare.1 = (bf16[2,256,256]{2,1,0:T(8,128)(2,1)S(1)}, bf16[2,256,256]{2,1,0:T(8,128)(2,1)S(1)}, f32[2,4,256,256]{3,2,1,0:T(8,128)S(1)}, bf16[8,256,256]{2,1,0:T(8,128)(2,1)S(1)}) custom-call(bf16[2,256,256]{2,1,0:T(8,128)(2,1)S(1)} %copy-done.3, bf16[2,256,256]{2,1,0:T(8,128)(2,1)S(1)} %copy-done.4, bf16[2,256,256]{2,1,0:T(8,128)(2,1)S(1)} %copy-done.5, ...), custom_call_target="tpu_custom_call" | custom-call | flops 536870912 | bytes 8388608 | tf_op jit(solution)/shard_map/prepare/pallas_call | solution.py:223
  12.3 0.0 copy-start.7
  12.3 0.0 copy-start.8
  12.3 7.4 %collective-permute-done.sec = bf16[2,1024,128]{2,1,0:T(8,128)(2,1)S(1)} collective-permute-done((bf16[2,1024,128]{2,1,0:T(8,128)(2,1)}, bf16[2,1024,128]{2,1,0:T(8,128)(2,1)S(1)}, u32[]{:S(2)}, u32[]{:S(2)}) %collective-permute-start) | collective-permute-done | bytes 524320 | tf_op jit(solution)/shard_map/ppermute | solution.py:287
  19.7 0.0 copy-done
  19.7 0.1 broadcast_select_fusion
  19.7 1.3 %collective-permute-start.2 = (bf16[2,1024,128]{2,1,0:T(8,128)(2,1)S(1)}, bf16[2,1024,128]{2,1,0:T(8,128)(2,1)S(1)}, u32[]{:S(2)}, u32[]{:S(2)}) collective-permute-start(bf16[2,1024,128]{2,1,0:T(8,128)(2,1)S(1)} %broadcast_select_fusion), channel_id=1, source_target_pairs={{0,1},{1,0},{2,3},{3,2},{4,5},{5,4},{6,7},{7,6},{8,9},{9,8},{10,11... | collective-permute-start | bytes 1572872 | tf_op jit(solution)/shard_map/ppermute | solution.py:287
  21.0 0.0 collective-permute-done.1.own_low
  21.0 0.0 collective-permute-done.3.sec_low
  21.1 0.1 collective-permute-start.4
  21.2 0.0 copy-done.7
  21.2 0.0 copy-done.8
  21.8 0.1 pad_add_fusion.info
  21.9 0.8 collective-permute-done.4.nxt_low
  22.8 0.0 collective-permute-done.2.nxt
  22.8 11.0 %slots.1 = (f32[2,1280,128]{2,1,0:T(8,128)S(1)}, bf16[2,1024,128]{2,1,0:T(8,128)(2,1)S(1)}, bf16[2,256,128]{2,1,0:T(8,128)(2,1)S(1)}, f32[2,1280,128]{2,1,0:T(8,...) custom-call(s32[18]{0:T(128)S(1)} %pad_add_fusion.info, ...), custom_call_target="tpu_custom_call" | custom-call | tf_op jit(solution)/shard_map/slots/pallas_call | solution.py:251
  33.8 0.5 collective-permute-start.5
  34.3 0.1 collective-permute-start.6
  34.4 1.4 %collective-permute-done.5 = bf16[2048,128]{1,0:T(8,128)(2,1)S(1)} collective-permute-done((bf16[2048,128]{1,0:T(8,128)(2,1)S(1)}, bf16[2048,128]{1,0:T(8,128)(2,1)S(1)}, u32[]{:S(2)}, u32[]{:S(2)}) %collective-permute-start.5) | collective-permute-done | bytes 524320 | tf_op jit(solution)/shard_map/ppermute | solution.py:287
  35.8 0.9 add_convert_fusion
  36.7 0.0 collective-permute-done.6
  36.7 0.4 collective-permute-start.7
  37.1 21.2 %all-to-all-start = ((bf16[64,32,128]{2,1,0:T(8,128)(2,1)}), bf16[64,32,128]{2,1,0:T(8,128)(2,1)}, u32[]{:S(2)}, u32[]{:S(2)}) async-start(bf16[64,32,128]{2,1,0:T(8,128)(2,1)} %bitcast.19), calls=%async_computation | async-start | bytes 1048576 | tf_op jit(solution)/shard_map/all_to_all | solution.py:337
  58.4 0.0 collective-permute-done.7
  58.4 1.0 %fusion.3 = bf16[2,1280,128]{2,1,0:T(8,128)(2,1)} fusion(f32[2,1280,128]{2,1,0:T(8,128)S(1)} %get-tuple-element.38, pred[]{:T(512)S(6)} %eq.15, bf16[2,256,128]{2,1,0:T(8,128)(2,1)S(1)} %collective-permute-done.7, bf16[2,1024,128]{2,1,0:T(8,128)(2,1)S(1)} %collective-permute-done.6), kind=kLoop, calls=%fused_computation.5 | loop fusion | flops 2293760 | bytes 2621441 | tf_op jit(solution)/shard_map/convert_element_type | solution.py:327
  59.4 2.9 %collective-permute-start.8 = (bf16[2,1280,128]{2,1,0:T(8,128)(2,1)}, bf16[2,1280,128]{2,1,0:T(8,128)(2,1)S(1)}, u32[]{:S(2)}, u32[]{:S(2)}) collective-permute-start(bf16[2,1280,128]{2,1,0:T(8,128)(2,1)} %fusion.3), channel_id=1, source_target_pairs={{0,2},{1,3},{2,4},{3,5},{4,6},{5,7},{6,8},{7,9},{8,10},{9,11},{10,... | collective-permute-start | bytes 1966088 | tf_op jit(solution)/shard_map/ppermute | solution.py:287
  62.3 8.2 %all-to-all-done = bf16[64,32,128]{2,1,0:T(8,128)(2,1)} async-done(((bf16[64,32,128]{2,1,0:T(8,128)(2,1)}), bf16[64,32,128]{2,1,0:T(8,128)(2,1)}, u32[]{:S(2)}, u32[]{:S(2)}) %all-to-all-start) | async-done | bytes 524320 | tf_op jit(solution)/shard_map/all_to_all | solution.py:337
  70.4 1.1 %convert_reduce_fusion = f32[32,128]{1,0:T(8,128)S(1)} fusion(bf16[64,32,128]{2,1,0:T(8,128)(2,1)} %all-to-all-done), kind=kLoop, calls=%fused_computation.8 | loop fusion | flops 520192 | bytes 540672 | tf_op jit(solution)/shard_map/reduce_sum | solution.py:339
  71.6 0.9 broadcast_in_dim.43
  72.5 5.5 %all-to-all-start.1 = ((bf16[64,32,128]{2,1,0:T(8,128)(2,1)}), bf16[64,32,128]{2,1,0:T(8,128)(2,1)}, u32[]{:S(2)}, u32[]{:S(2)}) async-start(bf16[64,32,128]{2,1,0:T(8,128)(2,1)} %broadcast_in_dim.43), calls=%async_computation.1 | async-start | bytes 1048576 | tf_op jit(solution)/shard_map/all_to_all | solution.py:340
  77.9 1.2 %collective-permute-done.8 = bf16[2,1280,128]{2,1,0:T(8,128)(2,1)S(1)} collective-permute-done((bf16[2,1280,128]{2,1,0:T(8,128)(2,1)}, bf16[2,1280,128]{2,1,0:T(8,128)(2,1)S(1)}, u32[]{:S(2)}, u32[]{:S(2)}) %collective-permute-start.8) | collective-permute-done | bytes 655392 | tf_op jit(solution)/shard_map/ppermute | solution.py:287
  79.1 0.0 copy-start.6
  79.1 0.8 copy-done.6
  80.0 1.3 %fusion.1 = f32[2,1280,128]{2,1,0:T(8,128)S(1)} fusion(f32[2,1280,128]{2,1,0:T(8,128)S(1)} %get-tuple-element.31, bf16[2,1280,128]{2,1,0:T(8,128)(2,1)} %copy-done.6, pred[]{:T(512)S(6)} %eq.16, bf16[2,256,128]{2,1,0:T(8,128)(2,1)S(1)} %collective-permute-done.7, bf16[2,1024,128]{2,1,0:T(8,128)(2,1)S(1)} %collective-permute-done.6), kind=kLoop, calls=%fused_computation.3 | loop fusion | flops 2621440 | bytes 3932161 | tf_op jit(solution)/shard_map/add | solution.py:329
  81.3 2.8 %collective-permute-start.9 = (bf16[2,256,128]{2,1,0:T(8,128)(2,1)S(1)}, bf16[2,256,128]{2,1,0:T(8,128)(2,1)S(1)}, u32[]{:S(2)}, u32[]{:S(2)}) collective-permute-start(bf16[2,256,128]{2,1,0:T(8,128)(2,1)S(1)} %slice.17), channel_id=1, source_target_pairs={{0,32},{1,33},{2,34},{3,35},{4,36},{5,37},{6,38},{7,39},{8,40},{9,... | collective-permute-start | bytes 393224 | tf_op jit(solution)/shard_map/ppermute | solution.py:287
  84.1 2.2 %collective-permute-done.9 = bf16[2,256,128]{2,1,0:T(8,128)(2,1)S(1)} collective-permute-done((bf16[2,256,128]{2,1,0:T(8,128)(2,1)S(1)}, bf16[2,256,128]{2,1,0:T(8,128)(2,1)S(1)}, u32[]{:S(2)}, u32[]{:S(2)}) %collective-permute-start.9) | collective-permute-done | bytes 131104 | tf_op jit(solution)/shard_map/ppermute | solution.py:287
  86.4 2.3 %all-to-all-done.1 = bf16[64,32,128]{2,1,0:T(8,128)(2,1)} async-done(((bf16[64,32,128]{2,1,0:T(8,128)(2,1)}), bf16[64,32,128]{2,1,0:T(8,128)(2,1)}, u32[]{:S(2)}, u32[]{:S(2)}) %all-to-all-start.1) | async-done | bytes 524320 | tf_op jit(solution)/shard_map/all_to_all | solution.py:340
  88.7 3.4 %collective-permute-start.10 = (bf16[2048,128]{1,0:T(8,128)(2,1)}, bf16[2048,128]{1,0:T(8,128)(2,1)S(1)}, u32[]{:S(2)}, u32[]{:S(2)}) collective-permute-start(bf16[2048,128]{1,0:T(8,128)(2,1)} %bitcast.8), channel_id=1, source_target_pairs={{0,1},{1,0},{2,3},{3,2},{4,5},{5,4},{6,7},{7,6},{8,9},{9,8},{10,11... | collective-permute-start | bytes 1572872 | tf_op jit(solution)/shard_map/ppermute | solution.py:287
  92.1 1.0 %slice_add_fusion = f32[2,1024,128]{2,1,0:T(8,128)} fusion(f32[2,1280,128]{2,1,0:T(8,128)S(1)} %fusion.1, bf16[2,256,128]{2,1,0:T(8,128)(2,1)S(1)} %collective-permute-done.9), kind=kLoop, calls=%fused_computation.6 | loop fusion | flops 524288 | bytes 2228224 | tf_op jit(solution)/shard_map/add | solution.py:348
  93.2 0.7 collective-permute-done.10
  93.9 2.6 %select_convert_fusion = f32[2,4,256,256]{3,2,1,0:T(8,128)} fusion(pred[2]{0:T(512)(128)(4,1)S(1)} %iota_compare_fusion, bf16[4,256,256]{2,1,0:T(8,128)(2,1)S(1)} %bitcast.20, bf16[4,256,256]{2,1,0:T(8,128)(2,1)} %bitcast.7), kind=kLoop, calls=%fused_computation.7 | loop fusion | flops 1048576 | bytes 3145730 | tf_op jit(solution)/shard_map/convert_element_type | solution.py:344
  (5 shorter events, 0.1 us)
Async XLA Ops:
  0.6 19.0 %collective-permute-start = (bf16[2,1024,128]{2,1,0:T(8,128)(2,1)}, bf16[2,1024,128]{2,1,0:T(8,128)(2,1)S(1)}, u32[]{:S(2)}, u32[]{:S(2)}) collective-permute-start(bf16[2,1024,128]{2,1,0:T(8,128)(2,1)} %own.1), channel_id=1, source_target_pairs={{2,0},{3,1},{4,2},{5,3},{6,4},{7,5},{8,6},{9,7},{10,8},{11,9},{12,... | collective-permute-start | bytes 1572872 | tf_op jit(solution)/shard_map/ppermute | solution.py:287
  2.9 18.2 %collective-permute-start.1 = (bf16[2,256,128]{2,1,0:T(8,128)(2,1)S(1)}, bf16[2,256,128]{2,1,0:T(8,128)(2,1)S(1)}, u32[]{:S(2)}, u32[]{:S(2)}) collective-permute-start(bf16[2,256,128]{2,1,0:T(8,128)(2,1)S(1)} %slice.10), channel_id=1, source_target_pairs={{32,0},{33,1},{34,2},{35,3},{36,4},{37,5},{38,6},{39,7},{40,8},{41... | collective-permute-start | bytes 393224 | tf_op jit(solution)/shard_map/ppermute | solution.py:287
  4.2 16.9 %collective-permute-start.3 = (bf16[2,256,128]{2,1,0:T(8,128)(2,1)S(1)}, bf16[2,256,128]{2,1,0:T(8,128)(2,1)S(1)}, u32[]{:S(2)}, u32[]{:S(2)}) collective-permute-start(bf16[2,256,128]{2,1,0:T(8,128)(2,1)S(1)} %slice.10), channel_id=1, source_target_pairs={{34,0},{35,1},{36,2},{37,3},{38,4},{39,5},{40,6},{41,7},{42,8},{43... | collective-permute-start | bytes 393224 | tf_op jit(solution)/shard_map/ppermute | solution.py:287
  5.5 1.6 %copy-start.1 = (f32[2,4,256,256]{3,2,1,0:T(8,128)S(1)}, f32[2,4,256,256]{3,2,1,0:T(8,128)}, u32[]{:S(2)}) copy-start(f32[2,4,256,256]{3,2,1,0:T(8,128)} %probe.1) | copy-start | bytes 6291460
  7.1 1.2 %copy-start.2 = (bf16[1,8,256,256]{3,2,1,0:T(8,128)(2,1)S(1)}, bf16[1,8,256,256]{3,2,1,0:T(8,128)(2,1)}, u32[]{:S(2)}) copy-start(bf16[1,8,256,256]{3,2,1,0:T(8,128)(2,1)} %meas.1) | copy-start | bytes 3145732
  8.3 0.9 copy-start.3
  9.2 0.9 copy-start.4
  10.2 0.9 copy-start.5
  11.1 8.5 %copy-start = (bf16[2,1024,128]{2,1,0:T(8,128)(2,1)S(1)}, bf16[2,1024,128]{2,1,0:T(8,128)(2,1)}, u32[]{:S(2)}) copy-start(bf16[2,1024,128]{2,1,0:T(8,128)(2,1)} %own.1) | copy-start | bytes 1572868
  12.3 8.9 %copy-start.7 = (s32[1,8]{1,0:T(1,128)S(1)}, s32[1,8]{1,0:T(1,128)}, u32[]{:S(2)}) copy-start(s32[1,8]{1,0:T(1,128)} %param.13) | copy-start | bytes 100
  12.3 8.9 %copy-start.8 = (s32[1,8]{1,0:T(1,128)S(1)}, s32[1,8]{1,0:T(1,128)}, u32[]{:S(2)}) copy-start(s32[1,8]{1,0:T(1,128)} %param.12) | copy-start | bytes 100
  19.7 3.1 %collective-permute-start.2 = (bf16[2,1024,128]{2,1,0:T(8,128)(2,1)S(1)}, bf16[2,1024,128]{2,1,0:T(8,128)(2,1)S(1)}, u32[]{:S(2)}, u32[]{:S(2)}) collective-permute-start(bf16[2,1024,128]{2,1,0:T(8,128)(2,1)S(1)} %broadcast_select_fusion), channel_id=1, source_target_pairs={{0,1},{1,0},{2,3},{3,2},{4,5},{5,4},{6,7},{7,6},{8,9},{9,8},{10,11... | collective-permute-start | bytes 1572872 | tf_op jit(solution)/shard_map/ppermute | solution.py:287
  21.1 1.7 %collective-permute-start.4 = (bf16[2,256,128]{2,1,0:T(8,128)(2,1)S(1)}, bf16[2,256,128]{2,1,0:T(8,128)(2,1)S(1)}, u32[]{:S(2)}, u32[]{:S(2)}) collective-permute-start(bf16[2,256,128]{2,1,0:T(8,128)(2,1)S(1)} %broadcast_select_fusion.1), channel_id=1, source_target_pairs={{0,1},{1,0},{2,3},{3,2},{4,5},{5,4},{6,7},{7,6},{8,9},{9,8},{10,11... | collective-permute-start | bytes 393224 | tf_op jit(solution)/shard_map/ppermute | solution.py:287
  33.8 2.0 %collective-permute-start.5 = (bf16[2048,128]{1,0:T(8,128)(2,1)S(1)}, bf16[2048,128]{1,0:T(8,128)(2,1)S(1)}, u32[]{:S(2)}, u32[]{:S(2)}) collective-permute-start(bf16[2048,128]{1,0:T(8,128)(2,1)S(1)} %get-tuple-element.33), channel_id=1, source_target_pairs={{0,1},{1,0},{2,3},{3,2},{4,5},{5,4},{6,7},{7,6},{8,9},{9,8},{10,11... | collective-permute-start | bytes 1572872 | tf_op jit(solution)/shard_map/ppermute | solution.py:287
  34.3 2.4 %collective-permute-start.6 = (bf16[2,1024,128]{2,1,0:T(8,128)(2,1)S(1)}, bf16[2,1024,128]{2,1,0:T(8,128)(2,1)S(1)}, u32[]{:S(2)}, u32[]{:S(2)}) collective-permute-start(bf16[2,1024,128]{2,1,0:T(8,128)(2,1)S(1)} %get-tuple-element.34), channel_id=1, source_target_pairs={{0,1},{1,0},{2,3},{3,2},{4,5},{5,4},{6,7},{7,6},{8,9},{9,8},{10,11... | collective-permute-start | bytes 1572872 | tf_op jit(solution)/shard_map/ppermute | solution.py:287
  36.7 21.6 %collective-permute-start.7 = (bf16[2,256,128]{2,1,0:T(8,128)(2,1)S(1)}, bf16[2,256,128]{2,1,0:T(8,128)(2,1)S(1)}, u32[]{:S(2)}, u32[]{:S(2)}) collective-permute-start(bf16[2,256,128]{2,1,0:T(8,128)(2,1)S(1)} %get-tuple-element.37), channel_id=1, source_target_pairs={{0,1},{1,0},{2,3},{3,2},{4,5},{5,4},{6,7},{7,6},{8,9},{9,8},{10,11... | collective-permute-start | bytes 393224 | tf_op jit(solution)/shard_map/ppermute | solution.py:287
  37.1 33.3 %all-to-all-start = ((bf16[64,32,128]{2,1,0:T(8,128)(2,1)}), bf16[64,32,128]{2,1,0:T(8,128)(2,1)}, u32[]{:S(2)}, u32[]{:S(2)}) async-start(bf16[64,32,128]{2,1,0:T(8,128)(2,1)} %bitcast.19), calls=%async_computation | async-start | bytes 1048576 | tf_op jit(solution)/shard_map/all_to_all | solution.py:337
  59.4 19.7 %collective-permute-start.8 = (bf16[2,1280,128]{2,1,0:T(8,128)(2,1)}, bf16[2,1280,128]{2,1,0:T(8,128)(2,1)S(1)}, u32[]{:S(2)}, u32[]{:S(2)}) collective-permute-start(bf16[2,1280,128]{2,1,0:T(8,128)(2,1)} %fusion.3), channel_id=1, source_target_pairs={{0,2},{1,3},{2,4},{3,5},{4,6},{5,7},{6,8},{7,9},{8,10},{9,11},{10,... | collective-permute-start | bytes 1966088 | tf_op jit(solution)/shard_map/ppermute | solution.py:287
  72.5 16.3 %all-to-all-start.1 = ((bf16[64,32,128]{2,1,0:T(8,128)(2,1)}), bf16[64,32,128]{2,1,0:T(8,128)(2,1)}, u32[]{:S(2)}, u32[]{:S(2)}) async-start(bf16[64,32,128]{2,1,0:T(8,128)(2,1)} %broadcast_in_dim.43), calls=%async_computation.1 | async-start | bytes 1048576 | tf_op jit(solution)/shard_map/all_to_all | solution.py:340
  79.1 0.8 copy-start.6
  81.3 5.1 %collective-permute-start.9 = (bf16[2,256,128]{2,1,0:T(8,128)(2,1)S(1)}, bf16[2,256,128]{2,1,0:T(8,128)(2,1)S(1)}, u32[]{:S(2)}, u32[]{:S(2)}) collective-permute-start(bf16[2,256,128]{2,1,0:T(8,128)(2,1)S(1)} %slice.17), channel_id=1, source_target_pairs={{0,32},{1,33},{2,34},{3,35},{4,36},{5,37},{6,38},{7,39},{8,40},{9,... | collective-permute-start | bytes 393224 | tf_op jit(solution)/shard_map/ppermute | solution.py:287
  88.7 5.1 %collective-permute-start.10 = (bf16[2048,128]{1,0:T(8,128)(2,1)}, bf16[2048,128]{1,0:T(8,128)(2,1)S(1)}, u32[]{:S(2)}, u32[]{:S(2)}) collective-permute-start(bf16[2048,128]{1,0:T(8,128)(2,1)} %bitcast.8), channel_id=1, source_target_pairs={{0,1},{1,0},{2,3},{3,2},{4,5},{5,4},{6,7},{7,6},{8,9},{9,8},{10,11... | collective-permute-start | bytes 1572872 | tf_op jit(solution)/shard_map/ppermute | solution.py:287
where the time goes:
time: 96 us; the launch traced here: 96.4 us
  starting transfers between devices  42.1 us (44%)
  waiting for transfers between devices  24.3 us (25%)
  Pallas kernels  12.2 us (13%)
  local copies, waits for them, and re-layouts  8.31 us (9%)
  other arithmetic  8.13 us (8%)
  between operations  1.44 us (2%)
    all_to_all x1, starting transfers between devices, local(): share = exchange(chip_sum.reshape(devices // 2, -1, LANES))  21.2 us
    ppermute x11, starting transfers between devices, moved(): return lax.ppermute(value, ('rows', 'cols'), pairs)  15.4 us
    ppermute x11, waiting for transfers between devices, moved(): return lax.ppermute(value, ('rows', 'cols'), pairs)  13.7 us
    pallas_call x1, Pallas kernels, run_slots(): pl.pallas_call(slots_kernel, in_specs=[pl.BlockSpec(memory_space=pltpu.SM...  11 us
    all_to_all x1, waiting for transfers between devices, local(): share = exchange(chip_sum.reshape(devices // 2, -1, LANES))  8.18 us
    unnamed x18, local copies, waits for them, and re-layouts  6.51 us
    all_to_all x1, starting transfers between devices, local(): exchange(jnp.broadcast_to(share[None], (devices // 2,) + share.shape))  5.49 us
    convert_element_type x1, other arithmetic, local(): jnp.where(part == core, mine[None], swap_cores(mine)[None]).astype(F32)  2.57 us
  transfers between devices with their start and end apart: 13, of which 8 were waited for; matrix products, arithmetic and copies ran while one was open for 8% of the time, Pallas kernels for 1%

commit v1 on v0

--- a/solution.py
+++ b/solution.py
@@ -40,7 +40,7 @@
 
 def slots_kernel(
     info, fwd, bwd, probe, meas, own, own_low, nxt, nxt_low, sec, sec_low,
-    g_own, g_next, g_next_low, g_sec, acc_keep, acc_send,
+    g_own, g_next, g_sec, acc_keep, acc_send,
     ext, mid, acc, owin, xs, hb, gb, kb,
 ):
     slots = meas.shape[0]
@@ -108,14 +108,14 @@
                     for pc in range(2):
                         for at in range(0, half, BLOCK):
                             for c in range(2):
-                                hb[
-                                    q, pc, (rp * half + at) // BLOCK, m * BLOCK : (m + 1) * BLOCK, sides[c]
-                                ] = v[pc][c * half + at : c * half + at + BLOCK]
+                                first = (q * modes + m) * BLOCK
+                                hb[pc, (rp * half + at) // BLOCK, first : first + BLOCK, sides[c]] = v[pc][c * half + at : c * half + at + BLOCK]
 
         for rb in range(blocks):
             for pc in range(2):
+                fields = jnp.dot(hb[pc, rb], bwd[pc], preferred_element_type=F32)
                 for q in range(2):
-                    field = jnp.dot(hb[q, pc, rb], bwd[pc], preferred_element_type=F32)
+                    field = fields[q * modes * BLOCK : (q + 1) * modes * BLOCK]
                     for at in range(0, BLOCK, CHUNK):
                         part = [field[m * BLOCK + at : m * BLOCK + at + CHUNK] for m in range(modes)]
                         total = 1.0
@@ -140,15 +140,12 @@
                     for at in range(0, half, BLOCK):
                         for pc in range(2):
                             for c in range(2):
-                                kb[
-                                    q, pc, (side * half + at) // BLOCK, m * BLOCK : (m + 1) * BLOCK, sides[c]
-                                ] = v[c * half + at : c * half + at + BLOCK, sides[pc]]
+                                first = (q * modes + m) * BLOCK
+                                kb[pc, (side * half + at) // BLOCK, first : first + BLOCK, sides[c]] = v[c * half + at : c * half + at + BLOCK, sides[pc]]
 
         for rb in range(blocks):
-            w = [
-                [jnp.dot(kb[q, pc, rb], fwd[pc], preferred_element_type=F32) for pc in range(2)]
-                for q in range(2)
-            ]
+            fields = [jnp.dot(kb[pc, rb], fwd[pc], preferred_element_type=F32) for pc in range(2)]
+            w = [[f[q * modes * BLOCK : (q + 1) * modes * BLOCK] for f in fields] for q in range(2)]
             for at in range(0, BLOCK, CHUNK):
                 rows = slice(rb * BLOCK + at, rb * BLOCK + at + CHUNK)
                 g = [[[None, None], [None, None]] for q in range(2)]
@@ -187,8 +184,7 @@
 
     lax.fori_loop(0, lax.div(live + 1, 2), pair_of_slots, 0)
 
-    g_next[...] = mid[:, :tile_rows, :].astype(BF16)
-    g_next_low[...] = mid[:, tile_rows:, :].astype(BF16)
+    g_next[...] = mid[...].astype(BF16)
     for m in range(modes):
         for at in range(0, win, 8):
             for h in range(2):
@@ -246,16 +242,15 @@
     modes, win = probe.shape[1:3]
     tall = (2, tile_rows + win, tile_cols)
     flat = (2 * modes * win, LANES)
-    blocks = (2, win // BLOCK, modes * BLOCK, win)
+    blocks = (2, win // BLOCK, 2 * modes * BLOCK, win)
     vmem = pl.BlockSpec(memory_space=pltpu.VMEM)
     return pl.pallas_call(
         slots_kernel,
         in_specs=[pl.BlockSpec(memory_space=pltpu.SMEM)] + [vmem] * 10,
-        out_specs=[vmem] * 6,
+        out_specs=[vmem] * 5,
         out_shape=[
             jax.ShapeDtypeStruct(tall, F32),
-            jax.ShapeDtypeStruct(own.shape, BF16),
-            jax.ShapeDtypeStruct(own_low.shape, BF16),
+            jax.ShapeDtypeStruct(tall, BF16),
             jax.ShapeDtypeStruct(tall, F32),
             jax.ShapeDtypeStruct(flat, F32),
             jax.ShapeDtypeStruct(flat, BF16),
@@ -266,9 +261,9 @@
             pltpu.VMEM((2, modes, win, win), F32),
             pltpu.VMEM((2, 2, 2, win, LANES), F32),
             pltpu.VMEM((2, modes, 2, win, win), BF16),
-            pltpu.VMEM((2,) + blocks, BF16),
+            pltpu.VMEM(blocks, BF16),
             pltpu.VMEM((2, modes, 2, win, win), BF16),
-            pltpu.VMEM((2,) + blocks, BF16),
+            pltpu.VMEM(blocks, BF16),
         ],
         compiler_params=pltpu.CompilerParams(vmem_limit_bytes=32 * 1024 * 1024),
         name="slots",
@@ -314,19 +309,20 @@
             core[None],
         ]
     )
-    g_own, g_next, g_next_low, g_sec, acc_keep, acc_send = run_slots(
+    g_own, g_next, g_sec, acc_keep, acc_send = run_slots(
         info, *prepared, object_field, own_low, nxt, nxt_low, sec, sec_low
     )
 
     acc_got = swap_cores(acc_send)
     near = swap_cores(g_next)
     chip_sum = (acc_keep + acc_got.astype(F32)).astype(BF16)
-    chip_sum, near, near_low = lax.optimization_barrier((chip_sum, near, g_next_low))
-    near = jnp.concatenate([near, swap_cores(near_low)], axis=1).astype(F32)
+    chip_sum, near = lax.optimization_barrier((chip_sum, near))
+    near = lax.optimization_barrier(near.astype(F32))
     none = jnp.zeros_like(near)
+    inner, near = lax.optimization_barrier((g_own + jnp.where(core == 1, near, none), near))
     outward = (g_sec + jnp.where(core == 0, near, none)).astype(BF16)
     far = moved(outward, lambda a, b: (a, b + 2))
-    total = g_own + jnp.where(core == 1, near, none) + far.astype(F32)
+    total = inner + far.astype(F32)
     rim = moved(total[:, tile_rows:].astype(BF16), lambda a, b: (a + 1, b))
 
     groups = [[i for i in range(devices) if i % 2 == c] for c in range(2)]

time: 96 us -> 101 us (1.052); the launches traced: 96.4 us -> 99.4 us
  starting transfers between devices: 42.1 us -> 35.5 us
  Pallas kernels: 12.2 us -> 17.9 us
  waiting for transfers between devices: 24.3 us -> 27.2 us
    pallas_call x1, Pallas kernels: 11 us -> 16.8 us  [run_slots(): pl.pallas_call(slots_kernel, in_specs=[pl.BlockSpec(memory_space=pltpu.SM...]
    all_to_all x1, starting transfers between devices: 21.2 us -> 15.7 us  [local(): share = exchange(chip_sum.reshape(devices // 2, -1, LANES))]
    ppermute x11 -> x10, waiting for transfers between devices: 13.7 us -> 16 us  [moved(): return lax.ppermute(value, ('rows', 'cols'), pairs)]
    convert_element_type x1, other arithmetic: 0.9 us -> 2.25 us  [local(): chip_sum = (acc_keep + acc_got.astype(F32)).astype(BF16)]
    add x1 -> x2, other arithmetic: 1.3 us -> 2.64 us  [the longest x1 1.45 us: local(): g_own + jnp.where(core == 1, near, none)]
    all_to_all x1, waiting for transfers between devices: 2.34 us -> 3.65 us  [local(): exchange(jnp.broadcast_to(share[None], (devices // 2,) + share.shape))]
    reduce_sum x1, other arithmetic: 1.14 us -> 0.1 us  [local(): share = (jnp.sum(share.astype(F32), axis=0) * scale).astype(BF16)]
    convert_element_type x1, other arithmetic: 2.57 us -> 1.53 us  [local(): jnp.where(part == core, mine[None], swap_cores(mine)[None]).astype(F32)]
  transfers between devices with their start and end apart: 13 -> 12, of which waited for: 8 -> 8; matrix products, arithmetic and copies ran while one was open for 8% -> 8% of each run, Pallas kernels for 1% -> 1%
where the time goes in v1:
time: 101 us; the launch traced here: 99.4 us
  starting transfers between devices  35.5 us (35%)
  waiting for transfers between devices  27.2 us (27%)
  Pallas kernels  17.9 us (18%)
  other arithmetic  8.81 us (9%)
  local copies, waits for them, and re-layouts  8.52 us (8%)
  between operations  1.43 us (1%)
    pallas_call x1, Pallas kernels, run_slots(): pl.pallas_call(slots_kernel, in_specs=[pl.BlockSpec(memory_space=pltpu.SM...  16.8 us
    ppermute x10, waiting for transfers between devices, moved(): return lax.ppermute(value, ('rows', 'cols'), pairs)  16 us
    all_to_all x1, starting transfers between devices, local(): share = exchange(chip_sum.reshape(devices // 2, -1, LANES))  15.7 us
    ppermute x10, starting transfers between devices, moved(): return lax.ppermute(value, ('rows', 'cols'), pairs)  15.1 us
    all_to_all x1, waiting for transfers between devices, local(): share = exchange(chip_sum.reshape(devices // 2, -1, LANES))  7.59 us
    unnamed x22, local copies, waits for them, and re-layouts  6.7 us
    all_to_all x1, starting transfers between devices, local(): exchange(jnp.broadcast_to(share[None], (devices // 2,) + share.shape))  4.69 us
    all_to_all x1, waiting for transfers between devices, local(): exchange(jnp.broadcast_to(share[None], (devices // 2,) + share.shape))  3.65 us
  transfers between devices with their start and end apart: 12, of which 8 were waited for; matrix products, arithmetic and copies ran while one was open for 8% of the time, Pallas kernels for 1%

profile of v1, /device:TPU:1, one launch (start us, length us, event | category | flops | bytes accessed | tf_op | source)
XLA Modules:
  0.0 99.4 jit_solution(15714611080129230851)
XLA Ops:
  0.6 1.3 %collective-permute-start = (bf16[2,1024,128]{2,1,0:T(8,128)(2,1)}, bf16[2,1024,128]{2,1,0:T(8,128)(2,1)S(1)}, u32[]{:S(2)}, u32[]{:S(2)}) collective-permute-start(bf16[2,1024,128]{2,1,0:T(8,128)(2,1)} %own.1), channel_id=1, source_target_pairs={{2,0},{3,1},{4,2},{5,3},{6,4},{7,5},{8,6},{9,7},{10,8},{11,9},{12,... | collective-permute-start | bytes 1572872 | tf_op jit(solution)/shard_map/ppermute | solution.py:282
  1.9 0.9 slice.10
  2.9 1.3 %collective-permute-start.1 = (bf16[2,256,128]{2,1,0:T(8,128)(2,1)S(1)}, bf16[2,256,128]{2,1,0:T(8,128)(2,1)S(1)}, u32[]{:S(2)}, u32[]{:S(2)}) collective-permute-start(bf16[2,256,128]{2,1,0:T(8,128)(2,1)S(1)} %slice.10), channel_id=1, source_target_pairs={{32,0},{33,1},{34,2},{35,3},{36,4},{37,5},{38,6},{39,7},{40,8},{41... | collective-permute-start | bytes 393224 | tf_op jit(solution)/shard_map/ppermute | solution.py:282
  4.2 1.3 %collective-permute-start.3 = (bf16[2,256,128]{2,1,0:T(8,128)(2,1)S(1)}, bf16[2,256,128]{2,1,0:T(8,128)(2,1)S(1)}, u32[]{:S(2)}, u32[]{:S(2)}) collective-permute-start(bf16[2,256,128]{2,1,0:T(8,128)(2,1)S(1)} %slice.10), channel_id=1, source_target_pairs={{34,0},{35,1},{36,2},{37,3},{38,4},{39,5},{40,6},{41,7},{42,8},{43... | collective-permute-start | bytes 393224 | tf_op jit(solution)/shard_map/ppermute | solution.py:282
  5.5 0.0 copy-start.1
  5.5 1.6 %copy-done.1 = f32[2,4,256,256]{3,2,1,0:T(8,128)S(1)} copy-done((f32[2,4,256,256]{3,2,1,0:T(8,128)S(1)}, f32[2,4,256,256]{3,2,1,0:T(8,128)}, u32[]{:S(2)}) %copy-start.1) | copy-done | bytes 2097176
  7.1 0.0 copy-start.3
  7.1 1.2 %copy-done.3 = bf16[1,8,256,256]{3,2,1,0:T(8,128)(2,1)S(1)} copy-done((bf16[1,8,256,256]{3,2,1,0:T(8,128)(2,1)S(1)}, bf16[1,8,256,256]{3,2,1,0:T(8,128)(2,1)}, u32[]{:S(2)}) %copy-start.3) | copy-done | bytes 1048600
  8.3 0.0 copy-start.4
  8.3 0.9 copy-done.4
  9.2 0.0 copy-start.5
  9.2 0.9 copy-done.5
  10.2 0.0 copy-start.6
  10.2 0.9 copy-done.6
  11.1 0.0 copy-start
  11.1 1.1 %prepare.1 = (bf16[2,256,256]{2,1,0:T(8,128)(2,1)S(1)}, bf16[2,256,256]{2,1,0:T(8,128)(2,1)S(1)}, f32[2,4,256,256]{3,2,1,0:T(8,128)S(1)}, bf16[8,256,256]{2,1,0:T(8,128)(2,1)S(1)}) custom-call(bf16[2,256,256]{2,1,0:T(8,128)(2,1)S(1)} %copy-done.4, bf16[2,256,256]{2,1,0:T(8,128)(2,1)S(1)} %copy-done.5, bf16[2,256,256]{2,1,0:T(8,128)(2,1)S(1)} %copy-done.6, ...), custom_call_target="tpu_custom_call" | custom-call | flops 536870912 | bytes 8388608 | tf_op jit(solution)/shard_map/prepare/pallas_call | solution.py:219
  12.3 0.0 copy-start.9
  12.3 0.0 copy-start.10
  12.3 7.4 %collective-permute-done.sec = bf16[2,1024,128]{2,1,0:T(8,128)(2,1)S(1)} collective-permute-done((bf16[2,1024,128]{2,1,0:T(8,128)(2,1)}, bf16[2,1024,128]{2,1,0:T(8,128)(2,1)S(1)}, u32[]{:S(2)}, u32[]{:S(2)}) %collective-permute-start) | collective-permute-done | bytes 524320 | tf_op jit(solution)/shard_map/ppermute | solution.py:282
  19.7 0.0 copy-done
  19.7 0.1 broadcast_select_fusion
  19.7 1.3 %collective-permute-start.2 = (bf16[2,1024,128]{2,1,0:T(8,128)(2,1)S(1)}, bf16[2,1024,128]{2,1,0:T(8,128)(2,1)S(1)}, u32[]{:S(2)}, u32[]{:S(2)}) collective-permute-start(bf16[2,1024,128]{2,1,0:T(8,128)(2,1)S(1)} %broadcast_select_fusion), channel_id=1, source_target_pairs={{0,1},{1,0},{2,3},{3,2},{4,5},{5,4},{6,7},{7,6},{8,9},{9,8},{10,11... | collective-permute-start | bytes 1572872 | tf_op jit(solution)/shard_map/ppermute | solution.py:282
  21.0 0.0 collective-permute-done.1.own_low
  21.0 0.0 collective-permute-done.3.sec_low
  21.1 0.1 collective-permute-start.4
  21.2 0.0 copy-done.9
  21.2 0.0 copy-done.10
  21.8 0.1 pad_add_fusion.info
  21.9 0.8 collective-permute-done.4.nxt_low
  22.8 0.0 collective-permute-done.2.nxt
  22.8 16.8 %slots.1 = (f32[2,1280,128]{2,1,0:T(8,128)S(1)}, bf16[2,1280,128]{2,1,0:T(8,128)(2,1)}, f32[2,1280,128]{2,1,0:T(8,128)S(1)}, f32[2048,128]{1,0:T(8,128)S(1)}, bf16[2048,128]{1,0:T(8,128)(2,1)}) custom-call(s32[18]{0:T(128)S(1)} %pad_add_fusion.info, bf16[2,256,256]{2,1,0:T(8,128)(2,1)S(1)} %get-tuple-element.26.fwd, ...), custom_call_target="tpu_custom_call" | custom-call | tf_op jit(solution)/shard_map/slots/pallas_call | solution.py:247
  39.6 0.0 copy-start.2
  39.6 1.0 copy-done.2
  40.5 0.3 collective-permute-start.5
  40.9 0.2 collective-permute-start.6
  41.0 1.7 %collective-permute-done.5 = bf16[2048,128]{1,0:T(8,128)(2,1)} collective-permute-done((bf16[2048,128]{1,0:T(8,128)(2,1)}, bf16[2048,128]{1,0:T(8,128)(2,1)}, u32[]{:S(2)}, u32[]{:S(2)}) %collective-permute-start.5) | collective-permute-done | bytes 524320 | tf_op jit(solution)/shard_map/ppermute | solution.py:282
  42.8 2.2 %add_convert_fusion.1 = bf16[2048,128]{1,0:T(8,128)(2,1)} fusion(f32[2048,128]{1,0:T(8,128)} %copy-done.2, bf16[2048,128]{1,0:T(8,128)(2,1)} %collective-permute-done.5), kind=kLoop, calls=%fused_computation.6 | loop fusion | flops 786432 | bytes 2097152 | tf_op jit(solution)/shard_map/convert_element_type | solution.py:318
  45.0 0.0 collective-permute-done.6
  45.0 0.1 convert_element_type.37
  45.1 0.0 copy-start.7
  45.1 1.4 %select_add_fusion = f32[2,1280,128]{2,1,0:T(8,128)} fusion(f32[2,1280,128]{2,1,0:T(8,128)S(1)} %get-tuple-element.31, f32[2,1280,128]{2,1,0:T(8,128)S(1)} %convert_element_type.37, pred[]{:T(512)S(6)} %eq.16), kind=kLoop, calls=%fused_computation.2 | loop fusion | flops 655360 | bytes 3932161 | tf_op jit(solution)/shard_map/add | solution.py:322
  46.6 0.0 copy-done.7
  46.6 15.7 %all-to-all-start = ((bf16[64,32,128]{2,1,0:T(8,128)(2,1)}), bf16[64,32,128]{2,1,0:T(8,128)(2,1)S(1)}, u32[]{:S(2)}, u32[]{:S(2)}) async-start(bf16[64,32,128]{2,1,0:T(8,128)(2,1)} %bitcast.4), calls=%async_computation | async-start | bytes 1048576 | tf_op jit(solution)/shard_map/all_to_all | solution.py:333
  62.3 1.0 %add_convert_fusion = bf16[2,1280,128]{2,1,0:T(8,128)(2,1)} fusion(f32[2,1280,128]{2,1,0:T(8,128)S(1)} %get-tuple-element.37, f32[2,1280,128]{2,1,0:T(8,128)} %copy-done.7, pred[]{:T(512)S(6)} %eq.15), kind=kLoop, calls=%fused_computation.1 | loop fusion | flops 983040 | bytes 3276801 | tf_op jit(solution)/shard_map/convert_element_type | solution.py:323
  63.3 0.0 copy-start.8
  63.3 3.9 %collective-permute-start.7 = (bf16[2,1280,128]{2,1,0:T(8,128)(2,1)}, bf16[2,1280,128]{2,1,0:T(8,128)(2,1)}, u32[]{:S(2)}, u32[]{:S(2)}) collective-permute-start(bf16[2,1280,128]{2,1,0:T(8,128)(2,1)} %add_convert_fusion), channel_id=1, source_target_pairs={{0,2},{1,3},{2,4},{3,5},{4,6},{5,7},{6,8},{7,9},{8,10},{9,11},{10,... | collective-permute-start | bytes 1966088 | tf_op jit(solution)/shard_map/ppermute | solution.py:282
  67.2 7.6 %all-to-all-done = bf16[64,32,128]{2,1,0:T(8,128)(2,1)S(1)} async-done(((bf16[64,32,128]{2,1,0:T(8,128)(2,1)}), bf16[64,32,128]{2,1,0:T(8,128)(2,1)S(1)}, u32[]{:S(2)}, u32[]{:S(2)}) %all-to-all-start) | async-done | bytes 524320 | tf_op jit(solution)/shard_map/all_to_all | solution.py:333
  74.8 0.1 convert_reduce_fusion
  74.9 0.9 broadcast_in_dim.43
  75.8 4.7 %all-to-all-start.1 = ((bf16[64,32,128]{2,1,0:T(8,128)(2,1)}), bf16[64,32,128]{2,1,0:T(8,128)(2,1)S(1)}, u32[]{:S(2)}, u32[]{:S(2)}) async-start(bf16[64,32,128]{2,1,0:T(8,128)(2,1)} %broadcast_in_dim.43), calls=%async_computation.1 | async-start | bytes 1048576 | tf_op jit(solution)/shard_map/all_to_all | solution.py:336
  80.5 3.6 %collective-permute-done.7 = bf16[2,1280,128]{2,1,0:T(8,128)(2,1)} collective-permute-done((bf16[2,1280,128]{2,1,0:T(8,128)(2,1)}, bf16[2,1280,128]{2,1,0:T(8,128)(2,1)}, u32[]{:S(2)}, u32[]{:S(2)}) %collective-permute-start.7) | collective-permute-done | bytes 655392 | tf_op jit(solution)/shard_map/ppermute | solution.py:282
  84.1 0.0 copy-done.8
  84.1 1.2 %convert_add_fusion = f32[2,1280,128]{2,1,0:T(8,128)S(1)} fusion(f32[2,1280,128]{2,1,0:T(8,128)S(1)} %copy-done.8, bf16[2,1280,128]{2,1,0:T(8,128)(2,1)} %collective-permute-done.7), kind=kLoop, calls=%fused_computation | loop fusion | flops 655360 | bytes 3276800 | tf_op jit(solution)/shard_map/add | solution.py:325
  85.3 2.9 %collective-permute-start.8 = (bf16[2,256,128]{2,1,0:T(8,128)(2,1)S(1)}, bf16[2,256,128]{2,1,0:T(8,128)(2,1)S(1)}, u32[]{:S(2)}, u32[]{:S(2)}) collective-permute-start(bf16[2,256,128]{2,1,0:T(8,128)(2,1)S(1)} %slice.17), channel_id=1, source_target_pairs={{0,32},{1,33},{2,34},{3,35},{4,36},{5,37},{6,38},{7,39},{8,40},{9,... | collective-permute-start | bytes 393224 | tf_op jit(solution)/shard_map/ppermute | solution.py:282
  88.2 1.9 %collective-permute-done.8 = bf16[2,256,128]{2,1,0:T(8,128)(2,1)S(1)} collective-permute-done((bf16[2,256,128]{2,1,0:T(8,128)(2,1)S(1)}, bf16[2,256,128]{2,1,0:T(8,128)(2,1)S(1)}, u32[]{:S(2)}, u32[]{:S(2)}) %collective-permute-start.8) | collective-permute-done | bytes 131104 | tf_op jit(solution)/shard_map/ppermute | solution.py:282
  90.2 3.7 %all-to-all-done.1 = bf16[64,32,128]{2,1,0:T(8,128)(2,1)S(1)} async-done(((bf16[64,32,128]{2,1,0:T(8,128)(2,1)}), bf16[64,32,128]{2,1,0:T(8,128)(2,1)S(1)}, u32[]{:S(2)}, u32[]{:S(2)}) %all-to-all-start.1) | async-done | bytes 524320 | tf_op jit(solution)/shard_map/all_to_all | solution.py:336
  93.8 2.5 %collective-permute-start.9 = (bf16[2048,128]{1,0:T(8,128)(2,1)S(1)}, bf16[2048,128]{1,0:T(8,128)(2,1)S(1)}, u32[]{:S(2)}, u32[]{:S(2)}) collective-permute-start(bf16[2048,128]{1,0:T(8,128)(2,1)S(1)} %bitcast.19), channel_id=1, source_target_pairs={{0,1},{1,0},{2,3},{3,2},{4,5},{5,4},{6,7},{7,6},{8,9},{9,8},{10,11... | collective-permute-start | bytes 1572872 | tf_op jit(solution)/shard_map/ppermute | solution.py:282
  96.3 1.0 %slice_add_fusion = f32[2,1024,128]{2,1,0:T(8,128)} fusion(f32[2,1280,128]{2,1,0:T(8,128)S(1)} %convert_add_fusion, bf16[2,256,128]{2,1,0:T(8,128)(2,1)S(1)} %collective-permute-done.8), kind=kLoop, calls=%fused_computation.3 | loop fusion | flops 524288 | bytes 2228224 | tf_op jit(solution)/shard_map/add | solution.py:344
  97.4 0.5 collective-permute-done.9
  97.9 1.5 %select_convert_fusion = f32[2,4,256,256]{3,2,1,0:T(8,128)} fusion(pred[2]{0:T(512)(128)(4,1)S(1)} %iota_compare_fusion, bf16[4,256,256]{2,1,0:T(8,128)(2,1)S(1)} %bitcast.21, bf16[4,256,256]{2,1,0:T(8,128)(2,1)S(1)} %bitcast.20), kind=kLoop, calls=%fused_computation.4 | loop fusion | flops 1048576 | bytes 3145730 | tf_op jit(solution)/shard_map/convert_element_type | solution.py:340
  (5 shorter events, 0.1 us)
Async XLA Ops:
  0.6 19.0 %collective-permute-start = (bf16[2,1024,128]{2,1,0:T(8,128)(2,1)}, bf16[2,1024,128]{2,1,0:T(8,128)(2,1)S(1)}, u32[]{:S(2)}, u32[]{:S(2)}) collective-permute-start(bf16[2,1024,128]{2,1,0:T(8,128)(2,1)} %own.1), channel_id=1, source_target_pairs={{2,0},{3,1},{4,2},{5,3},{6,4},{7,5},{8,6},{9,7},{10,8},{11,9},{12,... | collective-permute-start | bytes 1572872 | tf_op jit(solution)/shard_map/ppermute | solution.py:282
  2.9 18.2 %collective-permute-start.1 = (bf16[2,256,128]{2,1,0:T(8,128)(2,1)S(1)}, bf16[2,256,128]{2,1,0:T(8,128)(2,1)S(1)}, u32[]{:S(2)}, u32[]{:S(2)}) collective-permute-start(bf16[2,256,128]{2,1,0:T(8,128)(2,1)S(1)} %slice.10), channel_id=1, source_target_pairs={{32,0},{33,1},{34,2},{35,3},{36,4},{37,5},{38,6},{39,7},{40,8},{41... | collective-permute-start | bytes 393224 | tf_op jit(solution)/shard_map/ppermute | solution.py:282
  4.2 16.9 %collective-permute-start.3 = (bf16[2,256,128]{2,1,0:T(8,128)(2,1)S(1)}, bf16[2,256,128]{2,1,0:T(8,128)(2,1)S(1)}, u32[]{:S(2)}, u32[]{:S(2)}) collective-permute-start(bf16[2,256,128]{2,1,0:T(8,128)(2,1)S(1)} %slice.10), channel_id=1, source_target_pairs={{34,0},{35,1},{36,2},{37,3},{38,4},{39,5},{40,6},{41,7},{42,8},{43... | collective-permute-start | bytes 393224 | tf_op jit(solution)/shard_map/ppermute | solution.py:282
  5.5 1.6 %copy-start.1 = (f32[2,4,256,256]{3,2,1,0:T(8,128)S(1)}, f32[2,4,256,256]{3,2,1,0:T(8,128)}, u32[]{:S(2)}) copy-start(f32[2,4,256,256]{3,2,1,0:T(8,128)} %probe.1) | copy-start | bytes 6291460
  7.1 1.2 %copy-start.3 = (bf16[1,8,256,256]{3,2,1,0:T(8,128)(2,1)S(1)}, bf16[1,8,256,256]{3,2,1,0:T(8,128)(2,1)}, u32[]{:S(2)}) copy-start(bf16[1,8,256,256]{3,2,1,0:T(8,128)(2,1)} %meas.1) | copy-start | bytes 3145732
  8.3 0.9 copy-start.4
  9.2 0.9 copy-start.5
  10.2 0.9 copy-start.6
  11.1 8.5 %copy-start = (bf16[2,1024,128]{2,1,0:T(8,128)(2,1)S(1)}, bf16[2,1024,128]{2,1,0:T(8,128)(2,1)}, u32[]{:S(2)}) copy-start(bf16[2,1024,128]{2,1,0:T(8,128)(2,1)} %own.1) | copy-start | bytes 1572868
  12.3 8.9 %copy-start.9 = (s32[1,8]{1,0:T(1,128)S(1)}, s32[1,8]{1,0:T(1,128)}, u32[]{:S(2)}) copy-start(s32[1,8]{1,0:T(1,128)} %param.13) | copy-start | bytes 100
  12.3 8.9 %copy-start.10 = (s32[1,8]{1,0:T(1,128)S(1)}, s32[1,8]{1,0:T(1,128)}, u32[]{:S(2)}) copy-start(s32[1,8]{1,0:T(1,128)} %param.12) | copy-start | bytes 100
  19.7 3.1 %collective-permute-start.2 = (bf16[2,1024,128]{2,1,0:T(8,128)(2,1)S(1)}, bf16[2,1024,128]{2,1,0:T(8,128)(2,1)S(1)}, u32[]{:S(2)}, u32[]{:S(2)}) collective-permute-start(bf16[2,1024,128]{2,1,0:T(8,128)(2,1)S(1)} %broadcast_select_fusion), channel_id=1, source_target_pairs={{0,1},{1,0},{2,3},{3,2},{4,5},{5,4},{6,7},{7,6},{8,9},{9,8},{10,11... | collective-permute-start | bytes 1572872 | tf_op jit(solution)/shard_map/ppermute | solution.py:282
  21.1 1.7 %collective-permute-start.4 = (bf16[2,256,128]{2,1,0:T(8,128)(2,1)S(1)}, bf16[2,256,128]{2,1,0:T(8,128)(2,1)S(1)}, u32[]{:S(2)}, u32[]{:S(2)}) collective-permute-start(bf16[2,256,128]{2,1,0:T(8,128)(2,1)S(1)} %broadcast_select_fusion.1), channel_id=1, source_target_pairs={{0,1},{1,0},{2,3},{3,2},{4,5},{5,4},{6,7},{7,6},{8,9},{9,8},{10,11... | collective-permute-start | bytes 393224 | tf_op jit(solution)/shard_map/ppermute | solution.py:282
  39.6 1.0 copy-start.2
  40.5 2.3 %collective-permute-start.5 = (bf16[2048,128]{1,0:T(8,128)(2,1)}, bf16[2048,128]{1,0:T(8,128)(2,1)}, u32[]{:S(2)}, u32[]{:S(2)}) collective-permute-start(bf16[2048,128]{1,0:T(8,128)(2,1)} %get-tuple-element.33), channel_id=1, source_target_pairs={{0,1},{1,0},{2,3},{3,2},{4,5},{5,4},{6,7},{7,6},{8,9},{9,8},{10,11... | collective-permute-start | bytes 1572872 | tf_op jit(solution)/shard_map/ppermute | solution.py:282
  40.9 4.2 %collective-permute-start.6 = (bf16[2,1280,128]{2,1,0:T(8,128)(2,1)}, bf16[2,1280,128]{2,1,0:T(8,128)(2,1)S(1)}, u32[]{:S(2)}, u32[]{:S(2)}) collective-permute-start(bf16[2,1280,128]{2,1,0:T(8,128)(2,1)} %get-tuple-element.34), channel_id=1, source_target_pairs={{0,1},{1,0},{2,3},{3,2},{4,5},{5,4},{6,7},{7,6},{8,9},{9,8},{10,11... | collective-permute-start | bytes 1966088 | tf_op jit(solution)/shard_map/ppermute | solution.py:282
  45.1 1.5 %copy-start.7 = (f32[2,1280,128]{2,1,0:T(8,128)}, f32[2,1280,128]{2,1,0:T(8,128)S(1)}, u32[]{:S(2)}) copy-start(f32[2,1280,128]{2,1,0:T(8,128)S(1)} %convert_element_type.37) | copy-start | bytes 3932164
  46.6 28.2 %all-to-all-start = ((bf16[64,32,128]{2,1,0:T(8,128)(2,1)}), bf16[64,32,128]{2,1,0:T(8,128)(2,1)S(1)}, u32[]{:S(2)}, u32[]{:S(2)}) async-start(bf16[64,32,128]{2,1,0:T(8,128)(2,1)} %bitcast.4), calls=%async_computation | async-start | bytes 1048576 | tf_op jit(solution)/shard_map/all_to_all | solution.py:333
  63.3 20.8 %copy-start.8 = (f32[2,1280,128]{2,1,0:T(8,128)S(1)}, f32[2,1280,128]{2,1,0:T(8,128)}, u32[]{:S(2)}) copy-start(f32[2,1280,128]{2,1,0:T(8,128)} %select_add_fusion) | copy-start | bytes 3932164
  63.3 20.8 %collective-permute-start.7 = (bf16[2,1280,128]{2,1,0:T(8,128)(2,1)}, bf16[2,1280,128]{2,1,0:T(8,128)(2,1)}, u32[]{:S(2)}, u32[]{:S(2)}) collective-permute-start(bf16[2,1280,128]{2,1,0:T(8,128)(2,1)} %add_convert_fusion), channel_id=1, source_target_pairs={{0,2},{1,3},{2,4},{3,5},{4,6},{5,7},{6,8},{7,9},{8,10},{9,11},{10,... | collective-permute-start | bytes 1966088 | tf_op jit(solution)/shard_map/ppermute | solution.py:282
  75.8 18.0 %all-to-all-start.1 = ((bf16[64,32,128]{2,1,0:T(8,128)(2,1)}), bf16[64,32,128]{2,1,0:T(8,128)(2,1)S(1)}, u32[]{:S(2)}, u32[]{:S(2)}) async-start(bf16[64,32,128]{2,1,0:T(8,128)(2,1)} %broadcast_in_dim.43), calls=%async_computation.1 | async-start | bytes 1048576 | tf_op jit(solution)/shard_map/all_to_all | solution.py:336
  85.3 4.8 %collective-permute-start.8 = (bf16[2,256,128]{2,1,0:T(8,128)(2,1)S(1)}, bf16[2,256,128]{2,1,0:T(8,128)(2,1)S(1)}, u32[]{:S(2)}, u32[]{:S(2)}) collective-permute-start(bf16[2,256,128]{2,1,0:T(8,128)(2,1)S(1)} %slice.17), channel_id=1, source_target_pairs={{0,32},{1,33},{2,34},{3,35},{4,36},{5,37},{6,38},{7,39},{8,40},{9,... | collective-permute-start | bytes 393224 | tf_op jit(solution)/shard_map/ppermute | solution.py:282
  93.8 4.1 %collective-permute-start.9 = (bf16[2048,128]{1,0:T(8,128)(2,1)S(1)}, bf16[2048,128]{1,0:T(8,128)(2,1)S(1)}, u32[]{:S(2)}, u32[]{:S(2)}) collective-permute-start(bf16[2048,128]{1,0:T(8,128)(2,1)S(1)} %bitcast.19), channel_id=1, source_target_pairs={{0,1},{1,0},{2,3},{3,2},{4,5},{5,4},{6,7},{7,6},{8,9},{9,8},{10,11... | collective-permute-start | bytes 1572872 | tf_op jit(solution)/shard_map/ppermute | solution.py:282

commit v2 on v1

--- a/solution.py
+++ b/solution.py
@@ -40,7 +40,7 @@
 
 def slots_kernel(
     info, fwd, bwd, probe, meas, own, own_low, nxt, nxt_low, sec, sec_low,
-    g_own, g_next, g_sec, acc_keep, acc_send,
+    g_own, g_next, g_next_low, g_sec, acc_keep, acc_send,
     ext, mid, acc, owin, xs, hb, gb, kb,
 ):
     slots = meas.shape[0]
@@ -184,7 +184,8 @@
 
     lax.fori_loop(0, lax.div(live + 1, 2), pair_of_slots, 0)
 
-    g_next[...] = mid[...].astype(BF16)
+    g_next[...] = mid[:, :tile_rows, :].astype(BF16)
+    g_next_low[...] = mid[:, tile_rows:, :].astype(BF16)
     for m in range(modes):
         for at in range(0, win, 8):
             for h in range(2):
@@ -247,10 +248,11 @@
     return pl.pallas_call(
         slots_kernel,
         in_specs=[pl.BlockSpec(memory_space=pltpu.SMEM)] + [vmem] * 10,
-        out_specs=[vmem] * 5,
+        out_specs=[vmem] * 6,
         out_shape=[
             jax.ShapeDtypeStruct(tall, F32),
-            jax.ShapeDtypeStruct(tall, BF16),
+            jax.ShapeDtypeStruct(own.shape, BF16),
+            jax.ShapeDtypeStruct(own_low.shape, BF16),
             jax.ShapeDtypeStruct(tall, F32),
             jax.ShapeDtypeStruct(flat, F32),
             jax.ShapeDtypeStruct(flat, BF16),
@@ -265,9 +267,30 @@
             pltpu.VMEM((2, modes, 2, win, win), BF16),
             pltpu.VMEM(blocks, BF16),
         ],
-        compiler_params=pltpu.CompilerParams(vmem_limit_bytes=32 * 1024 * 1024),
+        compiler_params=pltpu.CompilerParams(vmem_limit_bytes=22 * 1024 * 1024),
         name="slots",
     )(info, fwd, bwd, probe, measured, own, own_low, nxt, nxt_low, sec, sec_low)
+
+
+def share_kernel(scale, parts, out):
+    total = parts[0].astype(F32)
+    for i in range(1, parts.shape[0]):
+        total = total + parts[i].astype(F32)
+    total = (total * scale).astype(BF16)
+    for i in range(out.shape[0]):
+        out[i] = total
+
+
+def share_out(parts, scale):
+    vmem = pl.BlockSpec(memory_space=pltpu.VMEM)
+    return pl.pallas_call(
+        functools.partial(share_kernel, scale),
+        in_specs=[vmem],
+        out_specs=vmem,
+        out_shape=jax.ShapeDtypeStruct(parts.shape, BF16),
+        compiler_params=pltpu.CompilerParams(vmem_limit_bytes=4 * 1024 * 1024),
+        name="share",
+    )(parts)
 
 
 def moved(value, target):
@@ -309,20 +332,19 @@
             core[None],
         ]
     )
-    g_own, g_next, g_sec, acc_keep, acc_send = run_slots(
+    g_own, g_next, g_next_low, g_sec, acc_keep, acc_send = run_slots(
         info, *prepared, object_field, own_low, nxt, nxt_low, sec, sec_low
     )
 
     acc_got = swap_cores(acc_send)
     near = swap_cores(g_next)
     chip_sum = (acc_keep + acc_got.astype(F32)).astype(BF16)
-    chip_sum, near = lax.optimization_barrier((chip_sum, near))
-    near = lax.optimization_barrier(near.astype(F32))
+    near, near_low = lax.optimization_barrier((near, g_next_low))
+    near = jnp.concatenate([near, swap_cores(near_low)], axis=1).astype(F32)
     none = jnp.zeros_like(near)
-    inner, near = lax.optimization_barrier((g_own + jnp.where(core == 1, near, none), near))
     outward = (g_sec + jnp.where(core == 0, near, none)).astype(BF16)
     far = moved(outward, lambda a, b: (a, b + 2))
-    total = inner + far.astype(F32)
+    total = g_own + jnp.where(core == 1, near, none) + far.astype(F32)
     rim = moved(total[:, tile_rows:].astype(BF16), lambda a, b: (a + 1, b))
 
     groups = [[i for i in range(devices) if i % 2 == c] for c in range(2)]
@@ -331,9 +353,7 @@
         axis_index_groups=groups, tiled=True,
     )
     share = exchange(chip_sum.reshape(devices // 2, -1, LANES))
-    scale = 1.0 / jnp.sqrt(jnp.float32(devices * slot_count))
-    share = (jnp.sum(share.astype(F32), axis=0) * scale).astype(BF16)
-    mine = exchange(jnp.broadcast_to(share[None], (devices // 2,) + share.shape))
+    mine = exchange(share_out(share, 1.0 / float(np.sqrt(devices * slot_count))))
     mine, rim = lax.optimization_barrier((mine, rim))
     mine = mine.reshape(-1, LANES)
     part = lax.broadcasted_iota(jnp.int32, (2,) + mine.shape, 0)

time: 101 us -> 104 us (1.030)
  starting transfers between devices: 35.5 us -> 49.8 us
  Pallas kernels: 17.9 us -> 8.27 us
  waiting for transfers between devices: 27.2 us -> 30.8 us
  other arithmetic: 8.81 us -> 5.29 us
  local copies, waits for them, and re-layouts: 8.52 us -> 7.45 us
    ppermute x10 -> x11, starting transfers between devices: 15.1 us -> 29.6 us  [moved(): return lax.ppermute(value, ('rows', 'cols'), pairs)]
    pallas_call x1, Pallas kernels: 16.8 us -> 6.22 us  [run_slots(): pl.pallas_call(slots_kernel, in_specs=[pl.BlockSpec(memory_space=pltpu.SM...]
    all_to_all x1, waiting for transfers between devices: 7.59 us -> 13.3 us  [local(): share = exchange(chip_sum.reshape(devices // 2, -1, LANES))]
    all_to_all x1, starting transfers between devices: 15.7 us -> 11 us  [local(): share = exchange(chip_sum.reshape(devices // 2, -1, LANES))]
    all_to_all x1, starting transfers between devices: 4.69 us -> 9.18 us  [local(): exchange(share_out(share, 1.0 / float(np.sqrt(devices * slot_count))))]
    ppermute x10 -> x11, waiting for transfers between devices: 16 us -> 14.6 us  [moved(): return lax.ppermute(value, ('rows', 'cols'), pairs)]
    convert_element_type x1, other arithmetic: 2.25 us -> 0.93 us  [local(): chip_sum = (acc_keep + acc_got.astype(F32)).astype(BF16)]
    add x2 -> x1, other arithmetic: 2.64 us -> 1.45 us  [local(): total = g_own + jnp.where(core == 1, near, none) + far.astype(F32)]
  transfers between devices with their start and end apart: 12 -> 13, of which waited for: 8 -> 8; matrix products, arithmetic and copies ran while one was open for 8% -> 5% of each run, Pallas kernels for 1% -> 2%
where the time goes in v2:
time: 104 us; the launch traced here: 103 us
  starting transfers between devices  49.8 us (48%)
  waiting for transfers between devices  30.8 us (30%)
  Pallas kernels  8.27 us (8%)
  local copies, waits for them, and re-layouts  7.45 us (7%)
  other arithmetic  5.29 us (5%)
  between operations  1.47 us (1%)
    ppermute x11, starting transfers between devices, moved(): return lax.ppermute(value, ('rows', 'cols'), pairs)  29.6 us
    ppermute x11, waiting for transfers between devices, moved(): return lax.ppermute(value, ('rows', 'cols'), pairs)  14.6 us
    all_to_all x1, waiting for transfers between devices, local(): share = exchange(chip_sum.reshape(devices // 2, -1, LANES))  13.3 us
    all_to_all x1, starting transfers between devices, local(): share = exchange(chip_sum.reshape(devices // 2, -1, LANES))  11 us
    all_to_all x1, starting transfers between devices, local(): exchange(share_out(share, 1.0 / float(np.sqrt(devices * slot_count))))  9.18 us
    unnamed x20, local copies, waits for them, and re-layouts  6.51 us
    pallas_call x1, Pallas kernels, run_slots(): pl.pallas_call(slots_kernel, in_specs=[pl.BlockSpec(memory_space=pltpu.SM...  6.22 us
    all_to_all x1, waiting for transfers between devices, local(): exchange(share_out(share, 1.0 / float(np.sqrt(devices * slot_count))))  2.92 us
  transfers between devices with their start and end apart: 13, of which 8 were waited for; matrix products, arithmetic and copies ran while one was open for 5% of the time, Pallas kernels for 2%

profile of v2, /device:TPU:1, one launch (start us, length us, event | category | flops | bytes accessed | tf_op | source)
XLA Modules:
  0.0 103.1 jit_solution(16007399146865015522)
XLA Ops:
  0.6 1.3 %collective-permute-start = (bf16[2,1024,128]{2,1,0:T(8,128)(2,1)}, bf16[2,1024,128]{2,1,0:T(8,128)(2,1)S(1)}, u32[]{:S(2)}, u32[]{:S(2)}) collective-permute-start(bf16[2,1024,128]{2,1,0:T(8,128)(2,1)} %own.1), channel_id=1, source_target_pairs={{2,0},{3,1},{4,2},{5,3},{6,4},{7,5},{8,6},{9,7},{10,8},{11,9},{12,... | collective-permute-start | bytes 1572872 | tf_op jit(solution)/shard_map/ppermute | solution.py:305
  1.9 0.9 slice.10
  2.9 1.3 %collective-permute-start.1 = (bf16[2,256,128]{2,1,0:T(8,128)(2,1)S(1)}, bf16[2,256,128]{2,1,0:T(8,128)(2,1)S(1)}, u32[]{:S(2)}, u32[]{:S(2)}) collective-permute-start(bf16[2,256,128]{2,1,0:T(8,128)(2,1)S(1)} %slice.10), channel_id=1, source_target_pairs={{32,0},{33,1},{34,2},{35,3},{36,4},{37,5},{38,6},{39,7},{40,8},{41... | collective-permute-start | bytes 393224 | tf_op jit(solution)/shard_map/ppermute | solution.py:305
  4.2 1.3 %collective-permute-start.3 = (bf16[2,256,128]{2,1,0:T(8,128)(2,1)S(1)}, bf16[2,256,128]{2,1,0:T(8,128)(2,1)S(1)}, u32[]{:S(2)}, u32[]{:S(2)}) collective-permute-start(bf16[2,256,128]{2,1,0:T(8,128)(2,1)S(1)} %slice.10), channel_id=1, source_target_pairs={{34,0},{35,1},{36,2},{37,3},{38,4},{39,5},{40,6},{41,7},{42,8},{43... | collective-permute-start | bytes 393224 | tf_op jit(solution)/shard_map/ppermute | solution.py:305
  5.5 0.0 copy-start.1
  5.5 1.6 %copy-done.1 = f32[2,4,256,256]{3,2,1,0:T(8,128)S(1)} copy-done((f32[2,4,256,256]{3,2,1,0:T(8,128)S(1)}, f32[2,4,256,256]{3,2,1,0:T(8,128)}, u32[]{:S(2)}) %copy-start.1) | copy-done | bytes 2097176
  7.1 0.0 copy-start.2
  7.1 1.2 %copy-done.2 = bf16[1,8,256,256]{3,2,1,0:T(8,128)(2,1)S(1)} copy-done((bf16[1,8,256,256]{3,2,1,0:T(8,128)(2,1)S(1)}, bf16[1,8,256,256]{3,2,1,0:T(8,128)(2,1)}, u32[]{:S(2)}) %copy-start.2) | copy-done | bytes 1048600
  8.3 0.0 copy-start.3
  8.3 0.9 copy-done.3
  9.2 0.0 copy-start.4
  9.2 0.9 copy-done.4
  10.2 0.0 copy-start.5
  10.2 0.9 copy-done.5
  11.1 0.0 copy-start
  11.1 1.1 %prepare.1 = (bf16[2,256,256]{2,1,0:T(8,128)(2,1)S(1)}, bf16[2,256,256]{2,1,0:T(8,128)(2,1)S(1)}, f32[2,4,256,256]{3,2,1,0:T(8,128)S(1)}, bf16[8,256,256]{2,1,0:T(8,128)(2,1)S(1)}) custom-call(bf16[2,256,256]{2,1,0:T(8,128)(2,1)S(1)} %copy-done.3, bf16[2,256,256]{2,1,0:T(8,128)(2,1)S(1)} %copy-done.4, bf16[2,256,256]{2,1,0:T(8,128)(2,1)S(1)} %copy-done.5, ...), custom_call_target="tpu_custom_call" | custom-call | flops 536870912 | bytes 8388608 | tf_op jit(solution)/shard_map/prepare/pallas_call | solution.py:220
  12.3 0.0 copy-start.8
  12.3 0.0 copy-start.9
  12.3 7.4 %collective-permute-done.sec = bf16[2,1024,128]{2,1,0:T(8,128)(2,1)S(1)} collective-permute-done((bf16[2,1024,128]{2,1,0:T(8,128)(2,1)}, bf16[2,1024,128]{2,1,0:T(8,128)(2,1)S(1)}, u32[]{:S(2)}, u32[]{:S(2)}) %collective-permute-start) | collective-permute-done | bytes 524320 | tf_op jit(solution)/shard_map/ppermute | solution.py:305
  19.7 0.0 copy-done
  19.7 0.1 broadcast_select_fusion
  19.7 1.3 %collective-permute-start.2 = (bf16[2,1024,128]{2,1,0:T(8,128)(2,1)S(1)}, bf16[2,1024,128]{2,1,0:T(8,128)(2,1)S(1)}, u32[]{:S(2)}, u32[]{:S(2)}) collective-permute-start(bf16[2,1024,128]{2,1,0:T(8,128)(2,1)S(1)} %broadcast_select_fusion), channel_id=1, source_target_pairs={{0,1},{1,0},{2,3},{3,2},{4,5},{5,4},{6,7},{7,6},{8,9},{9,8},{10,11... | collective-permute-start | bytes 1572872 | tf_op jit(solution)/shard_map/ppermute | solution.py:305
  21.0 0.0 collective-permute-done.1.own_low
  21.0 0.0 collective-permute-done.3.sec_low
  21.1 0.1 collective-permute-start.4
  21.2 0.0 copy-done.8
  21.2 0.0 copy-done.9
  21.8 0.1 pad_add_fusion.info
  21.9 0.8 collective-permute-done.4.nxt_low
  22.8 0.0 collective-permute-done.2.nxt
  22.8 6.2 %slots.1 = (f32[2,1280,128]{2,1,0:T(8,128)S(1)}, bf16[2,1024,128]{2,1,0:T(8,128)(2,1)S(1)}, bf16[2,256,128]{2,1,0:T(8,128)(2,1)S(1)}, f32[2,1280,128]{2,1,0:T(8,...) custom-call(s32[18]{0:T(128)S(1)} %pad_add_fusion.info, ...), custom_call_target="tpu_custom_call" | custom-call | tf_op jit(solution)/shard_map/slots/pallas_call | solution.py:248
  29.0 10.0 %collective-permute-start.5 = (bf16[2,1024,128]{2,1,0:T(8,128)(2,1)S(1)}, bf16[2,1024,128]{2,1,0:T(8,128)(2,1)S(1)}, u32[]{:S(2)}, u32[]{:S(2)}) collective-permute-start(bf16[2,1024,128]{2,1,0:T(8,128)(2,1)S(1)} %get-tuple-element.31), channel_id=1, source_target_pairs={{0,1},{1,0},{2,3},{3,2},{4,5},{5,4},{6,7},{7,6},{8,9},{9,8},{10,11... | collective-permute-start | bytes 1572872 | tf_op jit(solution)/shard_map/ppermute | solution.py:305
  39.0 1.5 %collective-permute-done.5 = bf16[2,1024,128]{2,1,0:T(8,128)(2,1)S(1)} collective-permute-done((bf16[2,1024,128]{2,1,0:T(8,128)(2,1)S(1)}, bf16[2,1024,128]{2,1,0:T(8,128)(2,1)S(1)}, u32[]{:S(2)}, u32[]{:S(2)}) %collective-permute-start.5) | collective-permute-done | bytes 524320 | tf_op jit(solution)/shard_map/ppermute | solution.py:305
  40.5 0.0 copy-start.6
  40.5 0.4 collective-permute-start.6
  40.9 0.1 collective-permute-start.8
  41.1 0.8 collective-permute-done.6
  41.9 0.2 fusion.3
  42.1 0.0 copy-done.6
  42.1 8.4 %collective-permute-start.7 = (bf16[2,1280,128]{2,1,0:T(8,128)(2,1)S(1)}, bf16[2,1280,128]{2,1,0:T(8,128)(2,1)S(1)}, u32[]{:S(2)}, u32[]{:S(2)}) collective-permute-start(bf16[2,1280,128]{2,1,0:T(8,128)(2,1)S(1)} %fusion.3), channel_id=1, source_target_pairs={{0,2},{1,3},{2,4},{3,5},{4,6},{5,7},{6,8},{7,9},{8,10},{9,11},{10,... | collective-permute-start | bytes 1966088 | tf_op jit(solution)/shard_map/ppermute | solution.py:305
  50.5 0.0 collective-permute-done.8
  50.5 0.9 add_convert_fusion
  51.4 11.0 %all-to-all-start = ((bf16[64,32,128]{2,1,0:T(8,128)(2,1)}), bf16[64,32,128]{2,1,0:T(8,128)(2,1)S(1)}, u32[]{:S(2)}, u32[]{:S(2)}) async-start(bf16[64,32,128]{2,1,0:T(8,128)(2,1)} %bitcast.4), calls=%async_computation | async-start | bytes 1048576 | tf_op jit(solution)/shard_map/all_to_all | solution.py:355
  62.4 13.3 %all-to-all-done.parts = bf16[64,32,128]{2,1,0:T(8,128)(2,1)S(1)} async-done(((bf16[64,32,128]{2,1,0:T(8,128)(2,1)}), bf16[64,32,128]{2,1,0:T(8,128)(2,1)S(1)}, u32[]{:S(2)}, u32[]{:S(2)}) %all-to-all-start) | async-done | bytes 524320 | tf_op jit(solution)/shard_map/all_to_all | solution.py:355
  75.7 0.9 share.1
  76.6 9.2 %all-to-all-start.1 = ((bf16[64,32,128]{2,1,0:T(8,128)(2,1)}), bf16[64,32,128]{2,1,0:T(8,128)(2,1)S(1)}, u32[]{:S(2)}, u32[]{:S(2)}) async-start(bf16[64,32,128]{2,1,0:T(8,128)(2,1)} %share.1), calls=%async_computation.1 | async-start | bytes 1048576 | tf_op jit(solution)/shard_map/all_to_all | solution.py:356
  85.8 0.0 collective-permute-done.7
  85.8 0.0 copy-start.7
  85.8 0.8 copy-done.7
  86.7 1.5 %fusion.1 = f32[2,1280,128]{2,1,0:T(8,128)S(1)} fusion(f32[2,1280,128]{2,1,0:T(8,128)S(1)} %get-tuple-element.30, bf16[2,1280,128]{2,1,0:T(8,128)(2,1)} %copy-done.7, pred[]{:T(512)S(6)} %eq.16, bf16[2,256,128]{2,1,0:T(8,128)(2,1)S(1)} %collective-permute-done.6, bf16[2,1024,128]{2,1,0:T(8,128)(2,1)} %copy-done.6), kind=kLoop, calls=%fused_computation.3 | loop fusion | flops 2621440 | bytes 3932161 | tf_op jit(solution)/shard_map/add | solution.py:347
  88.1 2.9 %collective-permute-start.9 = (bf16[2,256,128]{2,1,0:T(8,128)(2,1)S(1)}, bf16[2,256,128]{2,1,0:T(8,128)(2,1)S(1)}, u32[]{:S(2)}, u32[]{:S(2)}) collective-permute-start(bf16[2,256,128]{2,1,0:T(8,128)(2,1)S(1)} %slice.17), channel_id=1, source_target_pairs={{0,32},{1,33},{2,34},{3,35},{4,36},{5,37},{6,38},{7,39},{8,40},{9,... | collective-permute-start | bytes 393224 | tf_op jit(solution)/shard_map/ppermute | solution.py:305
  91.1 3.5 %collective-permute-done.9 = bf16[2,256,128]{2,1,0:T(8,128)(2,1)S(1)} collective-permute-done((bf16[2,256,128]{2,1,0:T(8,128)(2,1)S(1)}, bf16[2,256,128]{2,1,0:T(8,128)(2,1)S(1)}, u32[]{:S(2)}, u32[]{:S(2)}) %collective-permute-start.9) | collective-permute-done | bytes 131104 | tf_op jit(solution)/shard_map/ppermute | solution.py:305
  94.6 2.9 %all-to-all-done.1 = bf16[64,32,128]{2,1,0:T(8,128)(2,1)S(1)} async-done(((bf16[64,32,128]{2,1,0:T(8,128)(2,1)}), bf16[64,32,128]{2,1,0:T(8,128)(2,1)S(1)}, u32[]{:S(2)}, u32[]{:S(2)}) %all-to-all-start.1) | async-done | bytes 524320 | tf_op jit(solution)/shard_map/all_to_all | solution.py:356
  97.5 2.5 %collective-permute-start.10 = (bf16[2048,128]{1,0:T(8,128)(2,1)S(1)}, bf16[2048,128]{1,0:T(8,128)(2,1)S(1)}, u32[]{:S(2)}, u32[]{:S(2)}) collective-permute-start(bf16[2048,128]{1,0:T(8,128)(2,1)S(1)} %bitcast.19), channel_id=1, source_target_pairs={{0,1},{1,0},{2,3},{3,2},{4,5},{5,4},{6,7},{7,6},{8,9},{9,8},{10,11... | collective-permute-start | bytes 1572872 | tf_op jit(solution)/shard_map/ppermute | solution.py:305
  100.0 1.0 %slice_add_fusion = f32[2,1024,128]{2,1,0:T(8,128)} fusion(f32[2,1280,128]{2,1,0:T(8,128)S(1)} %fusion.1, bf16[2,256,128]{2,1,0:T(8,128)(2,1)S(1)} %collective-permute-done.9), kind=kLoop, calls=%fused_computation.6 | loop fusion | flops 524288 | bytes 2228224 | tf_op jit(solution)/shard_map/add | solution.py:364
  101.1 0.5 collective-permute-done.10
  101.6 1.5 %select_convert_fusion = f32[2,4,256,256]{3,2,1,0:T(8,128)} fusion(pred[2]{0:T(512)(128)(4,1)S(1)} %iota_compare_fusion, bf16[4,256,256]{2,1,0:T(8,128)(2,1)S(1)} %bitcast.21, bf16[4,256,256]{2,1,0:T(8,128)(2,1)S(1)} %bitcast.20), kind=kLoop, calls=%fused_computation.7 | loop fusion | flops 1048576 | bytes 3145730 | tf_op jit(solution)/shard_map/convert_element_type | solution.py:360
  (4 shorter events, 0.0 us)
Async XLA Ops:
  0.6 19.0 %collective-permute-start = (bf16[2,1024,128]{2,1,0:T(8,128)(2,1)}, bf16[2,1024,128]{2,1,0:T(8,128)(2,1)S(1)}, u32[]{:S(2)}, u32[]{:S(2)}) collective-permute-start(bf16[2,1024,128]{2,1,0:T(8,128)(2,1)} %own.1), channel_id=1, source_target_pairs={{2,0},{3,1},{4,2},{5,3},{6,4},{7,5},{8,6},{9,7},{10,8},{11,9},{12,... | collective-permute-start | bytes 1572872 | tf_op jit(solution)/shard_map/ppermute | solution.py:305
  2.9 18.2 %collective-permute-start.1 = (bf16[2,256,128]{2,1,0:T(8,128)(2,1)S(1)}, bf16[2,256,128]{2,1,0:T(8,128)(2,1)S(1)}, u32[]{:S(2)}, u32[]{:S(2)}) collective-permute-start(bf16[2,256,128]{2,1,0:T(8,128)(2,1)S(1)} %slice.10), channel_id=1, source_target_pairs={{32,0},{33,1},{34,2},{35,3},{36,4},{37,5},{38,6},{39,7},{40,8},{41... | collective-permute-start | bytes 393224 | tf_op jit(solution)/shard_map/ppermute | solution.py:305
  4.2 16.9 %collective-permute-start.3 = (bf16[2,256,128]{2,1,0:T(8,128)(2,1)S(1)}, bf16[2,256,128]{2,1,0:T(8,128)(2,1)S(1)}, u32[]{:S(2)}, u32[]{:S(2)}) collective-permute-start(bf16[2,256,128]{2,1,0:T(8,128)(2,1)S(1)} %slice.10), channel_id=1, source_target_pairs={{34,0},{35,1},{36,2},{37,3},{38,4},{39,5},{40,6},{41,7},{42,8},{43... | collective-permute-start | bytes 393224 | tf_op jit(solution)/shard_map/ppermute | solution.py:305
  5.5 1.6 %copy-start.1 = (f32[2,4,256,256]{3,2,1,0:T(8,128)S(1)}, f32[2,4,256,256]{3,2,1,0:T(8,128)}, u32[]{:S(2)}) copy-start(f32[2,4,256,256]{3,2,1,0:T(8,128)} %probe.1) | copy-start | bytes 6291460
  7.1 1.2 %copy-start.2 = (bf16[1,8,256,256]{3,2,1,0:T(8,128)(2,1)S(1)}, bf16[1,8,256,256]{3,2,1,0:T(8,128)(2,1)}, u32[]{:S(2)}) copy-start(bf16[1,8,256,256]{3,2,1,0:T(8,128)(2,1)} %meas.1) | copy-start | bytes 3145732
  8.3 0.9 copy-start.3
  9.2 0.9 copy-start.4
  10.2 0.9 copy-start.5
  11.1 8.5 %copy-start = (bf16[2,1024,128]{2,1,0:T(8,128)(2,1)S(1)}, bf16[2,1024,128]{2,1,0:T(8,128)(2,1)}, u32[]{:S(2)}) copy-start(bf16[2,1024,128]{2,1,0:T(8,128)(2,1)} %own.1) | copy-start | bytes 1572868
  12.3 8.9 %copy-start.8 = (s32[1,8]{1,0:T(1,128)S(1)}, s32[1,8]{1,0:T(1,128)}, u32[]{:S(2)}) copy-start(s32[1,8]{1,0:T(1,128)} %param.13) | copy-start | bytes 100
  12.3 8.9 %copy-start.9 = (s32[1,8]{1,0:T(1,128)S(1)}, s32[1,8]{1,0:T(1,128)}, u32[]{:S(2)}) copy-start(s32[1,8]{1,0:T(1,128)} %param.12) | copy-start | bytes 100
  19.7 3.1 %collective-permute-start.2 = (bf16[2,1024,128]{2,1,0:T(8,128)(2,1)S(1)}, bf16[2,1024,128]{2,1,0:T(8,128)(2,1)S(1)}, u32[]{:S(2)}, u32[]{:S(2)}) collective-permute-start(bf16[2,1024,128]{2,1,0:T(8,128)(2,1)S(1)} %broadcast_select_fusion), channel_id=1, source_target_pairs={{0,1},{1,0},{2,3},{3,2},{4,5},{5,4},{6,7},{7,6},{8,9},{9,8},{10,11... | collective-permute-start | bytes 1572872 | tf_op jit(solution)/shard_map/ppermute | solution.py:305
  21.1 1.7 %collective-permute-start.4 = (bf16[2,256,128]{2,1,0:T(8,128)(2,1)S(1)}, bf16[2,256,128]{2,1,0:T(8,128)(2,1)S(1)}, u32[]{:S(2)}, u32[]{:S(2)}) collective-permute-start(bf16[2,256,128]{2,1,0:T(8,128)(2,1)S(1)} %broadcast_select_fusion.1), channel_id=1, source_target_pairs={{0,1},{1,0},{2,3},{3,2},{4,5},{5,4},{6,7},{7,6},{8,9},{9,8},{10,11... | collective-permute-start | bytes 393224 | tf_op jit(solution)/shard_map/ppermute | solution.py:305
  29.0 11.5 %collective-permute-start.5 = (bf16[2,1024,128]{2,1,0:T(8,128)(2,1)S(1)}, bf16[2,1024,128]{2,1,0:T(8,128)(2,1)S(1)}, u32[]{:S(2)}, u32[]{:S(2)}) collective-permute-start(bf16[2,1024,128]{2,1,0:T(8,128)(2,1)S(1)} %get-tuple-element.31), channel_id=1, source_target_pairs={{0,1},{1,0},{2,3},{3,2},{4,5},{5,4},{6,7},{7,6},{8,9},{9,8},{10,11... | collective-permute-start | bytes 1572872 | tf_op jit(solution)/shard_map/ppermute | solution.py:305
  40.5 1.5 %copy-start.6 = (bf16[2,1024,128]{2,1,0:T(8,128)(2,1)}, bf16[2,1024,128]{2,1,0:T(8,128)(2,1)S(1)}, u32[]{:S(2)}) copy-start(bf16[2,1024,128]{2,1,0:T(8,128)(2,1)S(1)} %collective-permute-done.5) | copy-start | bytes 1572868
  40.5 1.4 %collective-permute-start.6 = (bf16[2,256,128]{2,1,0:T(8,128)(2,1)S(1)}, bf16[2,256,128]{2,1,0:T(8,128)(2,1)S(1)}, u32[]{:S(2)}, u32[]{:S(2)}) collective-permute-start(bf16[2,256,128]{2,1,0:T(8,128)(2,1)S(1)} %get-tuple-element.34), channel_id=1, source_target_pairs={{0,1},{1,0},{2,3},{3,2},{4,5},{5,4},{6,7},{7,6},{8,9},{9,8},{10,11... | collective-permute-start | bytes 393224 | tf_op jit(solution)/shard_map/ppermute | solution.py:305
  40.9 9.5 %collective-permute-start.8 = (bf16[2048,128]{1,0:T(8,128)(2,1)S(1)}, bf16[2048,128]{1,0:T(8,128)(2,1)S(1)}, u32[]{:S(2)}, u32[]{:S(2)}) collective-permute-start(bf16[2048,128]{1,0:T(8,128)(2,1)S(1)} %get-tuple-element.37), channel_id=1, source_target_pairs={{0,1},{1,0},{2,3},{3,2},{4,5},{5,4},{6,7},{7,6},{8,9},{9,8},{10,11... | collective-permute-start | bytes 1572872 | tf_op jit(solution)/shard_map/ppermute | solution.py:305
  42.1 43.7 %collective-permute-start.7 = (bf16[2,1280,128]{2,1,0:T(8,128)(2,1)S(1)}, bf16[2,1280,128]{2,1,0:T(8,128)(2,1)S(1)}, u32[]{:S(2)}, u32[]{:S(2)}) collective-permute-start(bf16[2,1280,128]{2,1,0:T(8,128)(2,1)S(1)} %fusion.3), channel_id=1, source_target_pairs={{0,2},{1,3},{2,4},{3,5},{4,6},{5,7},{6,8},{7,9},{8,10},{9,11},{10,... | collective-permute-start | bytes 1966088 | tf_op jit(solution)/shard_map/ppermute | solution.py:305
  51.4 24.3 %all-to-all-start = ((bf16[64,32,128]{2,1,0:T(8,128)(2,1)}), bf16[64,32,128]{2,1,0:T(8,128)(2,1)S(1)}, u32[]{:S(2)}, u32[]{:S(2)}) async-start(bf16[64,32,128]{2,1,0:T(8,128)(2,1)} %bitcast.4), calls=%async_computation | async-start | bytes 1048576 | tf_op jit(solution)/shard_map/all_to_all | solution.py:355
  76.6 20.9 %all-to-all-start.1 = ((bf16[64,32,128]{2,1,0:T(8,128)(2,1)}), bf16[64,32,128]{2,1,0:T(8,128)(2,1)S(1)}, u32[]{:S(2)}, u32[]{:S(2)}) async-start(bf16[64,32,128]{2,1,0:T(8,128)(2,1)} %share.1), calls=%async_computation.1 | async-start | bytes 1048576 | tf_op jit(solution)/shard_map/all_to_all | solution.py:356
  85.8 0.8 copy-start.7
  88.1 6.4 %collective-permute-start.9 = (bf16[2,256,128]{2,1,0:T(8,128)(2,1)S(1)}, bf16[2,256,128]{2,1,0:T(8,128)(2,1)S(1)}, u32[]{:S(2)}, u32[]{:S(2)}) collective-permute-start(bf16[2,256,128]{2,1,0:T(8,128)(2,1)S(1)} %slice.17), channel_id=1, source_target_pairs={{0,32},{1,33},{2,34},{3,35},{4,36},{5,37},{6,38},{7,39},{8,40},{9,... | collective-permute-start | bytes 393224 | tf_op jit(solution)/shard_map/ppermute | solution.py:305
  97.5 4.1 %collective-permute-start.10 = (bf16[2048,128]{1,0:T(8,128)(2,1)S(1)}, bf16[2048,128]{1,0:T(8,128)(2,1)S(1)}, u32[]{:S(2)}, u32[]{:S(2)}) collective-permute-start(bf16[2048,128]{1,0:T(8,128)(2,1)S(1)} %bitcast.19), channel_id=1, source_target_pairs={{0,1},{1,0},{2,3},{3,2},{4,5},{5,4},{6,7},{7,6},{8,9},{9,8},{10,11... | collective-permute-start | bytes 1572872 | tf_op jit(solution)/shard_map/ppermute | solution.py:305

commit v3 on v2

--- a/solution.py
+++ b/solution.py
@@ -288,6 +288,7 @@
         in_specs=[vmem],
         out_specs=vmem,
         out_shape=jax.ShapeDtypeStruct(parts.shape, BF16),
+        cost_estimate=pl.CostEstimate(flops=0, bytes_accessed=128 << 20, transcendentals=0),
         compiler_params=pltpu.CompilerParams(vmem_limit_bytes=4 * 1024 * 1024),
         name="share",
     )(parts)

time: 104 us -> 105 us (level); the launches traced: 103 us -> 106 us
  starting transfers between devices: 49.8 us -> 44.2 us
  Pallas kernels: 8.27 us -> 13 us
  waiting for transfers between devices: 30.8 us -> 34.9 us
    ppermute x11, starting transfers between devices: 29.6 us -> 13 us  [moved(): return lax.ppermute(value, ('rows', 'cols'), pairs)]
    all_to_all x1, starting transfers between devices: 11 us -> 23.1 us  [local(): share = exchange(chip_sum.reshape(devices // 2, -1, LANES))]
    pallas_call x1, Pallas kernels: 6.22 us -> 10.9 us  [run_slots(): pl.pallas_call(slots_kernel, in_specs=[pl.BlockSpec(memory_space=pltpu.SM...]
    all_to_all x1, waiting for transfers between devices: 13.3 us -> 17.4 us  [local(): share = exchange(chip_sum.reshape(devices // 2, -1, LANES))]
    all_to_all x1, starting transfers between devices: 9.18 us -> 8.12 us  [local(): exchange(share_out(share, 1.0 / float(np.sqrt(devices * slot_count))))]
  transfers between devices with their start and end apart: 13 -> 13, of which waited for: 8 -> 8; matrix products, arithmetic and copies ran while one was open for 5% -> 4% of each run, Pallas kernels for 2% -> 2%
where the time goes in v3:
time: 105 us; the launch traced here: 106 us
  starting transfers between devices  44.2 us (42%)
  waiting for transfers between devices  34.9 us (33%)
  Pallas kernels  13 us (12%)
  local copies, waits for them, and re-layouts  7.45 us (7%)
  other arithmetic  5.29 us (5%)
  between operations  1.47 us (1%)
    all_to_all x1, starting transfers between devices, local(): share = exchange(chip_sum.reshape(devices // 2, -1, LANES))  23.1 us
    all_to_all x1, waiting for transfers between devices, local(): share = exchange(chip_sum.reshape(devices // 2, -1, LANES))  17.4 us
    ppermute x11, waiting for transfers between devices, moved(): return lax.ppermute(value, ('rows', 'cols'), pairs)  14.8 us
    ppermute x11, starting transfers between devices, moved(): return lax.ppermute(value, ('rows', 'cols'), pairs)  13 us
    pallas_call x1, Pallas kernels, run_slots(): pl.pallas_call(slots_kernel, in_specs=[pl.BlockSpec(memory_space=pltpu.SM...  10.9 us
    all_to_all x1, starting transfers between devices, local(): exchange(share_out(share, 1.0 / float(np.sqrt(devices * slot_count))))  8.12 us
    unnamed x20, local copies, waits for them, and re-layouts  6.51 us
    all_to_all x1, waiting for transfers between devices, local(): exchange(share_out(share, 1.0 / float(np.sqrt(devices * slot_count))))  2.77 us
  transfers between devices with their start and end apart: 13, of which 8 were waited for; matrix products, arithmetic and copies ran while one was open for 4% of the time, Pallas kernels for 2%

profile of v3, /device:TPU:1, one launch (start us, length us, event | category | flops | bytes accessed | tf_op | source)
XLA Modules:
  0.0 106.4 jit_solution(16007399146865015522)
XLA Ops:
  0.6 1.3 %collective-permute-start = (bf16[2,1024,128]{2,1,0:T(8,128)(2,1)}, bf16[2,1024,128]{2,1,0:T(8,128)(2,1)S(1)}, u32[]{:S(2)}, u32[]{:S(2)}) collective-permute-start(bf16[2,1024,128]{2,1,0:T(8,128)(2,1)} %own.1), channel_id=1, source_target_pairs={{2,0},{3,1},{4,2},{5,3},{6,4},{7,5},{8,6},{9,7},{10,8},{11,9},{12,... | collective-permute-start | bytes 1572872 | tf_op jit(solution)/shard_map/ppermute | solution.py:306
  1.9 0.9 slice.10
  2.9 1.3 %collective-permute-start.1 = (bf16[2,256,128]{2,1,0:T(8,128)(2,1)S(1)}, bf16[2,256,128]{2,1,0:T(8,128)(2,1)S(1)}, u32[]{:S(2)}, u32[]{:S(2)}) collective-permute-start(bf16[2,256,128]{2,1,0:T(8,128)(2,1)S(1)} %slice.10), channel_id=1, source_target_pairs={{32,0},{33,1},{34,2},{35,3},{36,4},{37,5},{38,6},{39,7},{40,8},{41... | collective-permute-start | bytes 393224 | tf_op jit(solution)/shard_map/ppermute | solution.py:306
  4.2 1.3 %collective-permute-start.3 = (bf16[2,256,128]{2,1,0:T(8,128)(2,1)S(1)}, bf16[2,256,128]{2,1,0:T(8,128)(2,1)S(1)}, u32[]{:S(2)}, u32[]{:S(2)}) collective-permute-start(bf16[2,256,128]{2,1,0:T(8,128)(2,1)S(1)} %slice.10), channel_id=1, source_target_pairs={{34,0},{35,1},{36,2},{37,3},{38,4},{39,5},{40,6},{41,7},{42,8},{43... | collective-permute-start | bytes 393224 | tf_op jit(solution)/shard_map/ppermute | solution.py:306
  5.5 0.0 copy-start.1
  5.5 1.6 %copy-done.1 = f32[2,4,256,256]{3,2,1,0:T(8,128)S(1)} copy-done((f32[2,4,256,256]{3,2,1,0:T(8,128)S(1)}, f32[2,4,256,256]{3,2,1,0:T(8,128)}, u32[]{:S(2)}) %copy-start.1) | copy-done | bytes 2097176
  7.1 0.0 copy-start.2
  7.1 1.2 %copy-done.2 = bf16[1,8,256,256]{3,2,1,0:T(8,128)(2,1)S(1)} copy-done((bf16[1,8,256,256]{3,2,1,0:T(8,128)(2,1)S(1)}, bf16[1,8,256,256]{3,2,1,0:T(8,128)(2,1)}, u32[]{:S(2)}) %copy-start.2) | copy-done | bytes 1048600
  8.3 0.0 copy-start.3
  8.3 0.9 copy-done.3
  9.2 0.0 copy-start.4
  9.2 0.9 copy-done.4
  10.2 0.0 copy-start.5
  10.2 0.9 copy-done.5
  11.1 0.0 copy-start
  11.1 1.1 %prepare.1 = (bf16[2,256,256]{2,1,0:T(8,128)(2,1)S(1)}, bf16[2,256,256]{2,1,0:T(8,128)(2,1)S(1)}, f32[2,4,256,256]{3,2,1,0:T(8,128)S(1)}, bf16[8,256,256]{2,1,0:T(8,128)(2,1)S(1)}) custom-call(bf16[2,256,256]{2,1,0:T(8,128)(2,1)S(1)} %copy-done.3, bf16[2,256,256]{2,1,0:T(8,128)(2,1)S(1)} %copy-done.4, bf16[2,256,256]{2,1,0:T(8,128)(2,1)S(1)} %copy-done.5, ...), custom_call_target="tpu_custom_call" | custom-call | flops 536870912 | bytes 8388608 | tf_op jit(solution)/shard_map/prepare/pallas_call | solution.py:220
  12.3 0.0 copy-start.8
  12.3 0.0 copy-start.9
  12.3 7.4 %collective-permute-done.sec = bf16[2,1024,128]{2,1,0:T(8,128)(2,1)S(1)} collective-permute-done((bf16[2,1024,128]{2,1,0:T(8,128)(2,1)}, bf16[2,1024,128]{2,1,0:T(8,128)(2,1)S(1)}, u32[]{:S(2)}, u32[]{:S(2)}) %collective-permute-start) | collective-permute-done | bytes 524320 | tf_op jit(solution)/shard_map/ppermute | solution.py:306
  19.7 0.0 copy-done
  19.7 0.1 broadcast_select_fusion
  19.7 1.3 %collective-permute-start.2 = (bf16[2,1024,128]{2,1,0:T(8,128)(2,1)S(1)}, bf16[2,1024,128]{2,1,0:T(8,128)(2,1)S(1)}, u32[]{:S(2)}, u32[]{:S(2)}) collective-permute-start(bf16[2,1024,128]{2,1,0:T(8,128)(2,1)S(1)} %broadcast_select_fusion), channel_id=1, source_target_pairs={{0,1},{1,0},{2,3},{3,2},{4,5},{5,4},{6,7},{7,6},{8,9},{9,8},{10,11... | collective-permute-start | bytes 1572872 | tf_op jit(solution)/shard_map/ppermute | solution.py:306
  21.0 0.0 collective-permute-done.1.own_low
  21.0 0.0 collective-permute-done.3.sec_low
  21.1 0.1 collective-permute-start.4
  21.2 0.0 copy-done.8
  21.2 0.0 copy-done.9
  21.8 0.1 pad_add_fusion.info
  21.9 0.8 collective-permute-done.4.nxt_low
  22.8 0.0 collective-permute-done.2.nxt
  22.8 10.9 %slots.1 = (f32[2,1280,128]{2,1,0:T(8,128)S(1)}, bf16[2,1024,128]{2,1,0:T(8,128)(2,1)S(1)}, bf16[2,256,128]{2,1,0:T(8,128)(2,1)S(1)}, f32[2,1280,128]{2,1,0:T(8,...) custom-call(s32[18]{0:T(128)S(1)} %pad_add_fusion.info, ...), custom_call_target="tpu_custom_call" | custom-call | tf_op jit(solution)/shard_map/slots/pallas_call | solution.py:248
  33.7 0.4 collective-permute-start.5
  34.1 1.6 %collective-permute-done.5 = bf16[2,1024,128]{2,1,0:T(8,128)(2,1)S(1)} collective-permute-done((bf16[2,1024,128]{2,1,0:T(8,128)(2,1)S(1)}, bf16[2,1024,128]{2,1,0:T(8,128)(2,1)S(1)}, u32[]{:S(2)}, u32[]{:S(2)}) %collective-permute-start.5) | collective-permute-done | bytes 524320 | tf_op jit(solution)/shard_map/ppermute | solution.py:306
  35.7 0.0 copy-start.6
  35.7 0.3 collective-permute-start.6
  36.0 0.2 collective-permute-start.8
  36.2 0.8 collective-permute-done.6
  37.1 0.2 fusion.3
  37.2 0.0 copy-done.6
  37.2 1.3 %collective-permute-start.7 = (bf16[2,1280,128]{2,1,0:T(8,128)(2,1)S(1)}, bf16[2,1280,128]{2,1,0:T(8,128)(2,1)S(1)}, u32[]{:S(2)}, u32[]{:S(2)}) collective-permute-start(bf16[2,1280,128]{2,1,0:T(8,128)(2,1)S(1)} %fusion.3), channel_id=1, source_target_pairs={{0,2},{1,3},{2,4},{3,5},{4,6},{5,7},{6,8},{7,9},{8,10},{9,11},{10,... | collective-permute-start | bytes 1966088 | tf_op jit(solution)/shard_map/ppermute | solution.py:306
  38.6 0.0 collective-permute-done.8
  38.6 0.9 add_convert_fusion
  39.5 23.1 %all-to-all-start = ((bf16[64,32,128]{2,1,0:T(8,128)(2,1)}), bf16[64,32,128]{2,1,0:T(8,128)(2,1)S(1)}, u32[]{:S(2)}, u32[]{:S(2)}) async-start(bf16[64,32,128]{2,1,0:T(8,128)(2,1)} %bitcast.4), calls=%async_computation | async-start | bytes 1048576 | tf_op jit(solution)/shard_map/all_to_all | solution.py:356
  62.6 17.4 %all-to-all-done.parts = bf16[64,32,128]{2,1,0:T(8,128)(2,1)S(1)} async-done(((bf16[64,32,128]{2,1,0:T(8,128)(2,1)}), bf16[64,32,128]{2,1,0:T(8,128)(2,1)S(1)}, u32[]{:S(2)}, u32[]{:S(2)}) %all-to-all-start) | async-done | bytes 524320 | tf_op jit(solution)/shard_map/all_to_all | solution.py:356
  80.0 0.9 share.1
  80.9 8.1 %all-to-all-start.1 = ((bf16[64,32,128]{2,1,0:T(8,128)(2,1)}), bf16[64,32,128]{2,1,0:T(8,128)(2,1)S(1)}, u32[]{:S(2)}, u32[]{:S(2)}) async-start(bf16[64,32,128]{2,1,0:T(8,128)(2,1)} %share.1), calls=%async_computation.1 | async-start | bytes 1048576 | tf_op jit(solution)/shard_map/all_to_all | solution.py:357
  89.1 0.0 collective-permute-done.7
  89.1 0.0 copy-start.7
  89.1 0.8 copy-done.7
  89.9 1.5 %fusion.1 = f32[2,1280,128]{2,1,0:T(8,128)S(1)} fusion(f32[2,1280,128]{2,1,0:T(8,128)S(1)} %get-tuple-element.30, bf16[2,1280,128]{2,1,0:T(8,128)(2,1)} %copy-done.7, pred[]{:T(512)S(6)} %eq.16, bf16[2,256,128]{2,1,0:T(8,128)(2,1)S(1)} %collective-permute-done.6, bf16[2,1024,128]{2,1,0:T(8,128)(2,1)} %copy-done.6), kind=kLoop, calls=%fused_computation.3 | loop fusion | flops 2621440 | bytes 3932161 | tf_op jit(solution)/shard_map/add | solution.py:348
  91.4 2.9 %collective-permute-start.9 = (bf16[2,256,128]{2,1,0:T(8,128)(2,1)S(1)}, bf16[2,256,128]{2,1,0:T(8,128)(2,1)S(1)}, u32[]{:S(2)}, u32[]{:S(2)}) collective-permute-start(bf16[2,256,128]{2,1,0:T(8,128)(2,1)S(1)} %slice.17), channel_id=1, source_target_pairs={{0,32},{1,33},{2,34},{3,35},{4,36},{5,37},{6,38},{7,39},{8,40},{9,... | collective-permute-start | bytes 393224 | tf_op jit(solution)/shard_map/ppermute | solution.py:306
  94.3 3.6 %collective-permute-done.9 = bf16[2,256,128]{2,1,0:T(8,128)(2,1)S(1)} collective-permute-done((bf16[2,256,128]{2,1,0:T(8,128)(2,1)S(1)}, bf16[2,256,128]{2,1,0:T(8,128)(2,1)S(1)}, u32[]{:S(2)}, u32[]{:S(2)}) %collective-permute-start.9) | collective-permute-done | bytes 131104 | tf_op jit(solution)/shard_map/ppermute | solution.py:306
  97.9 2.8 %all-to-all-done.1 = bf16[64,32,128]{2,1,0:T(8,128)(2,1)S(1)} async-done(((bf16[64,32,128]{2,1,0:T(8,128)(2,1)}), bf16[64,32,128]{2,1,0:T(8,128)(2,1)S(1)}, u32[]{:S(2)}, u32[]{:S(2)}) %all-to-all-start.1) | async-done | bytes 524320 | tf_op jit(solution)/shard_map/all_to_all | solution.py:357
  100.7 2.6 %collective-permute-start.10 = (bf16[2048,128]{1,0:T(8,128)(2,1)S(1)}, bf16[2048,128]{1,0:T(8,128)(2,1)S(1)}, u32[]{:S(2)}, u32[]{:S(2)}) collective-permute-start(bf16[2048,128]{1,0:T(8,128)(2,1)S(1)} %bitcast.19), channel_id=1, source_target_pairs={{0,1},{1,0},{2,3},{3,2},{4,5},{5,4},{6,7},{7,6},{8,9},{9,8},{10,11... | collective-permute-start | bytes 1572872 | tf_op jit(solution)/shard_map/ppermute | solution.py:306
  103.3 1.0 slice_add_fusion
  104.3 0.5 collective-permute-done.10
  104.8 1.5 %select_convert_fusion = f32[2,4,256,256]{3,2,1,0:T(8,128)} fusion(pred[2]{0:T(512)(128)(4,1)S(1)} %iota_compare_fusion, bf16[4,256,256]{2,1,0:T(8,128)(2,1)S(1)} %bitcast.21, bf16[4,256,256]{2,1,0:T(8,128)(2,1)S(1)} %bitcast.20), kind=kLoop, calls=%fused_computation.7 | loop fusion | flops 1048576 | bytes 3145730 | tf_op jit(solution)/shard_map/convert_element_type | solution.py:361
  (4 shorter events, 0.0 us)
Async XLA Ops:
  0.6 19.0 %collective-permute-start = (bf16[2,1024,128]{2,1,0:T(8,128)(2,1)}, bf16[2,1024,128]{2,1,0:T(8,128)(2,1)S(1)}, u32[]{:S(2)}, u32[]{:S(2)}) collective-permute-start(bf16[2,1024,128]{2,1,0:T(8,128)(2,1)} %own.1), channel_id=1, source_target_pairs={{2,0},{3,1},{4,2},{5,3},{6,4},{7,5},{8,6},{9,7},{10,8},{11,9},{12,... | collective-permute-start | bytes 1572872 | tf_op jit(solution)/shard_map/ppermute | solution.py:306
  2.9 18.2 %collective-permute-start.1 = (bf16[2,256,128]{2,1,0:T(8,128)(2,1)S(1)}, bf16[2,256,128]{2,1,0:T(8,128)(2,1)S(1)}, u32[]{:S(2)}, u32[]{:S(2)}) collective-permute-start(bf16[2,256,128]{2,1,0:T(8,128)(2,1)S(1)} %slice.10), channel_id=1, source_target_pairs={{32,0},{33,1},{34,2},{35,3},{36,4},{37,5},{38,6},{39,7},{40,8},{41... | collective-permute-start | bytes 393224 | tf_op jit(solution)/shard_map/ppermute | solution.py:306
  4.2 16.9 %collective-permute-start.3 = (bf16[2,256,128]{2,1,0:T(8,128)(2,1)S(1)}, bf16[2,256,128]{2,1,0:T(8,128)(2,1)S(1)}, u32[]{:S(2)}, u32[]{:S(2)}) collective-permute-start(bf16[2,256,128]{2,1,0:T(8,128)(2,1)S(1)} %slice.10), channel_id=1, source_target_pairs={{34,0},{35,1},{36,2},{37,3},{38,4},{39,5},{40,6},{41,7},{42,8},{43... | collective-permute-start | bytes 393224 | tf_op jit(solution)/shard_map/ppermute | solution.py:306
  5.5 1.6 %copy-start.1 = (f32[2,4,256,256]{3,2,1,0:T(8,128)S(1)}, f32[2,4,256,256]{3,2,1,0:T(8,128)}, u32[]{:S(2)}) copy-start(f32[2,4,256,256]{3,2,1,0:T(8,128)} %probe.1) | copy-start | bytes 6291460
  7.1 1.2 %copy-start.2 = (bf16[1,8,256,256]{3,2,1,0:T(8,128)(2,1)S(1)}, bf16[1,8,256,256]{3,2,1,0:T(8,128)(2,1)}, u32[]{:S(2)}) copy-start(bf16[1,8,256,256]{3,2,1,0:T(8,128)(2,1)} %meas.1) | copy-start | bytes 3145732
  8.3 0.9 copy-start.3
  9.2 0.9 copy-start.4
  10.2 0.9 copy-start.5
  11.1 8.5 %copy-start = (bf16[2,1024,128]{2,1,0:T(8,128)(2,1)S(1)}, bf16[2,1024,128]{2,1,0:T(8,128)(2,1)}, u32[]{:S(2)}) copy-start(bf16[2,1024,128]{2,1,0:T(8,128)(2,1)} %own.1) | copy-start | bytes 1572868
  12.3 8.9 %copy-start.8 = (s32[1,8]{1,0:T(1,128)S(1)}, s32[1,8]{1,0:T(1,128)}, u32[]{:S(2)}) copy-start(s32[1,8]{1,0:T(1,128)} %param.13) | copy-start | bytes 100
  12.3 8.9 %copy-start.9 = (s32[1,8]{1,0:T(1,128)S(1)}, s32[1,8]{1,0:T(1,128)}, u32[]{:S(2)}) copy-start(s32[1,8]{1,0:T(1,128)} %param.12) | copy-start | bytes 100
  19.7 3.1 %collective-permute-start.2 = (bf16[2,1024,128]{2,1,0:T(8,128)(2,1)S(1)}, bf16[2,1024,128]{2,1,0:T(8,128)(2,1)S(1)}, u32[]{:S(2)}, u32[]{:S(2)}) collective-permute-start(bf16[2,1024,128]{2,1,0:T(8,128)(2,1)S(1)} %broadcast_select_fusion), channel_id=1, source_target_pairs={{0,1},{1,0},{2,3},{3,2},{4,5},{5,4},{6,7},{7,6},{8,9},{9,8},{10,11... | collective-permute-start | bytes 1572872 | tf_op jit(solution)/shard_map/ppermute | solution.py:306
  21.1 1.7 %collective-permute-start.4 = (bf16[2,256,128]{2,1,0:T(8,128)(2,1)S(1)}, bf16[2,256,128]{2,1,0:T(8,128)(2,1)S(1)}, u32[]{:S(2)}, u32[]{:S(2)}) collective-permute-start(bf16[2,256,128]{2,1,0:T(8,128)(2,1)S(1)} %broadcast_select_fusion.1), channel_id=1, source_target_pairs={{0,1},{1,0},{2,3},{3,2},{4,5},{5,4},{6,7},{7,6},{8,9},{9,8},{10,11... | collective-permute-start | bytes 393224 | tf_op jit(solution)/shard_map/ppermute | solution.py:306
  33.7 2.0 %collective-permute-start.5 = (bf16[2,1024,128]{2,1,0:T(8,128)(2,1)S(1)}, bf16[2,1024,128]{2,1,0:T(8,128)(2,1)S(1)}, u32[]{:S(2)}, u32[]{:S(2)}) collective-permute-start(bf16[2,1024,128]{2,1,0:T(8,128)(2,1)S(1)} %get-tuple-element.31), channel_id=1, source_target_pairs={{0,1},{1,0},{2,3},{3,2},{4,5},{5,4},{6,7},{7,6},{8,9},{9,8},{10,11... | collective-permute-start | bytes 1572872 | tf_op jit(solution)/shard_map/ppermute | solution.py:306
  35.7 1.5 %copy-start.6 = (bf16[2,1024,128]{2,1,0:T(8,128)(2,1)}, bf16[2,1024,128]{2,1,0:T(8,128)(2,1)S(1)}, u32[]{:S(2)}) copy-start(bf16[2,1024,128]{2,1,0:T(8,128)(2,1)S(1)} %collective-permute-done.5) | copy-start | bytes 1572868
  35.7 1.3 %collective-permute-start.6 = (bf16[2,256,128]{2,1,0:T(8,128)(2,1)S(1)}, bf16[2,256,128]{2,1,0:T(8,128)(2,1)S(1)}, u32[]{:S(2)}, u32[]{:S(2)}) collective-permute-start(bf16[2,256,128]{2,1,0:T(8,128)(2,1)S(1)} %get-tuple-element.34), channel_id=1, source_target_pairs={{0,1},{1,0},{2,3},{3,2},{4,5},{5,4},{6,7},{7,6},{8,9},{9,8},{10,11... | collective-permute-start | bytes 393224 | tf_op jit(solution)/shard_map/ppermute | solution.py:306
  36.0 2.6 %collective-permute-start.8 = (bf16[2048,128]{1,0:T(8,128)(2,1)S(1)}, bf16[2048,128]{1,0:T(8,128)(2,1)S(1)}, u32[]{:S(2)}, u32[]{:S(2)}) collective-permute-start(bf16[2048,128]{1,0:T(8,128)(2,1)S(1)} %get-tuple-element.37), channel_id=1, source_target_pairs={{0,1},{1,0},{2,3},{3,2},{4,5},{5,4},{6,7},{7,6},{8,9},{9,8},{10,11... | collective-permute-start | bytes 1572872 | tf_op jit(solution)/shard_map/ppermute | solution.py:306
  37.2 51.8 %collective-permute-start.7 = (bf16[2,1280,128]{2,1,0:T(8,128)(2,1)S(1)}, bf16[2,1280,128]{2,1,0:T(8,128)(2,1)S(1)}, u32[]{:S(2)}, u32[]{:S(2)}) collective-permute-start(bf16[2,1280,128]{2,1,0:T(8,128)(2,1)S(1)} %fusion.3), channel_id=1, source_target_pairs={{0,2},{1,3},{2,4},{3,5},{4,6},{5,7},{6,8},{7,9},{8,10},{9,11},{10,... | collective-permute-start | bytes 1966088 | tf_op jit(solution)/shard_map/ppermute | solution.py:306
  39.5 40.5 %all-to-all-start = ((bf16[64,32,128]{2,1,0:T(8,128)(2,1)}), bf16[64,32,128]{2,1,0:T(8,128)(2,1)S(1)}, u32[]{:S(2)}, u32[]{:S(2)}) async-start(bf16[64,32,128]{2,1,0:T(8,128)(2,1)} %bitcast.4), calls=%async_computation | async-start | bytes 1048576 | tf_op jit(solution)/shard_map/all_to_all | solution.py:356
  80.9 19.8 %all-to-all-start.1 = ((bf16[64,32,128]{2,1,0:T(8,128)(2,1)}), bf16[64,32,128]{2,1,0:T(8,128)(2,1)S(1)}, u32[]{:S(2)}, u32[]{:S(2)}) async-start(bf16[64,32,128]{2,1,0:T(8,128)(2,1)} %share.1), calls=%async_computation.1 | async-start | bytes 1048576 | tf_op jit(solution)/shard_map/all_to_all | solution.py:357
  89.1 0.8 copy-start.7
  91.4 6.5 %collective-permute-start.9 = (bf16[2,256,128]{2,1,0:T(8,128)(2,1)S(1)}, bf16[2,256,128]{2,1,0:T(8,128)(2,1)S(1)}, u32[]{:S(2)}, u32[]{:S(2)}) collective-permute-start(bf16[2,256,128]{2,1,0:T(8,128)(2,1)S(1)} %slice.17), channel_id=1, source_target_pairs={{0,32},{1,33},{2,34},{3,35},{4,36},{5,37},{6,38},{7,39},{8,40},{9,... | collective-permute-start | bytes 393224 | tf_op jit(solution)/shard_map/ppermute | solution.py:306
  100.7 4.1 %collective-permute-start.10 = (bf16[2048,128]{1,0:T(8,128)(2,1)S(1)}, bf16[2048,128]{1,0:T(8,128)(2,1)S(1)}, u32[]{:S(2)}, u32[]{:S(2)}) collective-permute-start(bf16[2048,128]{1,0:T(8,128)(2,1)S(1)} %bitcast.19), channel_id=1, source_target_pairs={{0,1},{1,0},{2,3},{3,2},{4,5},{5,4},{6,7},{7,6},{8,9},{9,8},{10,11... | collective-permute-start | bytes 1572872 | tf_op jit(solution)/shard_map/ppermute | solution.py:306

commit v4 on v0

--- a/solution.py
+++ b/solution.py
@@ -270,7 +270,7 @@
             pltpu.VMEM((2, modes, 2, win, win), BF16),
             pltpu.VMEM((2,) + blocks, BF16),
         ],
-        compiler_params=pltpu.CompilerParams(vmem_limit_bytes=32 * 1024 * 1024),
+        compiler_params=pltpu.CompilerParams(vmem_limit_bytes=22 * 1024 * 1024),
         name="slots",
     )(info, fwd, bwd, probe, measured, own, own_low, nxt, nxt_low, sec, sec_low)
 

time: 96 us -> 96.6 us (level); the launches traced: 96.4 us -> 95.3 us
  starting transfers between devices: 42.1 us -> 41 us
    all_to_all x1, starting transfers between devices: 21.2 us -> 15.3 us  [local(): share = exchange(chip_sum.reshape(devices // 2, -1, LANES))]
    ppermute x11, starting transfers between devices: 15.4 us -> 20.2 us  [moved(): return lax.ppermute(value, ('rows', 'cols'), pairs)]
where the time goes in v4:
time: 96.6 us; the launch traced here: 95.3 us
  starting transfers between devices  41 us (42%)
  waiting for transfers between devices  24.3 us (25%)
  Pallas kernels  12.1 us (13%)
  local copies, waits for them, and re-layouts  8.31 us (9%)
  other arithmetic  8.13 us (8%)
  between operations  1.44 us (1%)
    ppermute x11, starting transfers between devices, moved(): return lax.ppermute(value, ('rows', 'cols'), pairs)  20.2 us
    all_to_all x1, starting transfers between devices, local(): share = exchange(chip_sum.reshape(devices // 2, -1, LANES))  15.3 us
    ppermute x11, waiting for transfers between devices, moved(): return lax.ppermute(value, ('rows', 'cols'), pairs)  13.8 us
    pallas_call x1, Pallas kernels, run_slots(): pl.pallas_call(slots_kernel, in_specs=[pl.BlockSpec(memory_space=pltpu.SM...  11 us
    all_to_all x1, waiting for transfers between devices, local(): share = exchange(chip_sum.reshape(devices // 2, -1, LANES))  8.18 us
    unnamed x18, local copies, waits for them, and re-layouts  6.51 us
    all_to_all x1, starting transfers between devices, local(): exchange(jnp.broadcast_to(share[None], (devices // 2,) + share.shape))  5.49 us
    convert_element_type x1, other arithmetic, local(): jnp.where(part == core, mine[None], swap_cores(mine)[None]).astype(F32)  2.57 us
  transfers between devices with their start and end apart: 13, of which 8 were waited for; matrix products, arithmetic and copies ran while one was open for 8% of the time, Pallas kernels for 1%

profile of v4, /device:TPU:1, one launch (start us, length us, event | category | flops | bytes accessed | tf_op | source)
XLA Modules:
  0.0 95.3 jit_solution(5921011936905177415)
XLA Ops:
  0.6 1.3 %collective-permute-start = (bf16[2,1024,128]{2,1,0:T(8,128)(2,1)}, bf16[2,1024,128]{2,1,0:T(8,128)(2,1)S(1)}, u32[]{:S(2)}, u32[]{:S(2)}) collective-permute-start(bf16[2,1024,128]{2,1,0:T(8,128)(2,1)} %own.1), channel_id=1, source_target_pairs={{2,0},{3,1},{4,2},{5,3},{6,4},{7,5},{8,6},{9,7},{10,8},{11,9},{12,... | collective-permute-start | bytes 1572872 | tf_op jit(solution)/shard_map/ppermute | solution.py:287
  1.9 0.9 slice.10
  2.9 1.3 %collective-permute-start.1 = (bf16[2,256,128]{2,1,0:T(8,128)(2,1)S(1)}, bf16[2,256,128]{2,1,0:T(8,128)(2,1)S(1)}, u32[]{:S(2)}, u32[]{:S(2)}) collective-permute-start(bf16[2,256,128]{2,1,0:T(8,128)(2,1)S(1)} %slice.10), channel_id=1, source_target_pairs={{32,0},{33,1},{34,2},{35,3},{36,4},{37,5},{38,6},{39,7},{40,8},{41... | collective-permute-start | bytes 393224 | tf_op jit(solution)/shard_map/ppermute | solution.py:287
  4.2 1.3 %collective-permute-start.3 = (bf16[2,256,128]{2,1,0:T(8,128)(2,1)S(1)}, bf16[2,256,128]{2,1,0:T(8,128)(2,1)S(1)}, u32[]{:S(2)}, u32[]{:S(2)}) collective-permute-start(bf16[2,256,128]{2,1,0:T(8,128)(2,1)S(1)} %slice.10), channel_id=1, source_target_pairs={{34,0},{35,1},{36,2},{37,3},{38,4},{39,5},{40,6},{41,7},{42,8},{43... | collective-permute-start | bytes 393224 | tf_op jit(solution)/shard_map/ppermute | solution.py:287
  5.5 0.0 copy-start.1
  5.5 1.6 %copy-done.1 = f32[2,4,256,256]{3,2,1,0:T(8,128)S(1)} copy-done((f32[2,4,256,256]{3,2,1,0:T(8,128)S(1)}, f32[2,4,256,256]{3,2,1,0:T(8,128)}, u32[]{:S(2)}) %copy-start.1) | copy-done | bytes 2097176
  7.1 0.0 copy-start.2
  7.1 1.2 %copy-done.2 = bf16[1,8,256,256]{3,2,1,0:T(8,128)(2,1)S(1)} copy-done((bf16[1,8,256,256]{3,2,1,0:T(8,128)(2,1)S(1)}, bf16[1,8,256,256]{3,2,1,0:T(8,128)(2,1)}, u32[]{:S(2)}) %copy-start.2) | copy-done | bytes 1048600
  8.3 0.0 copy-start.3
  8.3 0.9 copy-done.3
  9.2 0.0 copy-start.4
  9.2 0.9 copy-done.4
  10.2 0.0 copy-start.5
  10.2 0.9 copy-done.5
  11.1 0.0 copy-start
  11.1 1.1 %prepare.1 = (bf16[2,256,256]{2,1,0:T(8,128)(2,1)S(1)}, bf16[2,256,256]{2,1,0:T(8,128)(2,1)S(1)}, f32[2,4,256,256]{3,2,1,0:T(8,128)S(1)}, bf16[8,256,256]{2,1,0:T(8,128)(2,1)S(1)}) custom-call(bf16[2,256,256]{2,1,0:T(8,128)(2,1)S(1)} %copy-done.3, bf16[2,256,256]{2,1,0:T(8,128)(2,1)S(1)} %copy-done.4, bf16[2,256,256]{2,1,0:T(8,128)(2,1)S(1)} %copy-done.5, ...), custom_call_target="tpu_custom_call" | custom-call | flops 536870912 | bytes 8388608 | tf_op jit(solution)/shard_map/prepare/pallas_call | solution.py:223
  12.3 0.0 copy-start.7
  12.3 0.0 copy-start.8
  12.3 7.4 %collective-permute-done.sec = bf16[2,1024,128]{2,1,0:T(8,128)(2,1)S(1)} collective-permute-done((bf16[2,1024,128]{2,1,0:T(8,128)(2,1)}, bf16[2,1024,128]{2,1,0:T(8,128)(2,1)S(1)}, u32[]{:S(2)}, u32[]{:S(2)}) %collective-permute-start) | collective-permute-done | bytes 524320 | tf_op jit(solution)/shard_map/ppermute | solution.py:287
  19.7 0.0 copy-done
  19.7 0.1 broadcast_select_fusion
  19.7 1.3 %collective-permute-start.2 = (bf16[2,1024,128]{2,1,0:T(8,128)(2,1)S(1)}, bf16[2,1024,128]{2,1,0:T(8,128)(2,1)S(1)}, u32[]{:S(2)}, u32[]{:S(2)}) collective-permute-start(bf16[2,1024,128]{2,1,0:T(8,128)(2,1)S(1)} %broadcast_select_fusion), channel_id=1, source_target_pairs={{0,1},{1,0},{2,3},{3,2},{4,5},{5,4},{6,7},{7,6},{8,9},{9,8},{10,11... | collective-permute-start | bytes 1572872 | tf_op jit(solution)/shard_map/ppermute | solution.py:287
  21.0 0.0 collective-permute-done.1.own_low
  21.0 0.0 collective-permute-done.3.sec_low
  21.1 0.1 collective-permute-start.4
  21.2 0.0 copy-done.7
  21.2 0.0 copy-done.8
  21.8 0.1 pad_add_fusion.info
  21.9 0.8 collective-permute-done.4.nxt_low
  22.8 0.0 collective-permute-done.2.nxt
  22.8 11.0 %slots.1 = (f32[2,1280,128]{2,1,0:T(8,128)S(1)}, bf16[2,1024,128]{2,1,0:T(8,128)(2,1)S(1)}, bf16[2,256,128]{2,1,0:T(8,128)(2,1)S(1)}, f32[2,1280,128]{2,1,0:T(8,...) custom-call(s32[18]{0:T(128)S(1)} %pad_add_fusion.info, ...), custom_call_target="tpu_custom_call" | custom-call | tf_op jit(solution)/shard_map/slots/pallas_call | solution.py:251
  33.8 5.4 %collective-permute-start.5 = (bf16[2048,128]{1,0:T(8,128)(2,1)S(1)}, bf16[2048,128]{1,0:T(8,128)(2,1)S(1)}, u32[]{:S(2)}, u32[]{:S(2)}) collective-permute-start(bf16[2048,128]{1,0:T(8,128)(2,1)S(1)} %get-tuple-element.33), channel_id=1, source_target_pairs={{0,1},{1,0},{2,3},{3,2},{4,5},{5,4},{6,7},{7,6},{8,9},{9,8},{10,11... | collective-permute-start | bytes 1572872 | tf_op jit(solution)/shard_map/ppermute | solution.py:287
  39.2 0.1 collective-permute-start.6
  39.3 1.4 %collective-permute-done.5 = bf16[2048,128]{1,0:T(8,128)(2,1)S(1)} collective-permute-done((bf16[2048,128]{1,0:T(8,128)(2,1)S(1)}, bf16[2048,128]{1,0:T(8,128)(2,1)S(1)}, u32[]{:S(2)}, u32[]{:S(2)}) %collective-permute-start.5) | collective-permute-done | bytes 524320 | tf_op jit(solution)/shard_map/ppermute | solution.py:287
  40.7 0.9 add_convert_fusion
  41.6 0.0 collective-permute-done.6
  41.6 0.4 collective-permute-start.7
  42.0 15.3 %all-to-all-start = ((bf16[64,32,128]{2,1,0:T(8,128)(2,1)}), bf16[64,32,128]{2,1,0:T(8,128)(2,1)}, u32[]{:S(2)}, u32[]{:S(2)}) async-start(bf16[64,32,128]{2,1,0:T(8,128)(2,1)} %bitcast.19), calls=%async_computation | async-start | bytes 1048576 | tf_op jit(solution)/shard_map/all_to_all | solution.py:337
  57.2 0.0 collective-permute-done.7
  57.2 1.0 %fusion.3 = bf16[2,1280,128]{2,1,0:T(8,128)(2,1)} fusion(f32[2,1280,128]{2,1,0:T(8,128)S(1)} %get-tuple-element.38, pred[]{:T(512)S(6)} %eq.15, bf16[2,256,128]{2,1,0:T(8,128)(2,1)S(1)} %collective-permute-done.7, bf16[2,1024,128]{2,1,0:T(8,128)(2,1)S(1)} %collective-permute-done.6), kind=kLoop, calls=%fused_computation.5 | loop fusion | flops 2293760 | bytes 2621441 | tf_op jit(solution)/shard_map/convert_element_type | solution.py:327
  58.3 2.9 %collective-permute-start.8 = (bf16[2,1280,128]{2,1,0:T(8,128)(2,1)}, bf16[2,1280,128]{2,1,0:T(8,128)(2,1)S(1)}, u32[]{:S(2)}, u32[]{:S(2)}) collective-permute-start(bf16[2,1280,128]{2,1,0:T(8,128)(2,1)} %fusion.3), channel_id=1, source_target_pairs={{0,2},{1,3},{2,4},{3,5},{4,6},{5,7},{6,8},{7,9},{8,10},{9,11},{10,... | collective-permute-start | bytes 1966088 | tf_op jit(solution)/shard_map/ppermute | solution.py:287
  61.1 8.2 %all-to-all-done = bf16[64,32,128]{2,1,0:T(8,128)(2,1)} async-done(((bf16[64,32,128]{2,1,0:T(8,128)(2,1)}), bf16[64,32,128]{2,1,0:T(8,128)(2,1)}, u32[]{:S(2)}, u32[]{:S(2)}) %all-to-all-start) | async-done | bytes 524320 | tf_op jit(solution)/shard_map/all_to_all | solution.py:337
  69.3 1.1 %convert_reduce_fusion = f32[32,128]{1,0:T(8,128)S(1)} fusion(bf16[64,32,128]{2,1,0:T(8,128)(2,1)} %all-to-all-done), kind=kLoop, calls=%fused_computation.8 | loop fusion | flops 520192 | bytes 540672 | tf_op jit(solution)/shard_map/reduce_sum | solution.py:339
  70.5 0.9 broadcast_in_dim.43
  71.3 5.5 %all-to-all-start.1 = ((bf16[64,32,128]{2,1,0:T(8,128)(2,1)}), bf16[64,32,128]{2,1,0:T(8,128)(2,1)}, u32[]{:S(2)}, u32[]{:S(2)}) async-start(bf16[64,32,128]{2,1,0:T(8,128)(2,1)} %broadcast_in_dim.43), calls=%async_computation.1 | async-start | bytes 1048576 | tf_op jit(solution)/shard_map/all_to_all | solution.py:340
  76.8 1.2 %collective-permute-done.8 = bf16[2,1280,128]{2,1,0:T(8,128)(2,1)S(1)} collective-permute-done((bf16[2,1280,128]{2,1,0:T(8,128)(2,1)}, bf16[2,1280,128]{2,1,0:T(8,128)(2,1)S(1)}, u32[]{:S(2)}, u32[]{:S(2)}) %collective-permute-start.8) | collective-permute-done | bytes 655392 | tf_op jit(solution)/shard_map/ppermute | solution.py:287
  78.0 0.0 copy-start.6
  78.0 0.8 copy-done.6
  78.8 1.3 %fusion.1 = f32[2,1280,128]{2,1,0:T(8,128)S(1)} fusion(f32[2,1280,128]{2,1,0:T(8,128)S(1)} %get-tuple-element.31, bf16[2,1280,128]{2,1,0:T(8,128)(2,1)} %copy-done.6, pred[]{:T(512)S(6)} %eq.16, bf16[2,256,128]{2,1,0:T(8,128)(2,1)S(1)} %collective-permute-done.7, bf16[2,1024,128]{2,1,0:T(8,128)(2,1)S(1)} %collective-permute-done.6), kind=kLoop, calls=%fused_computation.3 | loop fusion | flops 2621440 | bytes 3932161 | tf_op jit(solution)/shard_map/add | solution.py:329
  80.2 2.8 %collective-permute-start.9 = (bf16[2,256,128]{2,1,0:T(8,128)(2,1)S(1)}, bf16[2,256,128]{2,1,0:T(8,128)(2,1)S(1)}, u32[]{:S(2)}, u32[]{:S(2)}) collective-permute-start(bf16[2,256,128]{2,1,0:T(8,128)(2,1)S(1)} %slice.17), channel_id=1, source_target_pairs={{0,32},{1,33},{2,34},{3,35},{4,36},{5,37},{6,38},{7,39},{8,40},{9,... | collective-permute-start | bytes 393224 | tf_op jit(solution)/shard_map/ppermute | solution.py:287
  83.0 2.2 %collective-permute-done.9 = bf16[2,256,128]{2,1,0:T(8,128)(2,1)S(1)} collective-permute-done((bf16[2,256,128]{2,1,0:T(8,128)(2,1)S(1)}, bf16[2,256,128]{2,1,0:T(8,128)(2,1)S(1)}, u32[]{:S(2)}, u32[]{:S(2)}) %collective-permute-start.9) | collective-permute-done | bytes 131104 | tf_op jit(solution)/shard_map/ppermute | solution.py:287
  85.2 2.3 %all-to-all-done.1 = bf16[64,32,128]{2,1,0:T(8,128)(2,1)} async-done(((bf16[64,32,128]{2,1,0:T(8,128)(2,1)}), bf16[64,32,128]{2,1,0:T(8,128)(2,1)}, u32[]{:S(2)}, u32[]{:S(2)}) %all-to-all-start.1) | async-done | bytes 524320 | tf_op jit(solution)/shard_map/all_to_all | solution.py:340
  87.6 3.4 %collective-permute-start.10 = (bf16[2048,128]{1,0:T(8,128)(2,1)}, bf16[2048,128]{1,0:T(8,128)(2,1)S(1)}, u32[]{:S(2)}, u32[]{:S(2)}) collective-permute-start(bf16[2048,128]{1,0:T(8,128)(2,1)} %bitcast.8), channel_id=1, source_target_pairs={{0,1},{1,0},{2,3},{3,2},{4,5},{5,4},{6,7},{7,6},{8,9},{9,8},{10,11... | collective-permute-start | bytes 1572872 | tf_op jit(solution)/shard_map/ppermute | solution.py:287
  91.0 1.0 %slice_add_fusion = f32[2,1024,128]{2,1,0:T(8,128)} fusion(f32[2,1280,128]{2,1,0:T(8,128)S(1)} %fusion.1, bf16[2,256,128]{2,1,0:T(8,128)(2,1)S(1)} %collective-permute-done.9), kind=kLoop, calls=%fused_computation.6 | loop fusion | flops 524288 | bytes 2228224 | tf_op jit(solution)/shard_map/add | solution.py:348
  92.0 0.7 collective-permute-done.10
  92.7 2.6 %select_convert_fusion = f32[2,4,256,256]{3,2,1,0:T(8,128)} fusion(pred[2]{0:T(512)(128)(4,1)S(1)} %iota_compare_fusion, bf16[4,256,256]{2,1,0:T(8,128)(2,1)S(1)} %bitcast.20, bf16[4,256,256]{2,1,0:T(8,128)(2,1)} %bitcast.7), kind=kLoop, calls=%fused_computation.7 | loop fusion | flops 1048576 | bytes 3145730 | tf_op jit(solution)/shard_map/convert_element_type | solution.py:344
  (5 shorter events, 0.1 us)
Async XLA Ops:
  0.6 19.0 %collective-permute-start = (bf16[2,1024,128]{2,1,0:T(8,128)(2,1)}, bf16[2,1024,128]{2,1,0:T(8,128)(2,1)S(1)}, u32[]{:S(2)}, u32[]{:S(2)}) collective-permute-start(bf16[2,1024,128]{2,1,0:T(8,128)(2,1)} %own.1), channel_id=1, source_target_pairs={{2,0},{3,1},{4,2},{5,3},{6,4},{7,5},{8,6},{9,7},{10,8},{11,9},{12,... | collective-permute-start | bytes 1572872 | tf_op jit(solution)/shard_map/ppermute | solution.py:287
  2.9 18.2 %collective-permute-start.1 = (bf16[2,256,128]{2,1,0:T(8,128)(2,1)S(1)}, bf16[2,256,128]{2,1,0:T(8,128)(2,1)S(1)}, u32[]{:S(2)}, u32[]{:S(2)}) collective-permute-start(bf16[2,256,128]{2,1,0:T(8,128)(2,1)S(1)} %slice.10), channel_id=1, source_target_pairs={{32,0},{33,1},{34,2},{35,3},{36,4},{37,5},{38,6},{39,7},{40,8},{41... | collective-permute-start | bytes 393224 | tf_op jit(solution)/shard_map/ppermute | solution.py:287
  4.2 16.9 %collective-permute-start.3 = (bf16[2,256,128]{2,1,0:T(8,128)(2,1)S(1)}, bf16[2,256,128]{2,1,0:T(8,128)(2,1)S(1)}, u32[]{:S(2)}, u32[]{:S(2)}) collective-permute-start(bf16[2,256,128]{2,1,0:T(8,128)(2,1)S(1)} %slice.10), channel_id=1, source_target_pairs={{34,0},{35,1},{36,2},{37,3},{38,4},{39,5},{40,6},{41,7},{42,8},{43... | collective-permute-start | bytes 393224 | tf_op jit(solution)/shard_map/ppermute | solution.py:287
  5.5 1.6 %copy-start.1 = (f32[2,4,256,256]{3,2,1,0:T(8,128)S(1)}, f32[2,4,256,256]{3,2,1,0:T(8,128)}, u32[]{:S(2)}) copy-start(f32[2,4,256,256]{3,2,1,0:T(8,128)} %probe.1) | copy-start | bytes 6291460
  7.1 1.2 %copy-start.2 = (bf16[1,8,256,256]{3,2,1,0:T(8,128)(2,1)S(1)}, bf16[1,8,256,256]{3,2,1,0:T(8,128)(2,1)}, u32[]{:S(2)}) copy-start(bf16[1,8,256,256]{3,2,1,0:T(8,128)(2,1)} %meas.1) | copy-start | bytes 3145732
  8.3 0.9 copy-start.3
  9.2 0.9 copy-start.4
  10.2 0.9 copy-start.5
  11.1 8.5 %copy-start = (bf16[2,1024,128]{2,1,0:T(8,128)(2,1)S(1)}, bf16[2,1024,128]{2,1,0:T(8,128)(2,1)}, u32[]{:S(2)}) copy-start(bf16[2,1024,128]{2,1,0:T(8,128)(2,1)} %own.1) | copy-start | bytes 1572868
  12.3 8.9 %copy-start.7 = (s32[1,8]{1,0:T(1,128)S(1)}, s32[1,8]{1,0:T(1,128)}, u32[]{:S(2)}) copy-start(s32[1,8]{1,0:T(1,128)} %param.13) | copy-start | bytes 100
  12.3 8.9 %copy-start.8 = (s32[1,8]{1,0:T(1,128)S(1)}, s32[1,8]{1,0:T(1,128)}, u32[]{:S(2)}) copy-start(s32[1,8]{1,0:T(1,128)} %param.12) | copy-start | bytes 100
  19.7 3.1 %collective-permute-start.2 = (bf16[2,1024,128]{2,1,0:T(8,128)(2,1)S(1)}, bf16[2,1024,128]{2,1,0:T(8,128)(2,1)S(1)}, u32[]{:S(2)}, u32[]{:S(2)}) collective-permute-start(bf16[2,1024,128]{2,1,0:T(8,128)(2,1)S(1)} %broadcast_select_fusion), channel_id=1, source_target_pairs={{0,1},{1,0},{2,3},{3,2},{4,5},{5,4},{6,7},{7,6},{8,9},{9,8},{10,11... | collective-permute-start | bytes 1572872 | tf_op jit(solution)/shard_map/ppermute | solution.py:287
  21.1 1.7 %collective-permute-start.4 = (bf16[2,256,128]{2,1,0:T(8,128)(2,1)S(1)}, bf16[2,256,128]{2,1,0:T(8,128)(2,1)S(1)}, u32[]{:S(2)}, u32[]{:S(2)}) collective-permute-start(bf16[2,256,128]{2,1,0:T(8,128)(2,1)S(1)} %broadcast_select_fusion.1), channel_id=1, source_target_pairs={{0,1},{1,0},{2,3},{3,2},{4,5},{5,4},{6,7},{7,6},{8,9},{9,8},{10,11... | collective-permute-start | bytes 393224 | tf_op jit(solution)/shard_map/ppermute | solution.py:287
  33.8 6.9 %collective-permute-start.5 = (bf16[2048,128]{1,0:T(8,128)(2,1)S(1)}, bf16[2048,128]{1,0:T(8,128)(2,1)S(1)}, u32[]{:S(2)}, u32[]{:S(2)}) collective-permute-start(bf16[2048,128]{1,0:T(8,128)(2,1)S(1)} %get-tuple-element.33), channel_id=1, source_target_pairs={{0,1},{1,0},{2,3},{3,2},{4,5},{5,4},{6,7},{7,6},{8,9},{9,8},{10,11... | collective-permute-start | bytes 1572872 | tf_op jit(solution)/shard_map/ppermute | solution.py:287
  39.2 2.4 %collective-permute-start.6 = (bf16[2,1024,128]{2,1,0:T(8,128)(2,1)S(1)}, bf16[2,1024,128]{2,1,0:T(8,128)(2,1)S(1)}, u32[]{:S(2)}, u32[]{:S(2)}) collective-permute-start(bf16[2,1024,128]{2,1,0:T(8,128)(2,1)S(1)} %get-tuple-element.34), channel_id=1, source_target_pairs={{0,1},{1,0},{2,3},{3,2},{4,5},{5,4},{6,7},{7,6},{8,9},{9,8},{10,11... | collective-permute-start | bytes 1572872 | tf_op jit(solution)/shard_map/ppermute | solution.py:287
  41.6 15.6 %collective-permute-start.7 = (bf16[2,256,128]{2,1,0:T(8,128)(2,1)S(1)}, bf16[2,256,128]{2,1,0:T(8,128)(2,1)S(1)}, u32[]{:S(2)}, u32[]{:S(2)}) collective-permute-start(bf16[2,256,128]{2,1,0:T(8,128)(2,1)S(1)} %get-tuple-element.37), channel_id=1, source_target_pairs={{0,1},{1,0},{2,3},{3,2},{4,5},{5,4},{6,7},{7,6},{8,9},{9,8},{10,11... | collective-permute-start | bytes 393224 | tf_op jit(solution)/shard_map/ppermute | solution.py:287
  42.0 27.3 %all-to-all-start = ((bf16[64,32,128]{2,1,0:T(8,128)(2,1)}), bf16[64,32,128]{2,1,0:T(8,128)(2,1)}, u32[]{:S(2)}, u32[]{:S(2)}) async-start(bf16[64,32,128]{2,1,0:T(8,128)(2,1)} %bitcast.19), calls=%async_computation | async-start | bytes 1048576 | tf_op jit(solution)/shard_map/all_to_all | solution.py:337
  58.3 19.7 %collective-permute-start.8 = (bf16[2,1280,128]{2,1,0:T(8,128)(2,1)}, bf16[2,1280,128]{2,1,0:T(8,128)(2,1)S(1)}, u32[]{:S(2)}, u32[]{:S(2)}) collective-permute-start(bf16[2,1280,128]{2,1,0:T(8,128)(2,1)} %fusion.3), channel_id=1, source_target_pairs={{0,2},{1,3},{2,4},{3,5},{4,6},{5,7},{6,8},{7,9},{8,10},{9,11},{10,... | collective-permute-start | bytes 1966088 | tf_op jit(solution)/shard_map/ppermute | solution.py:287
  71.3 16.3 %all-to-all-start.1 = ((bf16[64,32,128]{2,1,0:T(8,128)(2,1)}), bf16[64,32,128]{2,1,0:T(8,128)(2,1)}, u32[]{:S(2)}, u32[]{:S(2)}) async-start(bf16[64,32,128]{2,1,0:T(8,128)(2,1)} %broadcast_in_dim.43), calls=%async_computation.1 | async-start | bytes 1048576 | tf_op jit(solution)/shard_map/all_to_all | solution.py:340
  78.0 0.8 copy-start.6
  80.2 5.1 %collective-permute-start.9 = (bf16[2,256,128]{2,1,0:T(8,128)(2,1)S(1)}, bf16[2,256,128]{2,1,0:T(8,128)(2,1)S(1)}, u32[]{:S(2)}, u32[]{:S(2)}) collective-permute-start(bf16[2,256,128]{2,1,0:T(8,128)(2,1)S(1)} %slice.17), channel_id=1, source_target_pairs={{0,32},{1,33},{2,34},{3,35},{4,36},{5,37},{6,38},{7,39},{8,40},{9,... | collective-permute-start | bytes 393224 | tf_op jit(solution)/shard_map/ppermute | solution.py:287
  87.6 5.1 %collective-permute-start.10 = (bf16[2048,128]{1,0:T(8,128)(2,1)}, bf16[2048,128]{1,0:T(8,128)(2,1)S(1)}, u32[]{:S(2)}, u32[]{:S(2)}) collective-permute-start(bf16[2048,128]{1,0:T(8,128)(2,1)} %bitcast.8), channel_id=1, source_target_pairs={{0,1},{1,0},{2,3},{3,2},{4,5},{5,4},{6,7},{7,6},{8,9},{9,8},{10,11... | collective-permute-start | bytes 1572872 | tf_op jit(solution)/shard_map/ppermute | solution.py:287

commit v5 on v4

--- a/solution.py
+++ b/solution.py
@@ -326,8 +326,9 @@
     none = jnp.zeros_like(near)
     outward = (g_sec + jnp.where(core == 0, near, none)).astype(BF16)
     far = moved(outward, lambda a, b: (a, b + 2))
-    total = g_own + jnp.where(core == 1, near, none) + far.astype(F32)
-    rim = moved(total[:, tile_rows:].astype(BF16), lambda a, b: (a + 1, b))
+    inner = jnp.where(core == 1, near, none)
+    below = g_own[:, tile_rows:] + inner[:, tile_rows:] + far[:, tile_rows:].astype(F32)
+    rim = moved(below.astype(BF16), lambda a, b: (a + 1, b))
 
     groups = [[i for i in range(devices) if i % 2 == c] for c in range(2)]
     exchange = functools.partial(
@@ -345,7 +346,8 @@
     probe_grad = probe_grad.reshape(2, modes, win // 8, 2, 8, LANES).transpose(0, 1, 2, 4, 3, 5)
     probe_grad = probe_grad.reshape(2, modes, win, win)
 
-    object_grad = total[:, :tile_rows] + jnp.pad(rim.astype(F32), ((0, 0), (0, tile_rows - win), (0, 0)))
+    rim = jnp.pad(rim.astype(F32), ((0, 0), (0, tile_rows - win), (0, 0)))
+    object_grad = g_own[:, :tile_rows] + inner[:, :tile_rows] + far[:, :tile_rows].astype(F32) + rim
     return (object_grad, probe_grad)
 
 

time: 96.6 us -> 95.6 us (0.990)
  starting transfers between devices: 41 us -> 46.7 us
  Pallas kernels: 12.1 us -> 7.35 us
    all_to_all x1, starting transfers between devices: 15.3 us -> 26 us  [local(): share = exchange(chip_sum.reshape(devices // 2, -1, LANES))]
    pallas_call x1, Pallas kernels: 11 us -> 6.22 us  [run_slots(): pl.pallas_call(slots_kernel, in_specs=[pl.BlockSpec(memory_space=pltpu.SM...]
    ppermute x11, starting transfers between devices: 20.2 us -> 16.1 us  [moved(): return lax.ppermute(value, ('rows', 'cols'), pairs)]
    all_to_all x1, waiting for transfers between devices: 8.18 us -> 6.75 us  [local(): share = exchange(chip_sum.reshape(devices // 2, -1, LANES))]
    convert_element_type x1, other arithmetic: 2.57 us -> 1.53 us  [local(): jnp.where(part == core, mine[None], swap_cores(mine)[None]).astype(F32)]
    add x2 -> x1, other arithmetic: 2.35 us -> 2.14 us  [local(): g_own[:, :tile_rows] + inner[:, :tile_rows] + far[:, :tile_rows].astype(F32)]
  transfers between devices with their start and end apart: 13 -> 13, of which waited for: 8 -> 7; matrix products, arithmetic and copies ran while one was open for 8% -> 9% of each run, Pallas kernels for 1% -> 1%
where the time goes in v5:
time: 95.6 us; the launch traced here: 95.1 us
  starting transfers between devices  46.7 us (49%)
  waiting for transfers between devices  23.8 us (25%)
  other arithmetic  8.33 us (9%)
  local copies, waits for them, and re-layouts  7.48 us (8%)
  Pallas kernels  7.35 us (8%)
  between operations  1.43 us (1%)
    all_to_all x1, starting transfers between devices, local(): share = exchange(chip_sum.reshape(devices // 2, -1, LANES))  26 us
    ppermute x11, starting transfers between devices, moved(): return lax.ppermute(value, ('rows', 'cols'), pairs)  16.1 us
    ppermute x11, waiting for transfers between devices, moved(): return lax.ppermute(value, ('rows', 'cols'), pairs)  14.4 us
    all_to_all x1, waiting for transfers between devices, local(): share = exchange(chip_sum.reshape(devices // 2, -1, LANES))  6.75 us
    pallas_call x1, Pallas kernels, run_slots(): pl.pallas_call(slots_kernel, in_specs=[pl.BlockSpec(memory_space=pltpu.SM...  6.22 us
    unnamed x18, local copies, waits for them, and re-layouts  5.68 us
    all_to_all x1, starting transfers between devices, local(): exchange(jnp.broadcast_to(share[None], (devices // 2,) + share.shape))  4.69 us
    all_to_all x1, waiting for transfers between devices, local(): exchange(jnp.broadcast_to(share[None], (devices // 2,) + share.shape))  2.62 us
  transfers between devices with their start and end apart: 13, of which 7 were waited for; matrix products, arithmetic and copies ran while one was open for 9% of the time, Pallas kernels for 1%

profile of v5, /device:TPU:1, one launch (start us, length us, event | category | flops | bytes accessed | tf_op | source)
XLA Modules:
  0.0 95.1 jit_solution(16269194430283381268)
XLA Ops:
  0.6 1.3 %collective-permute-start = (bf16[2,1024,128]{2,1,0:T(8,128)(2,1)}, bf16[2,1024,128]{2,1,0:T(8,128)(2,1)S(1)}, u32[]{:S(2)}, u32[]{:S(2)}) collective-permute-start(bf16[2,1024,128]{2,1,0:T(8,128)(2,1)} %own.1), channel_id=1, source_target_pairs={{2,0},{3,1},{4,2},{5,3},{6,4},{7,5},{8,6},{9,7},{10,8},{11,9},{12,... | collective-permute-start | bytes 1572872 | tf_op jit(solution)/shard_map/ppermute | solution.py:287
  1.9 0.9 slice.21
  2.9 1.3 %collective-permute-start.1 = (bf16[2,256,128]{2,1,0:T(8,128)(2,1)S(1)}, bf16[2,256,128]{2,1,0:T(8,128)(2,1)S(1)}, u32[]{:S(2)}, u32[]{:S(2)}) collective-permute-start(bf16[2,256,128]{2,1,0:T(8,128)(2,1)S(1)} %slice.21), channel_id=1, source_target_pairs={{32,0},{33,1},{34,2},{35,3},{36,4},{37,5},{38,6},{39,7},{40,8},{41... | collective-permute-start | bytes 393224 | tf_op jit(solution)/shard_map/ppermute | solution.py:287
  4.2 1.3 %collective-permute-start.3 = (bf16[2,256,128]{2,1,0:T(8,128)(2,1)S(1)}, bf16[2,256,128]{2,1,0:T(8,128)(2,1)S(1)}, u32[]{:S(2)}, u32[]{:S(2)}) collective-permute-start(bf16[2,256,128]{2,1,0:T(8,128)(2,1)S(1)} %slice.21), channel_id=1, source_target_pairs={{34,0},{35,1},{36,2},{37,3},{38,4},{39,5},{40,6},{41,7},{42,8},{43... | collective-permute-start | bytes 393224 | tf_op jit(solution)/shard_map/ppermute | solution.py:287
  5.5 0.0 copy-start.1
  5.5 1.6 %copy-done.1 = f32[2,4,256,256]{3,2,1,0:T(8,128)S(1)} copy-done((f32[2,4,256,256]{3,2,1,0:T(8,128)S(1)}, f32[2,4,256,256]{3,2,1,0:T(8,128)}, u32[]{:S(2)}) %copy-start.1) | copy-done | bytes 2097176
  7.1 0.0 copy-start.2
  7.1 1.2 %copy-done.2 = bf16[1,8,256,256]{3,2,1,0:T(8,128)(2,1)S(1)} copy-done((bf16[1,8,256,256]{3,2,1,0:T(8,128)(2,1)S(1)}, bf16[1,8,256,256]{3,2,1,0:T(8,128)(2,1)}, u32[]{:S(2)}) %copy-start.2) | copy-done | bytes 1048600
  8.3 0.0 copy-start.3
  8.3 0.9 copy-done.3
  9.2 0.0 copy-start.4
  9.2 0.9 copy-done.4
  10.2 0.0 copy-start.5
  10.2 0.9 copy-done.5
  11.1 0.0 copy-start
  11.1 1.1 %prepare.1 = (bf16[2,256,256]{2,1,0:T(8,128)(2,1)S(1)}, bf16[2,256,256]{2,1,0:T(8,128)(2,1)S(1)}, f32[2,4,256,256]{3,2,1,0:T(8,128)S(1)}, bf16[8,256,256]{2,1,0:T(8,128)(2,1)S(1)}) custom-call(bf16[2,256,256]{2,1,0:T(8,128)(2,1)S(1)} %copy-done.3, bf16[2,256,256]{2,1,0:T(8,128)(2,1)S(1)} %copy-done.4, bf16[2,256,256]{2,1,0:T(8,128)(2,1)S(1)} %copy-done.5, ...), custom_call_target="tpu_custom_call" | custom-call | flops 536870912 | bytes 8388608 | tf_op jit(solution)/shard_map/prepare/pallas_call | solution.py:223
  12.3 0.0 copy-start.7
  12.3 0.0 copy-start.8
  12.3 7.4 %collective-permute-done.sec = bf16[2,1024,128]{2,1,0:T(8,128)(2,1)S(1)} collective-permute-done((bf16[2,1024,128]{2,1,0:T(8,128)(2,1)}, bf16[2,1024,128]{2,1,0:T(8,128)(2,1)S(1)}, u32[]{:S(2)}, u32[]{:S(2)}) %collective-permute-start) | collective-permute-done | bytes 524320 | tf_op jit(solution)/shard_map/ppermute | solution.py:287
  19.7 0.0 copy-done
  19.7 0.1 broadcast_select_fusion
  19.7 1.3 %collective-permute-start.2 = (bf16[2,1024,128]{2,1,0:T(8,128)(2,1)S(1)}, bf16[2,1024,128]{2,1,0:T(8,128)(2,1)S(1)}, u32[]{:S(2)}, u32[]{:S(2)}) collective-permute-start(bf16[2,1024,128]{2,1,0:T(8,128)(2,1)S(1)} %broadcast_select_fusion), channel_id=1, source_target_pairs={{0,1},{1,0},{2,3},{3,2},{4,5},{5,4},{6,7},{7,6},{8,9},{9,8},{10,11... | collective-permute-start | bytes 1572872 | tf_op jit(solution)/shard_map/ppermute | solution.py:287
  21.1 0.0 collective-permute-done.1.own_low
  21.1 0.0 collective-permute-done.3.sec_low
  21.1 0.1 collective-permute-start.4
  21.2 0.0 copy-done.7
  21.2 0.0 copy-done.8
  21.9 0.1 pad_add_fusion.info
  21.9 0.8 collective-permute-done.4.nxt_low
  22.8 0.0 collective-permute-done.2.nxt
  22.8 6.2 %slots.1 = (f32[2,1280,128]{2,1,0:T(8,128)S(1)}, bf16[2,1024,128]{2,1,0:T(8,128)(2,1)S(1)}, bf16[2,256,128]{2,1,0:T(8,128)(2,1)S(1)}, f32[2,1280,128]{2,1,0:T(8,...) custom-call(s32[18]{0:T(128)S(1)} %pad_add_fusion.info, ...), custom_call_target="tpu_custom_call" | custom-call | tf_op jit(solution)/shard_map/slots/pallas_call | solution.py:251
  29.0 0.4 collective-permute-start.5
  29.4 0.2 collective-permute-start.6
  29.6 1.4 %collective-permute-done.5 = bf16[2048,128]{1,0:T(8,128)(2,1)S(1)} collective-permute-done((bf16[2048,128]{1,0:T(8,128)(2,1)S(1)}, bf16[2048,128]{1,0:T(8,128)(2,1)S(1)}, u32[]{:S(2)}, u32[]{:S(2)}) %collective-permute-start.5) | collective-permute-done | bytes 524320 | tf_op jit(solution)/shard_map/ppermute | solution.py:287
  31.0 0.9 add_convert_fusion
  31.9 0.0 collective-permute-done.6
  31.9 0.4 collective-permute-start.7
  32.3 26.0 %all-to-all-start = ((bf16[64,32,128]{2,1,0:T(8,128)(2,1)}), bf16[64,32,128]{2,1,0:T(8,128)(2,1)}, u32[]{:S(2)}, u32[]{:S(2)}) async-start(bf16[64,32,128]{2,1,0:T(8,128)(2,1)} %bitcast.4), calls=%async_computation | async-start | bytes 1048576 | tf_op jit(solution)/shard_map/all_to_all | solution.py:338
  58.2 0.0 collective-permute-done.7
  58.2 1.5 %fusion.1 = (bf16[2,1280,128]{2,1,0:T(8,128)(2,1)}, f32[2,1280,128]{2,1,0:T(8,128)}) fusion(f32[2,1280,128]{2,1,0:T(8,128)S(1)} %get-tuple-element.38, pred[]{:T(512)S(6)} %eq.15, bf16[2,256,128]{2,1,0:T(8,128)(2,1)S(1)} %collective-permute-done.7, bf16[2,1024,128]{2,1,0:T(8,128)(2,1)S(1)} %collective-permute-done.6, pred[]{:T(512)S(6)} %eq.16), kind=kLoop, calls=%fused_computation.3 | loop fusion | flops 2621440 | bytes 3932162 | tf_op jit(solution)/shard_map/convert_element_type | solution.py:327
  59.7 0.0 copy-start.6
  59.7 3.8 %collective-permute-start.8 = (bf16[2,1280,128]{2,1,0:T(8,128)(2,1)}, bf16[2,1280,128]{2,1,0:T(8,128)(2,1)}, u32[]{:S(2)}, u32[]{:S(2)}) collective-permute-start(bf16[2,1280,128]{2,1,0:T(8,128)(2,1)} %get-tuple-element.42), channel_id=1, source_target_pairs={{0,2},{1,3},{2,4},{3,5},{4,6},{5,7},{6,8},{7,9},{8,10},{9,11},{10,... | collective-permute-start | bytes 1966088 | tf_op jit(solution)/shard_map/ppermute | solution.py:287
  63.6 6.8 %all-to-all-done = bf16[64,32,128]{2,1,0:T(8,128)(2,1)} async-done(((bf16[64,32,128]{2,1,0:T(8,128)(2,1)}), bf16[64,32,128]{2,1,0:T(8,128)(2,1)}, u32[]{:S(2)}, u32[]{:S(2)}) %all-to-all-start) | async-done | bytes 524320 | tf_op jit(solution)/shard_map/all_to_all | solution.py:338
  70.3 1.1 %convert_reduce_fusion = f32[32,128]{1,0:T(8,128)S(1)} fusion(bf16[64,32,128]{2,1,0:T(8,128)(2,1)} %all-to-all-done), kind=kLoop, calls=%fused_computation.8 | loop fusion | flops 520192 | bytes 540672 | tf_op jit(solution)/shard_map/reduce_sum | solution.py:340
  71.5 0.9 broadcast_in_dim.43
  72.3 4.7 %all-to-all-start.1 = ((bf16[64,32,128]{2,1,0:T(8,128)(2,1)}), bf16[64,32,128]{2,1,0:T(8,128)(2,1)S(1)}, u32[]{:S(2)}, u32[]{:S(2)}) async-start(bf16[64,32,128]{2,1,0:T(8,128)(2,1)} %broadcast_in_dim.43), calls=%async_computation.1 | async-start | bytes 1048576 | tf_op jit(solution)/shard_map/all_to_all | solution.py:341
  77.0 2.8 %collective-permute-done.8 = bf16[2,1280,128]{2,1,0:T(8,128)(2,1)} collective-permute-done((bf16[2,1280,128]{2,1,0:T(8,128)(2,1)}, bf16[2,1280,128]{2,1,0:T(8,128)(2,1)}, u32[]{:S(2)}, u32[]{:S(2)}) %collective-permute-start.8) | collective-permute-done | bytes 655392 | tf_op jit(solution)/shard_map/ppermute | solution.py:287
  79.9 0.0 copy-done.6
  79.9 0.9 fusion.5
  80.8 3.2 %collective-permute-start.9 = (bf16[2,256,128]{2,1,0:T(8,128)(2,1)S(1)}, bf16[2,256,128]{2,1,0:T(8,128)(2,1)S(1)}, u32[]{:S(2)}, u32[]{:S(2)}) collective-permute-start(bf16[2,256,128]{2,1,0:T(8,128)(2,1)S(1)} %fusion.5), channel_id=1, source_target_pairs={{0,32},{1,33},{2,34},{3,35},{4,36},{5,37},{6,38},{7,39},{8,40},{9,... | collective-permute-start | bytes 393224 | tf_op jit(solution)/shard_map/ppermute | solution.py:287
  84.1 2.0 %collective-permute-done.9 = bf16[2,256,128]{2,1,0:T(8,128)(2,1)S(1)} collective-permute-done((bf16[2,256,128]{2,1,0:T(8,128)(2,1)S(1)}, bf16[2,256,128]{2,1,0:T(8,128)(2,1)S(1)}, u32[]{:S(2)}, u32[]{:S(2)}) %collective-permute-start.9) | collective-permute-done | bytes 131104 | tf_op jit(solution)/shard_map/ppermute | solution.py:287
  86.0 2.6 %all-to-all-done.1 = bf16[64,32,128]{2,1,0:T(8,128)(2,1)S(1)} async-done(((bf16[64,32,128]{2,1,0:T(8,128)(2,1)}), bf16[64,32,128]{2,1,0:T(8,128)(2,1)S(1)}, u32[]{:S(2)}, u32[]{:S(2)}) %all-to-all-start.1) | async-done | bytes 524320 | tf_op jit(solution)/shard_map/all_to_all | solution.py:341
  88.7 2.8 %collective-permute-start.10 = (bf16[2048,128]{1,0:T(8,128)(2,1)S(1)}, bf16[2048,128]{1,0:T(8,128)(2,1)S(1)}, u32[]{:S(2)}, u32[]{:S(2)}) collective-permute-start(bf16[2048,128]{1,0:T(8,128)(2,1)S(1)} %bitcast.19), channel_id=1, source_target_pairs={{0,1},{1,0},{2,3},{3,2},{4,5},{5,4},{6,7},{7,6},{8,9},{9,8},{10,11... | collective-permute-start | bytes 1572872 | tf_op jit(solution)/shard_map/ppermute | solution.py:287
  91.4 2.1 %fusion.3 = f32[2,1024,128]{2,1,0:T(8,128)} fusion(f32[2,1280,128]{2,1,0:T(8,128)S(1)} %copy-done.6, f32[2,1280,128]{2,1,0:T(8,128)S(1)} %get-tuple-element.31, bf16[2,1280,128]{2,1,0:T(8,128)(2,1)} %collective-permute-done.8, bf16[2,256,128]{2,1,0:T(8,128)(2,1)S(1)} %collective-permute-done.9), kind=kLoop, calls=%fused_computation.6 | loop fusion | flops 1310720 | bytes 3801088 | tf_op jit(solution)/shard_map/add | solution.py:350
  93.6 0.0 collective-permute-done.10
  93.6 1.5 %select_convert_fusion = f32[2,4,256,256]{3,2,1,0:T(8,128)} fusion(pred[2]{0:T(512)(128)(4,1)S(1)} %iota_compare_fusion, bf16[4,256,256]{2,1,0:T(8,128)(2,1)S(1)} %bitcast.21, bf16[4,256,256]{2,1,0:T(8,128)(2,1)S(1)} %bitcast.20), kind=kLoop, calls=%fused_computation.7 | loop fusion | flops 1048576 | bytes 3145730 | tf_op jit(solution)/shard_map/convert_element_type | solution.py:345
  (4 shorter events, 0.0 us)
Async XLA Ops:
  0.6 19.0 %collective-permute-start = (bf16[2,1024,128]{2,1,0:T(8,128)(2,1)}, bf16[2,1024,128]{2,1,0:T(8,128)(2,1)S(1)}, u32[]{:S(2)}, u32[]{:S(2)}) collective-permute-start(bf16[2,1024,128]{2,1,0:T(8,128)(2,1)} %own.1), channel_id=1, source_target_pairs={{2,0},{3,1},{4,2},{5,3},{6,4},{7,5},{8,6},{9,7},{10,8},{11,9},{12,... | collective-permute-start | bytes 1572872 | tf_op jit(solution)/shard_map/ppermute | solution.py:287
  2.9 18.2 %collective-permute-start.1 = (bf16[2,256,128]{2,1,0:T(8,128)(2,1)S(1)}, bf16[2,256,128]{2,1,0:T(8,128)(2,1)S(1)}, u32[]{:S(2)}, u32[]{:S(2)}) collective-permute-start(bf16[2,256,128]{2,1,0:T(8,128)(2,1)S(1)} %slice.21), channel_id=1, source_target_pairs={{32,0},{33,1},{34,2},{35,3},{36,4},{37,5},{38,6},{39,7},{40,8},{41... | collective-permute-start | bytes 393224 | tf_op jit(solution)/shard_map/ppermute | solution.py:287
  4.2 16.9 %collective-permute-start.3 = (bf16[2,256,128]{2,1,0:T(8,128)(2,1)S(1)}, bf16[2,256,128]{2,1,0:T(8,128)(2,1)S(1)}, u32[]{:S(2)}, u32[]{:S(2)}) collective-permute-start(bf16[2,256,128]{2,1,0:T(8,128)(2,1)S(1)} %slice.21), channel_id=1, source_target_pairs={{34,0},{35,1},{36,2},{37,3},{38,4},{39,5},{40,6},{41,7},{42,8},{43... | collective-permute-start | bytes 393224 | tf_op jit(solution)/shard_map/ppermute | solution.py:287
  5.5 1.6 %copy-start.1 = (f32[2,4,256,256]{3,2,1,0:T(8,128)S(1)}, f32[2,4,256,256]{3,2,1,0:T(8,128)}, u32[]{:S(2)}) copy-start(f32[2,4,256,256]{3,2,1,0:T(8,128)} %probe.1) | copy-start | bytes 6291460
  7.1 1.2 %copy-start.2 = (bf16[1,8,256,256]{3,2,1,0:T(8,128)(2,1)S(1)}, bf16[1,8,256,256]{3,2,1,0:T(8,128)(2,1)}, u32[]{:S(2)}) copy-start(bf16[1,8,256,256]{3,2,1,0:T(8,128)(2,1)} %meas.1) | copy-start | bytes 3145732
  8.3 0.9 copy-start.3
  9.2 0.9 copy-start.4
  10.2 0.9 copy-start.5
  11.1 8.5 %copy-start = (bf16[2,1024,128]{2,1,0:T(8,128)(2,1)S(1)}, bf16[2,1024,128]{2,1,0:T(8,128)(2,1)}, u32[]{:S(2)}) copy-start(bf16[2,1024,128]{2,1,0:T(8,128)(2,1)} %own.1) | copy-start | bytes 1572868
  12.3 8.9 %copy-start.7 = (s32[1,8]{1,0:T(1,128)S(1)}, s32[1,8]{1,0:T(1,128)}, u32[]{:S(2)}) copy-start(s32[1,8]{1,0:T(1,128)} %param.13) | copy-start | bytes 100
  12.3 8.9 %copy-start.8 = (s32[1,8]{1,0:T(1,128)S(1)}, s32[1,8]{1,0:T(1,128)}, u32[]{:S(2)}) copy-start(s32[1,8]{1,0:T(1,128)} %param.12) | copy-start | bytes 100
  19.7 3.1 %collective-permute-start.2 = (bf16[2,1024,128]{2,1,0:T(8,128)(2,1)S(1)}, bf16[2,1024,128]{2,1,0:T(8,128)(2,1)S(1)}, u32[]{:S(2)}, u32[]{:S(2)}) collective-permute-start(bf16[2,1024,128]{2,1,0:T(8,128)(2,1)S(1)} %broadcast_select_fusion), channel_id=1, source_target_pairs={{0,1},{1,0},{2,3},{3,2},{4,5},{5,4},{6,7},{7,6},{8,9},{9,8},{10,11... | collective-permute-start | bytes 1572872 | tf_op jit(solution)/shard_map/ppermute | solution.py:287
  21.1 1.7 %collective-permute-start.4 = (bf16[2,256,128]{2,1,0:T(8,128)(2,1)S(1)}, bf16[2,256,128]{2,1,0:T(8,128)(2,1)S(1)}, u32[]{:S(2)}, u32[]{:S(2)}) collective-permute-start(bf16[2,256,128]{2,1,0:T(8,128)(2,1)S(1)} %broadcast_select_fusion.1), channel_id=1, source_target_pairs={{0,1},{1,0},{2,3},{3,2},{4,5},{5,4},{6,7},{7,6},{8,9},{9,8},{10,11... | collective-permute-start | bytes 393224 | tf_op jit(solution)/shard_map/ppermute | solution.py:287
  29.0 2.0 %collective-permute-start.5 = (bf16[2048,128]{1,0:T(8,128)(2,1)S(1)}, bf16[2048,128]{1,0:T(8,128)(2,1)S(1)}, u32[]{:S(2)}, u32[]{:S(2)}) collective-permute-start(bf16[2048,128]{1,0:T(8,128)(2,1)S(1)} %get-tuple-element.33), channel_id=1, source_target_pairs={{0,1},{1,0},{2,3},{3,2},{4,5},{5,4},{6,7},{7,6},{8,9},{9,8},{10,11... | collective-permute-start | bytes 1572872 | tf_op jit(solution)/shard_map/ppermute | solution.py:287
  29.4 2.5 %collective-permute-start.6 = (bf16[2,1024,128]{2,1,0:T(8,128)(2,1)S(1)}, bf16[2,1024,128]{2,1,0:T(8,128)(2,1)S(1)}, u32[]{:S(2)}, u32[]{:S(2)}) collective-permute-start(bf16[2,1024,128]{2,1,0:T(8,128)(2,1)S(1)} %get-tuple-element.34), channel_id=1, source_target_pairs={{0,1},{1,0},{2,3},{3,2},{4,5},{5,4},{6,7},{7,6},{8,9},{9,8},{10,11... | collective-permute-start | bytes 1572872 | tf_op jit(solution)/shard_map/ppermute | solution.py:287
  31.9 26.3 %collective-permute-start.7 = (bf16[2,256,128]{2,1,0:T(8,128)(2,1)S(1)}, bf16[2,256,128]{2,1,0:T(8,128)(2,1)S(1)}, u32[]{:S(2)}, u32[]{:S(2)}) collective-permute-start(bf16[2,256,128]{2,1,0:T(8,128)(2,1)S(1)} %get-tuple-element.37), channel_id=1, source_target_pairs={{0,1},{1,0},{2,3},{3,2},{4,5},{5,4},{6,7},{7,6},{8,9},{9,8},{10,11... | collective-permute-start | bytes 393224 | tf_op jit(solution)/shard_map/ppermute | solution.py:287
  32.3 38.1 %all-to-all-start = ((bf16[64,32,128]{2,1,0:T(8,128)(2,1)}), bf16[64,32,128]{2,1,0:T(8,128)(2,1)}, u32[]{:S(2)}, u32[]{:S(2)}) async-start(bf16[64,32,128]{2,1,0:T(8,128)(2,1)} %bitcast.4), calls=%async_computation | async-start | bytes 1048576 | tf_op jit(solution)/shard_map/all_to_all | solution.py:338
  59.7 20.1 %copy-start.6 = (f32[2,1280,128]{2,1,0:T(8,128)S(1)}, f32[2,1280,128]{2,1,0:T(8,128)}, u32[]{:S(2)}) copy-start(f32[2,1280,128]{2,1,0:T(8,128)} %get-tuple-element.43) | copy-start | bytes 3932164
  59.7 20.1 %collective-permute-start.8 = (bf16[2,1280,128]{2,1,0:T(8,128)(2,1)}, bf16[2,1280,128]{2,1,0:T(8,128)(2,1)}, u32[]{:S(2)}, u32[]{:S(2)}) collective-permute-start(bf16[2,1280,128]{2,1,0:T(8,128)(2,1)} %get-tuple-element.42), channel_id=1, source_target_pairs={{0,2},{1,3},{2,4},{3,5},{4,6},{5,7},{6,8},{7,9},{8,10},{9,11},{10,... | collective-permute-start | bytes 1966088 | tf_op jit(solution)/shard_map/ppermute | solution.py:287
  72.3 16.3 %all-to-all-start.1 = ((bf16[64,32,128]{2,1,0:T(8,128)(2,1)}), bf16[64,32,128]{2,1,0:T(8,128)(2,1)S(1)}, u32[]{:S(2)}, u32[]{:S(2)}) async-start(bf16[64,32,128]{2,1,0:T(8,128)(2,1)} %broadcast_in_dim.43), calls=%async_computation.1 | async-start | bytes 1048576 | tf_op jit(solution)/shard_map/all_to_all | solution.py:341
  80.8 5.2 %collective-permute-start.9 = (bf16[2,256,128]{2,1,0:T(8,128)(2,1)S(1)}, bf16[2,256,128]{2,1,0:T(8,128)(2,1)S(1)}, u32[]{:S(2)}, u32[]{:S(2)}) collective-permute-start(bf16[2,256,128]{2,1,0:T(8,128)(2,1)S(1)} %fusion.5), channel_id=1, source_target_pairs={{0,32},{1,33},{2,34},{3,35},{4,36},{5,37},{6,38},{7,39},{8,40},{9,... | collective-permute-start | bytes 393224 | tf_op jit(solution)/shard_map/ppermute | solution.py:287
  88.7 4.9 %collective-permute-start.10 = (bf16[2048,128]{1,0:T(8,128)(2,1)S(1)}, bf16[2048,128]{1,0:T(8,128)(2,1)S(1)}, u32[]{:S(2)}, u32[]{:S(2)}) collective-permute-start(bf16[2048,128]{1,0:T(8,128)(2,1)S(1)} %bitcast.19), channel_id=1, source_target_pairs={{0,1},{1,0},{2,3},{3,2},{4,5},{5,4},{6,7},{7,6},{8,9},{9,8},{10,11... | collective-permute-start | bytes 1572872 | tf_op jit(solution)/shard_map/ppermute | solution.py:287

commit v6 on v4

--- a/solution.py
+++ b/solution.py
@@ -82,7 +82,7 @@
                     for h in range(2):
                         owin[q, c, h, at : at + CHUNK, :] = jnp.where(keep_left[q], parts[h], parts[h + 1])
 
-        for m in range(modes):
+        def exit_waves(m):
             for at in range(0, half, CHUNK):
                 for h in range(2):
                     psi = ([], [])
@@ -98,57 +98,71 @@
                             rows = slice(c * half + at, c * half + at + CHUNK)
                             xs[q, m, 0, rows, sides[h]] = (psi[q][0][c] + psi[q][1][c]).astype(BF16)
                             xs[q, m, 1, rows, sides[h]] = (psi[q][0][c] - psi[q][1][c]).astype(BF16)
-            for q in range(2):
-                for rp in range(2):
-                    v = jnp.dot(fwd[rp], xs[q, m, rp], preferred_element_type=F32)
-                    v = (
-                        (v[:, :half] + v[:, half:]).astype(BF16),
-                        (v[:, :half] - v[:, half:]).astype(BF16),
-                    )
+
+        def half_products(job):
+            m, q = job
+            if q == 0:
+                exit_waves(m)
+            return [jnp.dot(fwd[rp], xs[q, m, rp], preferred_element_type=F32) for rp in range(2)]
+
+        def keep_half_done(job, values):
+            m, q = job
+            for rp, v in enumerate(values):
+                v = (
+                    (v[:, :half] + v[:, half:]).astype(BF16),
+                    (v[:, :half] - v[:, half:]).astype(BF16),
+                )
+                for pc in range(2):
+                    for at in range(0, half, BLOCK):
+                        for c in range(2):
+                            hb[
+                                q, pc, (rp * half + at) // BLOCK, m * BLOCK : (m + 1) * BLOCK, sides[c]
+                            ] = v[pc][c * half + at : c * half + at + BLOCK]
+
+        def far_products(job):
+            rb, pc, q = job
+            return jnp.dot(hb[q, pc, rb], bwd[pc], preferred_element_type=F32)
+
+        def correct(job, field):
+            rb, pc, q = job
+            for at in range(0, BLOCK, CHUNK):
+                part = [field[m * BLOCK + at : m * BLOCK + at + CHUNK] for m in range(modes)]
+                total = 1.0
+                for f in part:
+                    total = total + (f[:, :half] * f[:, :half] + f[:, half:] * f[:, half:])
+                f_row = rb * BLOCK + at
+                factor = 1.0 - meas[slot[q], f_row : f_row + CHUNK, sides[pc]].astype(F32) * lax.rsqrt(total)
+                if q == 1:
+                    factor = factor * weight[q]
+                rp, f_row = divmod(f_row, half)
+                for m in range(modes):
+                    for c in range(2):
+                        gb[q, m, rp, c * half + f_row : c * half + f_row + CHUNK, sides[pc]] = (
+                            part[m][:, sides[c]] * factor
+                        ).astype(BF16)
+
+        def back_products(job):
+            m, q = job
+            return [jnp.dot(bwd[rp], gb[q, m, rp], preferred_element_type=F32) for rp in range(2)]
+
+        def keep_back_half(job, values):
+            m, q = job
+            v0, v1 = values
+            for side, v in enumerate(((v0 + v1).astype(BF16), (v0 - v1).astype(BF16))):
+                for at in range(0, half, BLOCK):
                     for pc in range(2):
-                        for at in range(0, half, BLOCK):
-                            for c in range(2):
-                                hb[
-                                    q, pc, (rp * half + at) // BLOCK, m * BLOCK : (m + 1) * BLOCK, sides[c]
-                                ] = v[pc][c * half + at : c * half + at + BLOCK]
-
-        for rb in range(blocks):
-            for pc in range(2):
-                for q in range(2):
-                    field = jnp.dot(hb[q, pc, rb], bwd[pc], preferred_element_type=F32)
-                    for at in range(0, BLOCK, CHUNK):
-                        part = [field[m * BLOCK + at : m * BLOCK + at + CHUNK] for m in range(modes)]
-                        total = 1.0
-                        for f in part:
-                            total = total + (f[:, :half] * f[:, :half] + f[:, half:] * f[:, half:])
-                        f_row = rb * BLOCK + at
-                        factor = 1.0 - meas[slot[q], f_row : f_row + CHUNK, sides[pc]].astype(F32) * lax.rsqrt(total)
-                        if q == 1:
-                            factor = factor * weight[q]
-                        rp, f_row = divmod(f_row, half)
-                        for m in range(modes):
-                            for c in range(2):
-                                gb[q, m, rp, c * half + f_row : c * half + f_row + CHUNK, sides[pc]] = (
-                                    part[m][:, sides[c]] * factor
-                                ).astype(BF16)
-
-        for m in range(modes):
-            for q in range(2):
-                v0 = jnp.dot(bwd[0], gb[q, m, 0], preferred_element_type=F32)
-                v1 = jnp.dot(bwd[1], gb[q, m, 1], preferred_element_type=F32)
-                for side, v in enumerate(((v0 + v1).astype(BF16), (v0 - v1).astype(BF16))):
-                    for at in range(0, half, BLOCK):
-                        for pc in range(2):
-                            for c in range(2):
-                                kb[
-                                    q, pc, (side * half + at) // BLOCK, m * BLOCK : (m + 1) * BLOCK, sides[c]
-                                ] = v[c * half + at : c * half + at + BLOCK, sides[pc]]
-
-        for rb in range(blocks):
-            w = [
+                        for c in range(2):
+                            kb[
+                                q, pc, (side * half + at) // BLOCK, m * BLOCK : (m + 1) * BLOCK, sides[c]
+                            ] = v[c * half + at : c * half + at + BLOCK, sides[pc]]
+
+        def chi_products(rb):
+            return [
                 [jnp.dot(kb[q, pc, rb], fwd[pc], preferred_element_type=F32) for pc in range(2)]
                 for q in range(2)
             ]
+
+        def gather_up(rb, w):
             for at in range(0, BLOCK, CHUNK):
                 rows = slice(rb * BLOCK + at, rb * BLOCK + at + CHUNK)
                 g = [[[None, None], [None, None]] for q in range(2)]
@@ -183,6 +197,21 @@
                         )
                         for t in range(3):
                             sums[t][c, pl.ds(row[q] + rows.start, CHUNK), :] += spread[t]
+
+        def one_ahead(jobs, products, use):
+            ready = products(jobs[0])
+            for n, job in enumerate(jobs):
+                later = products(jobs[n + 1]) if n + 1 < len(jobs) else None
+                use(job, ready)
+                ready = later
+
+        by_mode = [(m, q) for m in range(modes) for q in range(2)]
+        one_ahead(by_mode, half_products, keep_half_done)
+        one_ahead(
+            [(rb, pc, q) for rb in range(blocks) for pc in range(2) for q in range(2)], far_products, correct
+        )
+        one_ahead(by_mode, back_products, keep_back_half)
+        one_ahead(list(range(blocks)), chi_products, gather_up)
         return 0
 
     lax.fori_loop(0, lax.div(live + 1, 2), pair_of_slots, 0)

time: 96.6 us -> 95.7 us (level); the launches traced: 95.3 us -> 95.8 us
  starting transfers between devices: 41 us -> 46.2 us
  Pallas kernels: 12.1 us -> 7.39 us
    ppermute x11, starting transfers between devices: 20.2 us -> 29.8 us  [moved(): return lax.ppermute(value, ('rows', 'cols'), pairs)]
    pallas_call x1, Pallas kernels: 11 us -> 6.26 us  [run_slots(): pl.pallas_call(slots_kernel, in_specs=[pl.BlockSpec(memory_space=pltpu.SM...]
    all_to_all x1, starting transfers between devices: 15.3 us -> 10.9 us  [local(): share = exchange(chip_sum.reshape(devices // 2, -1, LANES))]
where the time goes in v6:
time: 95.7 us; the launch traced here: 95.8 us
  starting transfers between devices  46.2 us (48%)
  waiting for transfers between devices  24.3 us (25%)
  local copies, waits for them, and re-layouts  8.31 us (9%)
  other arithmetic  8.13 us (8%)
  Pallas kernels  7.39 us (8%)
  between operations  1.44 us (2%)
    ppermute x11, starting transfers between devices, moved(): return lax.ppermute(value, ('rows', 'cols'), pairs)  29.8 us
    ppermute x11, waiting for transfers between devices, moved(): return lax.ppermute(value, ('rows', 'cols'), pairs)  13.8 us
    all_to_all x1, starting transfers between devices, local(): share = exchange(chip_sum.reshape(devices // 2, -1, LANES))  10.9 us
    all_to_all x1, waiting for transfers between devices, local(): share = exchange(chip_sum.reshape(devices // 2, -1, LANES))  8.18 us
    unnamed x18, local copies, waits for them, and re-layouts  6.51 us
    pallas_call x1, Pallas kernels, run_slots(): pl.pallas_call(slots_kernel, in_specs=[pl.BlockSpec(memory_space=pltpu.SM...  6.26 us
    all_to_all x1, starting transfers between devices, local(): exchange(jnp.broadcast_to(share[None], (devices // 2,) + share.shape))  5.49 us
    convert_element_type x1, other arithmetic, local(): jnp.where(part == core, mine[None], swap_cores(mine)[None]).astype(F32)  2.57 us
  transfers between devices with their start and end apart: 13, of which 8 were waited for; matrix products, arithmetic and copies ran while one was open for 8% of the time, Pallas kernels for 1%

profile of v6, /device:TPU:1, one launch (start us, length us, event | category | flops | bytes accessed | tf_op | source)
XLA Modules:
  0.0 95.8 jit_solution(17215910623246934227)
XLA Ops:
  0.6 1.3 %collective-permute-start = (bf16[2,1024,128]{2,1,0:T(8,128)(2,1)}, bf16[2,1024,128]{2,1,0:T(8,128)(2,1)S(1)}, u32[]{:S(2)}, u32[]{:S(2)}) collective-permute-start(bf16[2,1024,128]{2,1,0:T(8,128)(2,1)} %own.1), channel_id=1, source_target_pairs={{2,0},{3,1},{4,2},{5,3},{6,4},{7,5},{8,6},{9,7},{10,8},{11,9},{12,... | collective-permute-start | bytes 1572872 | tf_op jit(solution)/shard_map/ppermute | solution.py:316
  1.9 0.9 slice.10
  2.9 1.3 %collective-permute-start.1 = (bf16[2,256,128]{2,1,0:T(8,128)(2,1)S(1)}, bf16[2,256,128]{2,1,0:T(8,128)(2,1)S(1)}, u32[]{:S(2)}, u32[]{:S(2)}) collective-permute-start(bf16[2,256,128]{2,1,0:T(8,128)(2,1)S(1)} %slice.10), channel_id=1, source_target_pairs={{32,0},{33,1},{34,2},{35,3},{36,4},{37,5},{38,6},{39,7},{40,8},{41... | collective-permute-start | bytes 393224 | tf_op jit(solution)/shard_map/ppermute | solution.py:316
  4.2 1.3 %collective-permute-start.3 = (bf16[2,256,128]{2,1,0:T(8,128)(2,1)S(1)}, bf16[2,256,128]{2,1,0:T(8,128)(2,1)S(1)}, u32[]{:S(2)}, u32[]{:S(2)}) collective-permute-start(bf16[2,256,128]{2,1,0:T(8,128)(2,1)S(1)} %slice.10), channel_id=1, source_target_pairs={{34,0},{35,1},{36,2},{37,3},{38,4},{39,5},{40,6},{41,7},{42,8},{43... | collective-permute-start | bytes 393224 | tf_op jit(solution)/shard_map/ppermute | solution.py:316
  5.5 0.0 copy-start.1
  5.5 1.6 %copy-done.1 = f32[2,4,256,256]{3,2,1,0:T(8,128)S(1)} copy-done((f32[2,4,256,256]{3,2,1,0:T(8,128)S(1)}, f32[2,4,256,256]{3,2,1,0:T(8,128)}, u32[]{:S(2)}) %copy-start.1) | copy-done | bytes 2097176
  7.1 0.0 copy-start.2
  7.1 1.2 %copy-done.2 = bf16[1,8,256,256]{3,2,1,0:T(8,128)(2,1)S(1)} copy-done((bf16[1,8,256,256]{3,2,1,0:T(8,128)(2,1)S(1)}, bf16[1,8,256,256]{3,2,1,0:T(8,128)(2,1)}, u32[]{:S(2)}) %copy-start.2) | copy-done | bytes 1048600
  8.3 0.0 copy-start.3
  8.3 0.9 copy-done.3
  9.2 0.0 copy-start.4
  9.2 0.9 copy-done.4
  10.2 0.0 copy-start.5
  10.2 0.9 copy-done.5
  11.1 0.0 copy-start
  11.1 1.1 %prepare.1 = (bf16[2,256,256]{2,1,0:T(8,128)(2,1)S(1)}, bf16[2,256,256]{2,1,0:T(8,128)(2,1)S(1)}, f32[2,4,256,256]{3,2,1,0:T(8,128)S(1)}, bf16[8,256,256]{2,1,0:T(8,128)(2,1)S(1)}) custom-call(bf16[2,256,256]{2,1,0:T(8,128)(2,1)S(1)} %copy-done.3, bf16[2,256,256]{2,1,0:T(8,128)(2,1)S(1)} %copy-done.4, bf16[2,256,256]{2,1,0:T(8,128)(2,1)S(1)} %copy-done.5, ...), custom_call_target="tpu_custom_call" | custom-call | flops 536870912 | bytes 8388608 | tf_op jit(solution)/shard_map/prepare/pallas_call | solution.py:252
  12.3 0.0 copy-start.7
  12.3 0.0 copy-start.8
  12.3 7.4 %collective-permute-done.sec = bf16[2,1024,128]{2,1,0:T(8,128)(2,1)S(1)} collective-permute-done((bf16[2,1024,128]{2,1,0:T(8,128)(2,1)}, bf16[2,1024,128]{2,1,0:T(8,128)(2,1)S(1)}, u32[]{:S(2)}, u32[]{:S(2)}) %collective-permute-start) | collective-permute-done | bytes 524320 | tf_op jit(solution)/shard_map/ppermute | solution.py:316
  19.7 0.0 copy-done
  19.7 0.1 broadcast_select_fusion
  19.7 1.3 %collective-permute-start.2 = (bf16[2,1024,128]{2,1,0:T(8,128)(2,1)S(1)}, bf16[2,1024,128]{2,1,0:T(8,128)(2,1)S(1)}, u32[]{:S(2)}, u32[]{:S(2)}) collective-permute-start(bf16[2,1024,128]{2,1,0:T(8,128)(2,1)S(1)} %broadcast_select_fusion), channel_id=1, source_target_pairs={{0,1},{1,0},{2,3},{3,2},{4,5},{5,4},{6,7},{7,6},{8,9},{9,8},{10,11... | collective-permute-start | bytes 1572872 | tf_op jit(solution)/shard_map/ppermute | solution.py:316
  21.0 0.0 collective-permute-done.1.own_low
  21.0 0.0 collective-permute-done.3.sec_low
  21.1 0.1 collective-permute-start.4
  21.2 0.0 copy-done.7
  21.2 0.0 copy-done.8
  21.8 0.1 pad_add_fusion.info
  21.9 0.8 collective-permute-done.4.nxt_low
  22.8 0.0 collective-permute-done.2.nxt
  22.8 6.3 %slots.1 = (f32[2,1280,128]{2,1,0:T(8,128)S(1)}, bf16[2,1024,128]{2,1,0:T(8,128)(2,1)S(1)}, bf16[2,256,128]{2,1,0:T(8,128)(2,1)S(1)}, f32[2,1280,128]{2,1,0:T(8,...) custom-call(s32[18]{0:T(128)S(1)} %pad_add_fusion.info, ...), custom_call_target="tpu_custom_call" | custom-call | tf_op jit(solution)/shard_map/slots/pallas_call | solution.py:280
  29.0 14.9 %collective-permute-start.5 = (bf16[2048,128]{1,0:T(8,128)(2,1)S(1)}, bf16[2048,128]{1,0:T(8,128)(2,1)S(1)}, u32[]{:S(2)}, u32[]{:S(2)}) collective-permute-start(bf16[2048,128]{1,0:T(8,128)(2,1)S(1)} %get-tuple-element.33), channel_id=1, source_target_pairs={{0,1},{1,0},{2,3},{3,2},{4,5},{5,4},{6,7},{7,6},{8,9},{9,8},{10,11... | collective-permute-start | bytes 1572872 | tf_op jit(solution)/shard_map/ppermute | solution.py:316
  43.9 0.1 collective-permute-start.6
  44.0 1.4 %collective-permute-done.5 = bf16[2048,128]{1,0:T(8,128)(2,1)S(1)} collective-permute-done((bf16[2048,128]{1,0:T(8,128)(2,1)S(1)}, bf16[2048,128]{1,0:T(8,128)(2,1)S(1)}, u32[]{:S(2)}, u32[]{:S(2)}) %collective-permute-start.5) | collective-permute-done | bytes 524320 | tf_op jit(solution)/shard_map/ppermute | solution.py:316
  45.5 0.9 add_convert_fusion
  46.4 0.0 collective-permute-done.6
  46.4 0.4 collective-permute-start.7
  46.8 10.9 %all-to-all-start = ((bf16[64,32,128]{2,1,0:T(8,128)(2,1)}), bf16[64,32,128]{2,1,0:T(8,128)(2,1)}, u32[]{:S(2)}, u32[]{:S(2)}) async-start(bf16[64,32,128]{2,1,0:T(8,128)(2,1)} %bitcast.19), calls=%async_computation | async-start | bytes 1048576 | tf_op jit(solution)/shard_map/all_to_all | solution.py:366
  57.7 0.0 collective-permute-done.7
  57.7 1.0 %fusion.3 = bf16[2,1280,128]{2,1,0:T(8,128)(2,1)} fusion(f32[2,1280,128]{2,1,0:T(8,128)S(1)} %get-tuple-element.38, pred[]{:T(512)S(6)} %eq.15, bf16[2,256,128]{2,1,0:T(8,128)(2,1)S(1)} %collective-permute-done.7, bf16[2,1024,128]{2,1,0:T(8,128)(2,1)S(1)} %collective-permute-done.6), kind=kLoop, calls=%fused_computation.5 | loop fusion | flops 2293760 | bytes 2621441 | tf_op jit(solution)/shard_map/convert_element_type | solution.py:356
  58.7 2.9 %collective-permute-start.8 = (bf16[2,1280,128]{2,1,0:T(8,128)(2,1)}, bf16[2,1280,128]{2,1,0:T(8,128)(2,1)S(1)}, u32[]{:S(2)}, u32[]{:S(2)}) collective-permute-start(bf16[2,1280,128]{2,1,0:T(8,128)(2,1)} %fusion.3), channel_id=1, source_target_pairs={{0,2},{1,3},{2,4},{3,5},{4,6},{5,7},{6,8},{7,9},{8,10},{9,11},{10,... | collective-permute-start | bytes 1966088 | tf_op jit(solution)/shard_map/ppermute | solution.py:316
  61.6 8.2 %all-to-all-done = bf16[64,32,128]{2,1,0:T(8,128)(2,1)} async-done(((bf16[64,32,128]{2,1,0:T(8,128)(2,1)}), bf16[64,32,128]{2,1,0:T(8,128)(2,1)}, u32[]{:S(2)}, u32[]{:S(2)}) %all-to-all-start) | async-done | bytes 524320 | tf_op jit(solution)/shard_map/all_to_all | solution.py:366
  69.8 1.1 %convert_reduce_fusion = f32[32,128]{1,0:T(8,128)S(1)} fusion(bf16[64,32,128]{2,1,0:T(8,128)(2,1)} %all-to-all-done), kind=kLoop, calls=%fused_computation.8 | loop fusion | flops 520192 | bytes 540672 | tf_op jit(solution)/shard_map/reduce_sum | solution.py:368
  70.9 0.9 broadcast_in_dim.43
  71.8 5.5 %all-to-all-start.1 = ((bf16[64,32,128]{2,1,0:T(8,128)(2,1)}), bf16[64,32,128]{2,1,0:T(8,128)(2,1)}, u32[]{:S(2)}, u32[]{:S(2)}) async-start(bf16[64,32,128]{2,1,0:T(8,128)(2,1)} %broadcast_in_dim.43), calls=%async_computation.1 | async-start | bytes 1048576 | tf_op jit(solution)/shard_map/all_to_all | solution.py:369
  77.3 1.2 %collective-permute-done.8 = bf16[2,1280,128]{2,1,0:T(8,128)(2,1)S(1)} collective-permute-done((bf16[2,1280,128]{2,1,0:T(8,128)(2,1)}, bf16[2,1280,128]{2,1,0:T(8,128)(2,1)S(1)}, u32[]{:S(2)}, u32[]{:S(2)}) %collective-permute-start.8) | collective-permute-done | bytes 655392 | tf_op jit(solution)/shard_map/ppermute | solution.py:316
  78.5 0.0 copy-start.6
  78.5 0.8 copy-done.6
  79.3 1.3 %fusion.1 = f32[2,1280,128]{2,1,0:T(8,128)S(1)} fusion(f32[2,1280,128]{2,1,0:T(8,128)S(1)} %get-tuple-element.31, bf16[2,1280,128]{2,1,0:T(8,128)(2,1)} %copy-done.6, pred[]{:T(512)S(6)} %eq.16, bf16[2,256,128]{2,1,0:T(8,128)(2,1)S(1)} %collective-permute-done.7, bf16[2,1024,128]{2,1,0:T(8,128)(2,1)S(1)} %collective-permute-done.6), kind=kLoop, calls=%fused_computation.3 | loop fusion | flops 2621440 | bytes 3932161 | tf_op jit(solution)/shard_map/add | solution.py:358
  80.6 2.8 %collective-permute-start.9 = (bf16[2,256,128]{2,1,0:T(8,128)(2,1)S(1)}, bf16[2,256,128]{2,1,0:T(8,128)(2,1)S(1)}, u32[]{:S(2)}, u32[]{:S(2)}) collective-permute-start(bf16[2,256,128]{2,1,0:T(8,128)(2,1)S(1)} %slice.17), channel_id=1, source_target_pairs={{0,32},{1,33},{2,34},{3,35},{4,36},{5,37},{6,38},{7,39},{8,40},{9,... | collective-permute-start | bytes 393224 | tf_op jit(solution)/shard_map/ppermute | solution.py:316
  83.5 2.2 %collective-permute-done.9 = bf16[2,256,128]{2,1,0:T(8,128)(2,1)S(1)} collective-permute-done((bf16[2,256,128]{2,1,0:T(8,128)(2,1)S(1)}, bf16[2,256,128]{2,1,0:T(8,128)(2,1)S(1)}, u32[]{:S(2)}, u32[]{:S(2)}) %collective-permute-start.9) | collective-permute-done | bytes 131104 | tf_op jit(solution)/shard_map/ppermute | solution.py:316
  85.7 2.3 %all-to-all-done.1 = bf16[64,32,128]{2,1,0:T(8,128)(2,1)} async-done(((bf16[64,32,128]{2,1,0:T(8,128)(2,1)}), bf16[64,32,128]{2,1,0:T(8,128)(2,1)}, u32[]{:S(2)}, u32[]{:S(2)}) %all-to-all-start.1) | async-done | bytes 524320 | tf_op jit(solution)/shard_map/all_to_all | solution.py:369
  88.1 3.4 %collective-permute-start.10 = (bf16[2048,128]{1,0:T(8,128)(2,1)}, bf16[2048,128]{1,0:T(8,128)(2,1)S(1)}, u32[]{:S(2)}, u32[]{:S(2)}) collective-permute-start(bf16[2048,128]{1,0:T(8,128)(2,1)} %bitcast.8), channel_id=1, source_target_pairs={{0,1},{1,0},{2,3},{3,2},{4,5},{5,4},{6,7},{7,6},{8,9},{9,8},{10,11... | collective-permute-start | bytes 1572872 | tf_op jit(solution)/shard_map/ppermute | solution.py:316
  91.5 1.0 %slice_add_fusion = f32[2,1024,128]{2,1,0:T(8,128)} fusion(f32[2,1280,128]{2,1,0:T(8,128)S(1)} %fusion.1, bf16[2,256,128]{2,1,0:T(8,128)(2,1)S(1)} %collective-permute-done.9), kind=kLoop, calls=%fused_computation.6 | loop fusion | flops 524288 | bytes 2228224 | tf_op jit(solution)/shard_map/add | solution.py:377
  92.5 0.7 collective-permute-done.10
  93.2 2.6 %select_convert_fusion = f32[2,4,256,256]{3,2,1,0:T(8,128)} fusion(pred[2]{0:T(512)(128)(4,1)S(1)} %iota_compare_fusion, bf16[4,256,256]{2,1,0:T(8,128)(2,1)S(1)} %bitcast.20, bf16[4,256,256]{2,1,0:T(8,128)(2,1)} %bitcast.7), kind=kLoop, calls=%fused_computation.7 | loop fusion | flops 1048576 | bytes 3145730 | tf_op jit(solution)/shard_map/convert_element_type | solution.py:373
  (5 shorter events, 0.1 us)
Async XLA Ops:
  0.6 19.0 %collective-permute-start = (bf16[2,1024,128]{2,1,0:T(8,128)(2,1)}, bf16[2,1024,128]{2,1,0:T(8,128)(2,1)S(1)}, u32[]{:S(2)}, u32[]{:S(2)}) collective-permute-start(bf16[2,1024,128]{2,1,0:T(8,128)(2,1)} %own.1), channel_id=1, source_target_pairs={{2,0},{3,1},{4,2},{5,3},{6,4},{7,5},{8,6},{9,7},{10,8},{11,9},{12,... | collective-permute-start | bytes 1572872 | tf_op jit(solution)/shard_map/ppermute | solution.py:316
  2.9 18.2 %collective-permute-start.1 = (bf16[2,256,128]{2,1,0:T(8,128)(2,1)S(1)}, bf16[2,256,128]{2,1,0:T(8,128)(2,1)S(1)}, u32[]{:S(2)}, u32[]{:S(2)}) collective-permute-start(bf16[2,256,128]{2,1,0:T(8,128)(2,1)S(1)} %slice.10), channel_id=1, source_target_pairs={{32,0},{33,1},{34,2},{35,3},{36,4},{37,5},{38,6},{39,7},{40,8},{41... | collective-permute-start | bytes 393224 | tf_op jit(solution)/shard_map/ppermute | solution.py:316
  4.2 16.9 %collective-permute-start.3 = (bf16[2,256,128]{2,1,0:T(8,128)(2,1)S(1)}, bf16[2,256,128]{2,1,0:T(8,128)(2,1)S(1)}, u32[]{:S(2)}, u32[]{:S(2)}) collective-permute-start(bf16[2,256,128]{2,1,0:T(8,128)(2,1)S(1)} %slice.10), channel_id=1, source_target_pairs={{34,0},{35,1},{36,2},{37,3},{38,4},{39,5},{40,6},{41,7},{42,8},{43... | collective-permute-start | bytes 393224 | tf_op jit(solution)/shard_map/ppermute | solution.py:316
  5.5 1.6 %copy-start.1 = (f32[2,4,256,256]{3,2,1,0:T(8,128)S(1)}, f32[2,4,256,256]{3,2,1,0:T(8,128)}, u32[]{:S(2)}) copy-start(f32[2,4,256,256]{3,2,1,0:T(8,128)} %probe.1) | copy-start | bytes 6291460
  7.1 1.2 %copy-start.2 = (bf16[1,8,256,256]{3,2,1,0:T(8,128)(2,1)S(1)}, bf16[1,8,256,256]{3,2,1,0:T(8,128)(2,1)}, u32[]{:S(2)}) copy-start(bf16[1,8,256,256]{3,2,1,0:T(8,128)(2,1)} %meas.1) | copy-start | bytes 3145732
  8.3 0.9 copy-start.3
  9.2 0.9 copy-start.4
  10.2 0.9 copy-start.5
  11.1 8.5 %copy-start = (bf16[2,1024,128]{2,1,0:T(8,128)(2,1)S(1)}, bf16[2,1024,128]{2,1,0:T(8,128)(2,1)}, u32[]{:S(2)}) copy-start(bf16[2,1024,128]{2,1,0:T(8,128)(2,1)} %own.1) | copy-start | bytes 1572868
  12.3 8.9 %copy-start.7 = (s32[1,8]{1,0:T(1,128)S(1)}, s32[1,8]{1,0:T(1,128)}, u32[]{:S(2)}) copy-start(s32[1,8]{1,0:T(1,128)} %param.13) | copy-start | bytes 100
  12.3 8.9 %copy-start.8 = (s32[1,8]{1,0:T(1,128)S(1)}, s32[1,8]{1,0:T(1,128)}, u32[]{:S(2)}) copy-start(s32[1,8]{1,0:T(1,128)} %param.12) | copy-start | bytes 100
  19.7 3.1 %collective-permute-start.2 = (bf16[2,1024,128]{2,1,0:T(8,128)(2,1)S(1)}, bf16[2,1024,128]{2,1,0:T(8,128)(2,1)S(1)}, u32[]{:S(2)}, u32[]{:S(2)}) collective-permute-start(bf16[2,1024,128]{2,1,0:T(8,128)(2,1)S(1)} %broadcast_select_fusion), channel_id=1, source_target_pairs={{0,1},{1,0},{2,3},{3,2},{4,5},{5,4},{6,7},{7,6},{8,9},{9,8},{10,11... | collective-permute-start | bytes 1572872 | tf_op jit(solution)/shard_map/ppermute | solution.py:316
  21.1 1.7 %collective-permute-start.4 = (bf16[2,256,128]{2,1,0:T(8,128)(2,1)S(1)}, bf16[2,256,128]{2,1,0:T(8,128)(2,1)S(1)}, u32[]{:S(2)}, u32[]{:S(2)}) collective-permute-start(bf16[2,256,128]{2,1,0:T(8,128)(2,1)S(1)} %broadcast_select_fusion.1), channel_id=1, source_target_pairs={{0,1},{1,0},{2,3},{3,2},{4,5},{5,4},{6,7},{7,6},{8,9},{9,8},{10,11... | collective-permute-start | bytes 393224 | tf_op jit(solution)/shard_map/ppermute | solution.py:316
  29.0 16.4 %collective-permute-start.5 = (bf16[2048,128]{1,0:T(8,128)(2,1)S(1)}, bf16[2048,128]{1,0:T(8,128)(2,1)S(1)}, u32[]{:S(2)}, u32[]{:S(2)}) collective-permute-start(bf16[2048,128]{1,0:T(8,128)(2,1)S(1)} %get-tuple-element.33), channel_id=1, source_target_pairs={{0,1},{1,0},{2,3},{3,2},{4,5},{5,4},{6,7},{7,6},{8,9},{9,8},{10,11... | collective-permute-start | bytes 1572872 | tf_op jit(solution)/shard_map/ppermute | solution.py:316
  43.9 2.4 %collective-permute-start.6 = (bf16[2,1024,128]{2,1,0:T(8,128)(2,1)S(1)}, bf16[2,1024,128]{2,1,0:T(8,128)(2,1)S(1)}, u32[]{:S(2)}, u32[]{:S(2)}) collective-permute-start(bf16[2,1024,128]{2,1,0:T(8,128)(2,1)S(1)} %get-tuple-element.34), channel_id=1, source_target_pairs={{0,1},{1,0},{2,3},{3,2},{4,5},{5,4},{6,7},{7,6},{8,9},{9,8},{10,11... | collective-permute-start | bytes 1572872 | tf_op jit(solution)/shard_map/ppermute | solution.py:316
  46.4 11.3 %collective-permute-start.7 = (bf16[2,256,128]{2,1,0:T(8,128)(2,1)S(1)}, bf16[2,256,128]{2,1,0:T(8,128)(2,1)S(1)}, u32[]{:S(2)}, u32[]{:S(2)}) collective-permute-start(bf16[2,256,128]{2,1,0:T(8,128)(2,1)S(1)} %get-tuple-element.37), channel_id=1, source_target_pairs={{0,1},{1,0},{2,3},{3,2},{4,5},{5,4},{6,7},{7,6},{8,9},{9,8},{10,11... | collective-permute-start | bytes 393224 | tf_op jit(solution)/shard_map/ppermute | solution.py:316
  46.8 23.0 %all-to-all-start = ((bf16[64,32,128]{2,1,0:T(8,128)(2,1)}), bf16[64,32,128]{2,1,0:T(8,128)(2,1)}, u32[]{:S(2)}, u32[]{:S(2)}) async-start(bf16[64,32,128]{2,1,0:T(8,128)(2,1)} %bitcast.19), calls=%async_computation | async-start | bytes 1048576 | tf_op jit(solution)/shard_map/all_to_all | solution.py:366
  58.7 19.7 %collective-permute-start.8 = (bf16[2,1280,128]{2,1,0:T(8,128)(2,1)}, bf16[2,1280,128]{2,1,0:T(8,128)(2,1)S(1)}, u32[]{:S(2)}, u32[]{:S(2)}) collective-permute-start(bf16[2,1280,128]{2,1,0:T(8,128)(2,1)} %fusion.3), channel_id=1, source_target_pairs={{0,2},{1,3},{2,4},{3,5},{4,6},{5,7},{6,8},{7,9},{8,10},{9,11},{10,... | collective-permute-start | bytes 1966088 | tf_op jit(solution)/shard_map/ppermute | solution.py:316
  71.8 16.3 %all-to-all-start.1 = ((bf16[64,32,128]{2,1,0:T(8,128)(2,1)}), bf16[64,32,128]{2,1,0:T(8,128)(2,1)}, u32[]{:S(2)}, u32[]{:S(2)}) async-start(bf16[64,32,128]{2,1,0:T(8,128)(2,1)} %broadcast_in_dim.43), calls=%async_computation.1 | async-start | bytes 1048576 | tf_op jit(solution)/shard_map/all_to_all | solution.py:369
  78.5 0.8 copy-start.6
  80.6 5.1 %collective-permute-start.9 = (bf16[2,256,128]{2,1,0:T(8,128)(2,1)S(1)}, bf16[2,256,128]{2,1,0:T(8,128)(2,1)S(1)}, u32[]{:S(2)}, u32[]{:S(2)}) collective-permute-start(bf16[2,256,128]{2,1,0:T(8,128)(2,1)S(1)} %slice.17), channel_id=1, source_target_pairs={{0,32},{1,33},{2,34},{3,35},{4,36},{5,37},{6,38},{7,39},{8,40},{9,... | collective-permute-start | bytes 393224 | tf_op jit(solution)/shard_map/ppermute | solution.py:316
  88.1 5.1 %collective-permute-start.10 = (bf16[2048,128]{1,0:T(8,128)(2,1)}, bf16[2048,128]{1,0:T(8,128)(2,1)S(1)}, u32[]{:S(2)}, u32[]{:S(2)}) collective-permute-start(bf16[2048,128]{1,0:T(8,128)(2,1)} %bitcast.8), channel_id=1, source_target_pairs={{0,1},{1,0},{2,3},{3,2},{4,5},{5,4},{6,7},{7,6},{8,9},{9,8},{10,11... | collective-permute-start | bytes 1572872 | tf_op jit(solution)/shard_map/ppermute | solution.py:316

commit v7 on v4

--- a/solution.py
+++ b/solution.py
@@ -322,7 +322,7 @@
     near = swap_cores(g_next)
     chip_sum = (acc_keep + acc_got.astype(F32)).astype(BF16)
     chip_sum, near, near_low = lax.optimization_barrier((chip_sum, near, g_next_low))
-    near = jnp.concatenate([near, swap_cores(near_low)], axis=1).astype(F32)
+    near = lax.optimization_barrier(jnp.concatenate([near, swap_cores(near_low)], axis=1).astype(F32))
     none = jnp.zeros_like(near)
     outward = (g_sec + jnp.where(core == 0, near, none)).astype(BF16)
     far = moved(outward, lambda a, b: (a, b + 2))

time: 96.6 us -> 99.2 us (1.027)
  Pallas kernels: 12.1 us -> 7.33 us
  starting transfers between devices: 41 us -> 45.7 us
  waiting for transfers between devices: 24.3 us -> 25.8 us
    all_to_all x1, starting transfers between devices: 15.3 us -> 25.3 us  [local(): share = exchange(chip_sum.reshape(devices // 2, -1, LANES))]
    ppermute x11, waiting for transfers between devices: 13.8 us -> 19.5 us  [moved(): return lax.ppermute(value, ('rows', 'cols'), pairs)]
    pallas_call x1, Pallas kernels: 11 us -> 6.2 us  [run_slots(): pl.pallas_call(slots_kernel, in_specs=[pl.BlockSpec(memory_space=pltpu.SM...]
    ppermute x11, starting transfers between devices: 20.2 us -> 15.7 us  [moved(): return lax.ppermute(value, ('rows', 'cols'), pairs)]
    all_to_all x1, waiting for transfers between devices: 2.34 us -> 0.01 us  [local(): exchange(jnp.broadcast_to(share[None], (devices // 2,) + share.shape))]
    all_to_all x1, waiting for transfers between devices: 8.18 us -> 6.31 us  [local(): share = exchange(chip_sum.reshape(devices // 2, -1, LANES))]
    add x1, other arithmetic: 1.04 us -> 2.27 us  [local(): total[:, :tile_rows]]
    convert_element_type x0 -> x1, other arithmetic: none -> 1.13 us  [local(): jnp.concatenate([near, swap_cores(near_low)], axis=1).astype(F32)]
  transfers between devices with their start and end apart: 13 -> 13, of which waited for: 8 -> 6; matrix products, arithmetic and copies ran while one was open for 8% -> 9% of each run, Pallas kernels for 1% -> 1%
where the time goes in v7:
time: 99.2 us; the launch traced here: 97.9 us
  starting transfers between devices  45.7 us (46%)
  waiting for transfers between devices  25.8 us (26%)
  local copies, waits for them, and re-layouts  8.97 us (9%)
  other arithmetic  8.63 us (9%)
  Pallas kernels  7.33 us (7%)
  between operations  1.45 us (1%)
    all_to_all x1, starting transfers between devices, local(): share = exchange(chip_sum.reshape(devices // 2, -1, LANES))  25.3 us
    ppermute x11, waiting for transfers between devices, moved(): return lax.ppermute(value, ('rows', 'cols'), pairs)  19.5 us
    ppermute x11, starting transfers between devices, moved(): return lax.ppermute(value, ('rows', 'cols'), pairs)  15.7 us
    unnamed x24, local copies, waits for them, and re-layouts  7.15 us
    all_to_all x1, waiting for transfers between devices, local(): share = exchange(chip_sum.reshape(devices // 2, -1, LANES))  6.31 us
    pallas_call x1, Pallas kernels, run_slots(): pl.pallas_call(slots_kernel, in_specs=[pl.BlockSpec(memory_space=pltpu.SM...  6.2 us
    all_to_all x1, starting transfers between devices, local(): exchange(jnp.broadcast_to(share[None], (devices // 2,) + share.shape))  4.69 us
    add x1, other arithmetic, local(): total[:, :tile_rows]  2.27 us
  transfers between devices with their start and end apart: 13, of which 6 were waited for; matrix products, arithmetic and copies ran while one was open for 9% of the time, Pallas kernels for 1%

profile of v7, /device:TPU:1, one launch (start us, length us, event | category | flops | bytes accessed | tf_op | source)
XLA Modules:
  0.0 97.9 jit_solution(16541146054180110150)
XLA Ops:
  0.6 1.3 %collective-permute-start = (bf16[2,1024,128]{2,1,0:T(8,128)(2,1)}, bf16[2,1024,128]{2,1,0:T(8,128)(2,1)S(1)}, u32[]{:S(2)}, u32[]{:S(2)}) collective-permute-start(bf16[2,1024,128]{2,1,0:T(8,128)(2,1)} %own.1), channel_id=1, source_target_pairs={{2,0},{3,1},{4,2},{5,3},{6,4},{7,5},{8,6},{9,7},{10,8},{11,9},{12,... | collective-permute-start | bytes 1572872 | tf_op jit(solution)/shard_map/ppermute | solution.py:287
  1.9 0.9 slice.10
  2.9 1.3 %collective-permute-start.1 = (bf16[2,256,128]{2,1,0:T(8,128)(2,1)S(1)}, bf16[2,256,128]{2,1,0:T(8,128)(2,1)S(1)}, u32[]{:S(2)}, u32[]{:S(2)}) collective-permute-start(bf16[2,256,128]{2,1,0:T(8,128)(2,1)S(1)} %slice.10), channel_id=1, source_target_pairs={{32,0},{33,1},{34,2},{35,3},{36,4},{37,5},{38,6},{39,7},{40,8},{41... | collective-permute-start | bytes 393224 | tf_op jit(solution)/shard_map/ppermute | solution.py:287
  4.2 1.3 %collective-permute-start.3 = (bf16[2,256,128]{2,1,0:T(8,128)(2,1)S(1)}, bf16[2,256,128]{2,1,0:T(8,128)(2,1)S(1)}, u32[]{:S(2)}, u32[]{:S(2)}) collective-permute-start(bf16[2,256,128]{2,1,0:T(8,128)(2,1)S(1)} %slice.10), channel_id=1, source_target_pairs={{34,0},{35,1},{36,2},{37,3},{38,4},{39,5},{40,6},{41,7},{42,8},{43... | collective-permute-start | bytes 393224 | tf_op jit(solution)/shard_map/ppermute | solution.py:287
  5.5 0.0 copy-start.1
  5.5 1.6 %copy-done.1 = f32[2,4,256,256]{3,2,1,0:T(8,128)S(1)} copy-done((f32[2,4,256,256]{3,2,1,0:T(8,128)S(1)}, f32[2,4,256,256]{3,2,1,0:T(8,128)}, u32[]{:S(2)}) %copy-start.1) | copy-done | bytes 2097176
  7.1 0.0 copy-start.2
  7.1 1.2 %copy-done.2 = bf16[1,8,256,256]{3,2,1,0:T(8,128)(2,1)S(1)} copy-done((bf16[1,8,256,256]{3,2,1,0:T(8,128)(2,1)S(1)}, bf16[1,8,256,256]{3,2,1,0:T(8,128)(2,1)}, u32[]{:S(2)}) %copy-start.2) | copy-done | bytes 1048600
  8.3 0.0 copy-start.3
  8.3 0.9 copy-done.3
  9.2 0.0 copy-start.4
  9.2 0.9 copy-done.4
  10.2 0.0 copy-start.5
  10.2 0.9 copy-done.5
  11.1 0.0 copy-start
  11.1 1.1 %prepare.1 = (bf16[2,256,256]{2,1,0:T(8,128)(2,1)S(1)}, bf16[2,256,256]{2,1,0:T(8,128)(2,1)S(1)}, f32[2,4,256,256]{3,2,1,0:T(8,128)S(1)}, bf16[8,256,256]{2,1,0:T(8,128)(2,1)S(1)}) custom-call(bf16[2,256,256]{2,1,0:T(8,128)(2,1)S(1)} %copy-done.3, bf16[2,256,256]{2,1,0:T(8,128)(2,1)S(1)} %copy-done.4, bf16[2,256,256]{2,1,0:T(8,128)(2,1)S(1)} %copy-done.5, ...), custom_call_target="tpu_custom_call" | custom-call | flops 536870912 | bytes 8388608 | tf_op jit(solution)/shard_map/prepare/pallas_call | solution.py:223
  12.3 0.0 copy-start.10
  12.3 0.0 copy-start.11
  12.3 7.4 %collective-permute-done.sec = bf16[2,1024,128]{2,1,0:T(8,128)(2,1)S(1)} collective-permute-done((bf16[2,1024,128]{2,1,0:T(8,128)(2,1)}, bf16[2,1024,128]{2,1,0:T(8,128)(2,1)S(1)}, u32[]{:S(2)}, u32[]{:S(2)}) %collective-permute-start) | collective-permute-done | bytes 524320 | tf_op jit(solution)/shard_map/ppermute | solution.py:287
  19.7 0.0 copy-done
  19.7 0.1 broadcast_select_fusion
  19.7 1.3 %collective-permute-start.2 = (bf16[2,1024,128]{2,1,0:T(8,128)(2,1)S(1)}, bf16[2,1024,128]{2,1,0:T(8,128)(2,1)S(1)}, u32[]{:S(2)}, u32[]{:S(2)}) collective-permute-start(bf16[2,1024,128]{2,1,0:T(8,128)(2,1)S(1)} %broadcast_select_fusion), channel_id=1, source_target_pairs={{0,1},{1,0},{2,3},{3,2},{4,5},{5,4},{6,7},{7,6},{8,9},{9,8},{10,11... | collective-permute-start | bytes 1572872 | tf_op jit(solution)/shard_map/ppermute | solution.py:287
  21.0 0.0 collective-permute-done.1.own_low
  21.0 0.0 collective-permute-done.3.sec_low
  21.1 0.1 collective-permute-start.4
  21.2 0.0 copy-done.10
  21.2 0.0 copy-done.11
  21.8 0.1 pad_add_fusion.info
  21.9 0.8 collective-permute-done.4.nxt_low
  22.8 0.0 collective-permute-done.2.nxt
  22.8 6.2 %slots.1 = (f32[2,1280,128]{2,1,0:T(8,128)S(1)}, bf16[2,1024,128]{2,1,0:T(8,128)(2,1)S(1)}, bf16[2,256,128]{2,1,0:T(8,128)(2,1)S(1)}, f32[2,1280,128]{2,1,0:T(8,...) custom-call(s32[18]{0:T(128)S(1)} %pad_add_fusion.info, ...), custom_call_target="tpu_custom_call" | custom-call | tf_op jit(solution)/shard_map/slots/pallas_call | solution.py:251
  29.0 0.5 collective-permute-start.5
  29.5 0.1 collective-permute-start.6
  29.6 1.4 %collective-permute-done.5 = bf16[2048,128]{1,0:T(8,128)(2,1)S(1)} collective-permute-done((bf16[2048,128]{1,0:T(8,128)(2,1)S(1)}, bf16[2048,128]{1,0:T(8,128)(2,1)S(1)}, u32[]{:S(2)}, u32[]{:S(2)}) %collective-permute-start.5) | collective-permute-done | bytes 524320 | tf_op jit(solution)/shard_map/ppermute | solution.py:287
  31.0 0.9 add_convert_fusion.1
  31.9 0.0 collective-permute-done.6
  31.9 0.0 copy-start.9
  31.9 0.4 collective-permute-start.7
  32.3 0.4 copy-done.9
  32.7 25.3 %all-to-all-start = ((bf16[64,32,128]{2,1,0:T(8,128)(2,1)}), bf16[64,32,128]{2,1,0:T(8,128)(2,1)S(1)}, u32[]{:S(2)}, u32[]{:S(2)}) async-start(bf16[64,32,128]{2,1,0:T(8,128)(2,1)} %bitcast.21), calls=%async_computation | async-start | bytes 1048576 | tf_op jit(solution)/shard_map/all_to_all | solution.py:337
  58.0 0.0 collective-permute-done.7
  58.0 1.1 %maximum_convert_fusion = f32[2,1280,128]{2,1,0:T(8,128)S(1)} fusion(bf16[2,256,128]{2,1,0:T(8,128)(2,1)S(1)} %collective-permute-done.7, bf16[2,1024,128]{2,1,0:T(8,128)(2,1)} %copy-done.9), kind=kLoop, calls=%fused_computation.6 | loop fusion | flops 1310720 | bytes 1966080 | tf_op jit(solution)/shard_map/convert_element_type | solution.py:325
  59.1 0.0 copy-start.6
  59.2 1.3 %add_convert_fusion = bf16[2,1280,128]{2,1,0:T(8,128)(2,1)} fusion(f32[2,1280,128]{2,1,0:T(8,128)S(1)} %get-tuple-element.38, f32[2,1280,128]{2,1,0:T(8,128)S(1)} %maximum_convert_fusion, pred[]{:T(512)S(6)} %eq.15), kind=kLoop, calls=%fused_computation.1 | loop fusion | flops 983040 | bytes 3276801 | tf_op jit(solution)/shard_map/convert_element_type | solution.py:327
  60.4 0.0 copy-done.6
  60.4 3.8 %collective-permute-start.8 = (bf16[2,1280,128]{2,1,0:T(8,128)(2,1)}, bf16[2,1280,128]{2,1,0:T(8,128)(2,1)}, u32[]{:S(2)}, u32[]{:S(2)}) collective-permute-start(bf16[2,1280,128]{2,1,0:T(8,128)(2,1)} %add_convert_fusion), channel_id=1, source_target_pairs={{0,2},{1,3},{2,4},{3,5},{4,6},{5,7},{6,8},{7,9},{8,10},{9,11},{10,... | collective-permute-start | bytes 1966088 | tf_op jit(solution)/shard_map/ppermute | solution.py:287
  64.2 0.0 copy-start.7
  64.2 6.3 %all-to-all-done = bf16[64,32,128]{2,1,0:T(8,128)(2,1)S(1)} async-done(((bf16[64,32,128]{2,1,0:T(8,128)(2,1)}), bf16[64,32,128]{2,1,0:T(8,128)(2,1)S(1)}, u32[]{:S(2)}, u32[]{:S(2)}) %all-to-all-start) | async-done | bytes 524320 | tf_op jit(solution)/shard_map/all_to_all | solution.py:337
  70.5 0.1 convert_reduce_fusion
  70.6 0.9 broadcast_in_dim.43
  71.5 4.7 %all-to-all-start.1 = ((bf16[64,32,128]{2,1,0:T(8,128)(2,1)}), bf16[64,32,128]{2,1,0:T(8,128)(2,1)S(1)}, u32[]{:S(2)}, u32[]{:S(2)}) async-start(bf16[64,32,128]{2,1,0:T(8,128)(2,1)} %broadcast_in_dim.43), calls=%async_computation.1 | async-start | bytes 1048576 | tf_op jit(solution)/shard_map/all_to_all | solution.py:340
  76.2 7.9 %collective-permute-done.8 = bf16[2,1280,128]{2,1,0:T(8,128)(2,1)} collective-permute-done((bf16[2,1280,128]{2,1,0:T(8,128)(2,1)}, bf16[2,1280,128]{2,1,0:T(8,128)(2,1)}, u32[]{:S(2)}, u32[]{:S(2)}) %collective-permute-start.8) | collective-permute-done | bytes 655392 | tf_op jit(solution)/shard_map/ppermute | solution.py:287
  84.1 0.0 copy-done.7
  84.1 1.3 %convert_add_fusion = f32[2,1280,128]{2,1,0:T(8,128)S(1)} fusion(bf16[2,1280,128]{2,1,0:T(8,128)(2,1)} %collective-permute-done.8, f32[2,1280,128]{2,1,0:T(8,128)S(1)} %get-tuple-element.31, f32[2,1280,128]{2,1,0:T(8,128)S(1)} %copy-done.7, pred[]{:T(512)S(6)} %eq.16), kind=kLoop, calls=%fused_computation | loop fusion | flops 1310720 | bytes 4587521 | tf_op jit(solution)/shard_map/add | solution.py:329
  85.4 0.0 copy-start.8
  85.4 1.0 %copy-done.8 = f32[2,1280,128]{2,1,0:T(8,128)} copy-done((f32[2,1280,128]{2,1,0:T(8,128)}, f32[2,1280,128]{2,1,0:T(8,128)S(1)}, u32[]{:S(2)}) %copy-start.8) | copy-done | bytes 1310744
  86.5 3.6 %collective-permute-start.9 = (bf16[2,256,128]{2,1,0:T(8,128)(2,1)S(1)}, bf16[2,256,128]{2,1,0:T(8,128)(2,1)S(1)}, u32[]{:S(2)}, u32[]{:S(2)}) collective-permute-start(bf16[2,256,128]{2,1,0:T(8,128)(2,1)S(1)} %slice.17), channel_id=1, source_target_pairs={{0,32},{1,33},{2,34},{3,35},{4,36},{5,37},{6,38},{7,39},{8,40},{9,... | collective-permute-start | bytes 393224 | tf_op jit(solution)/shard_map/ppermute | solution.py:287
  90.0 1.9 %collective-permute-done.9 = bf16[2,256,128]{2,1,0:T(8,128)(2,1)S(1)} collective-permute-done((bf16[2,256,128]{2,1,0:T(8,128)(2,1)S(1)}, bf16[2,256,128]{2,1,0:T(8,128)(2,1)S(1)}, u32[]{:S(2)}, u32[]{:S(2)}) %collective-permute-start.9) | collective-permute-done | bytes 131104 | tf_op jit(solution)/shard_map/ppermute | solution.py:287
  91.9 0.0 all-to-all-done.1
  91.9 2.1 %collective-permute-start.10 = (bf16[2048,128]{1,0:T(8,128)(2,1)S(1)}, bf16[2048,128]{1,0:T(8,128)(2,1)S(1)}, u32[]{:S(2)}, u32[]{:S(2)}) collective-permute-start(bf16[2048,128]{1,0:T(8,128)(2,1)S(1)} %bitcast.19), channel_id=1, source_target_pairs={{0,1},{1,0},{2,3},{3,2},{4,5},{5,4},{6,7},{7,6},{8,9},{9,8},{10,11... | collective-permute-start | bytes 1572872 | tf_op jit(solution)/shard_map/ppermute | solution.py:287
  94.1 2.3 %slice_add_fusion = f32[2,1024,128]{2,1,0:T(8,128)} fusion(f32[2,1280,128]{2,1,0:T(8,128)} %copy-done.8, bf16[2,256,128]{2,1,0:T(8,128)(2,1)S(1)} %collective-permute-done.9), kind=kLoop, calls=%fused_computation.2 | loop fusion | flops 524288 | bytes 2228224 | tf_op jit(solution)/shard_map/add | solution.py:348
  96.3 0.0 collective-permute-done.10
  96.3 1.5 %select_convert_fusion = f32[2,4,256,256]{3,2,1,0:T(8,128)} fusion(pred[2]{0:T(512)(128)(4,1)S(1)} %iota_compare_fusion, bf16[4,256,256]{2,1,0:T(8,128)(2,1)S(1)} %bitcast.22, bf16[4,256,256]{2,1,0:T(8,128)(2,1)S(1)} %bitcast.20), kind=kLoop, calls=%fused_computation.3 | loop fusion | flops 1048576 | bytes 3145730 | tf_op jit(solution)/shard_map/convert_element_type | solution.py:344
  (5 shorter events, 0.1 us)
Async XLA Ops:
  0.6 19.0 %collective-permute-start = (bf16[2,1024,128]{2,1,0:T(8,128)(2,1)}, bf16[2,1024,128]{2,1,0:T(8,128)(2,1)S(1)}, u32[]{:S(2)}, u32[]{:S(2)}) collective-permute-start(bf16[2,1024,128]{2,1,0:T(8,128)(2,1)} %own.1), channel_id=1, source_target_pairs={{2,0},{3,1},{4,2},{5,3},{6,4},{7,5},{8,6},{9,7},{10,8},{11,9},{12,... | collective-permute-start | bytes 1572872 | tf_op jit(solution)/shard_map/ppermute | solution.py:287
  2.9 18.2 %collective-permute-start.1 = (bf16[2,256,128]{2,1,0:T(8,128)(2,1)S(1)}, bf16[2,256,128]{2,1,0:T(8,128)(2,1)S(1)}, u32[]{:S(2)}, u32[]{:S(2)}) collective-permute-start(bf16[2,256,128]{2,1,0:T(8,128)(2,1)S(1)} %slice.10), channel_id=1, source_target_pairs={{32,0},{33,1},{34,2},{35,3},{36,4},{37,5},{38,6},{39,7},{40,8},{41... | collective-permute-start | bytes 393224 | tf_op jit(solution)/shard_map/ppermute | solution.py:287
  4.2 16.9 %collective-permute-start.3 = (bf16[2,256,128]{2,1,0:T(8,128)(2,1)S(1)}, bf16[2,256,128]{2,1,0:T(8,128)(2,1)S(1)}, u32[]{:S(2)}, u32[]{:S(2)}) collective-permute-start(bf16[2,256,128]{2,1,0:T(8,128)(2,1)S(1)} %slice.10), channel_id=1, source_target_pairs={{34,0},{35,1},{36,2},{37,3},{38,4},{39,5},{40,6},{41,7},{42,8},{43... | collective-permute-start | bytes 393224 | tf_op jit(solution)/shard_map/ppermute | solution.py:287
  5.5 1.6 %copy-start.1 = (f32[2,4,256,256]{3,2,1,0:T(8,128)S(1)}, f32[2,4,256,256]{3,2,1,0:T(8,128)}, u32[]{:S(2)}) copy-start(f32[2,4,256,256]{3,2,1,0:T(8,128)} %probe.1) | copy-start | bytes 6291460
  7.1 1.2 %copy-start.2 = (bf16[1,8,256,256]{3,2,1,0:T(8,128)(2,1)S(1)}, bf16[1,8,256,256]{3,2,1,0:T(8,128)(2,1)}, u32[]{:S(2)}) copy-start(bf16[1,8,256,256]{3,2,1,0:T(8,128)(2,1)} %meas.1) | copy-start | bytes 3145732
  8.3 0.9 copy-start.3
  9.2 0.9 copy-start.4
  10.2 0.9 copy-start.5
  11.1 8.5 %copy-start = (bf16[2,1024,128]{2,1,0:T(8,128)(2,1)S(1)}, bf16[2,1024,128]{2,1,0:T(8,128)(2,1)}, u32[]{:S(2)}) copy-start(bf16[2,1024,128]{2,1,0:T(8,128)(2,1)} %own.1) | copy-start | bytes 1572868
  12.3 8.9 %copy-start.10 = (s32[1,8]{1,0:T(1,128)S(1)}, s32[1,8]{1,0:T(1,128)}, u32[]{:S(2)}) copy-start(s32[1,8]{1,0:T(1,128)} %param.13) | copy-start | bytes 100
  12.3 8.9 %copy-start.11 = (s32[1,8]{1,0:T(1,128)S(1)}, s32[1,8]{1,0:T(1,128)}, u32[]{:S(2)}) copy-start(s32[1,8]{1,0:T(1,128)} %param.12) | copy-start | bytes 100
  19.7 3.1 %collective-permute-start.2 = (bf16[2,1024,128]{2,1,0:T(8,128)(2,1)S(1)}, bf16[2,1024,128]{2,1,0:T(8,128)(2,1)S(1)}, u32[]{:S(2)}, u32[]{:S(2)}) collective-permute-start(bf16[2,1024,128]{2,1,0:T(8,128)(2,1)S(1)} %broadcast_select_fusion), channel_id=1, source_target_pairs={{0,1},{1,0},{2,3},{3,2},{4,5},{5,4},{6,7},{7,6},{8,9},{9,8},{10,11... | collective-permute-start | bytes 1572872 | tf_op jit(solution)/shard_map/ppermute | solution.py:287
  21.1 1.7 %collective-permute-start.4 = (bf16[2,256,128]{2,1,0:T(8,128)(2,1)S(1)}, bf16[2,256,128]{2,1,0:T(8,128)(2,1)S(1)}, u32[]{:S(2)}, u32[]{:S(2)}) collective-permute-start(bf16[2,256,128]{2,1,0:T(8,128)(2,1)S(1)} %broadcast_select_fusion.1), channel_id=1, source_target_pairs={{0,1},{1,0},{2,3},{3,2},{4,5},{5,4},{6,7},{7,6},{8,9},{9,8},{10,11... | collective-permute-start | bytes 393224 | tf_op jit(solution)/shard_map/ppermute | solution.py:287
  29.0 2.0 %collective-permute-start.5 = (bf16[2048,128]{1,0:T(8,128)(2,1)S(1)}, bf16[2048,128]{1,0:T(8,128)(2,1)S(1)}, u32[]{:S(2)}, u32[]{:S(2)}) collective-permute-start(bf16[2048,128]{1,0:T(8,128)(2,1)S(1)} %get-tuple-element.33), channel_id=1, source_target_pairs={{0,1},{1,0},{2,3},{3,2},{4,5},{5,4},{6,7},{7,6},{8,9},{9,8},{10,11... | collective-permute-start | bytes 1572872 | tf_op jit(solution)/shard_map/ppermute | solution.py:287
  29.5 2.5 %collective-permute-start.6 = (bf16[2,1024,128]{2,1,0:T(8,128)(2,1)S(1)}, bf16[2,1024,128]{2,1,0:T(8,128)(2,1)S(1)}, u32[]{:S(2)}, u32[]{:S(2)}) collective-permute-start(bf16[2,1024,128]{2,1,0:T(8,128)(2,1)S(1)} %get-tuple-element.34), channel_id=1, source_target_pairs={{0,1},{1,0},{2,3},{3,2},{4,5},{5,4},{6,7},{7,6},{8,9},{9,8},{10,11... | collective-permute-start | bytes 1572872 | tf_op jit(solution)/shard_map/ppermute | solution.py:287
  31.9 0.8 copy-start.9
  31.9 26.1 %collective-permute-start.7 = (bf16[2,256,128]{2,1,0:T(8,128)(2,1)S(1)}, bf16[2,256,128]{2,1,0:T(8,128)(2,1)S(1)}, u32[]{:S(2)}, u32[]{:S(2)}) collective-permute-start(bf16[2,256,128]{2,1,0:T(8,128)(2,1)S(1)} %get-tuple-element.37), channel_id=1, source_target_pairs={{0,1},{1,0},{2,3},{3,2},{4,5},{5,4},{6,7},{7,6},{8,9},{9,8},{10,11... | collective-permute-start | bytes 393224 | tf_op jit(solution)/shard_map/ppermute | solution.py:287
  32.7 37.8 %all-to-all-start = ((bf16[64,32,128]{2,1,0:T(8,128)(2,1)}), bf16[64,32,128]{2,1,0:T(8,128)(2,1)S(1)}, u32[]{:S(2)}, u32[]{:S(2)}) async-start(bf16[64,32,128]{2,1,0:T(8,128)(2,1)} %bitcast.21), calls=%async_computation | async-start | bytes 1048576 | tf_op jit(solution)/shard_map/all_to_all | solution.py:337
  59.1 1.3 %copy-start.6 = (f32[2,1280,128]{2,1,0:T(8,128)}, f32[2,1280,128]{2,1,0:T(8,128)S(1)}, u32[]{:S(2)}) copy-start(f32[2,1280,128]{2,1,0:T(8,128)S(1)} %maximum_convert_fusion) | copy-start | bytes 3932164
  60.4 23.7 %collective-permute-start.8 = (bf16[2,1280,128]{2,1,0:T(8,128)(2,1)}, bf16[2,1280,128]{2,1,0:T(8,128)(2,1)}, u32[]{:S(2)}, u32[]{:S(2)}) collective-permute-start(bf16[2,1280,128]{2,1,0:T(8,128)(2,1)} %add_convert_fusion), channel_id=1, source_target_pairs={{0,2},{1,3},{2,4},{3,5},{4,6},{5,7},{6,8},{7,9},{8,10},{9,11},{10,... | collective-permute-start | bytes 1966088 | tf_op jit(solution)/shard_map/ppermute | solution.py:287
  64.2 19.9 %copy-start.7 = (f32[2,1280,128]{2,1,0:T(8,128)S(1)}, f32[2,1280,128]{2,1,0:T(8,128)}, u32[]{:S(2)}) copy-start(f32[2,1280,128]{2,1,0:T(8,128)} %copy-done.6) | copy-start | bytes 3932164
  71.5 20.5 %all-to-all-start.1 = ((bf16[64,32,128]{2,1,0:T(8,128)(2,1)}), bf16[64,32,128]{2,1,0:T(8,128)(2,1)S(1)}, u32[]{:S(2)}, u32[]{:S(2)}) async-start(bf16[64,32,128]{2,1,0:T(8,128)(2,1)} %broadcast_in_dim.43), calls=%async_computation.1 | async-start | bytes 1048576 | tf_op jit(solution)/shard_map/all_to_all | solution.py:340
  85.4 1.1 %copy-start.8 = (f32[2,1280,128]{2,1,0:T(8,128)}, f32[2,1280,128]{2,1,0:T(8,128)S(1)}, u32[]{:S(2)}) copy-start(f32[2,1280,128]{2,1,0:T(8,128)S(1)} %convert_add_fusion) | copy-start | bytes 3932164
  86.5 5.5 %collective-permute-start.9 = (bf16[2,256,128]{2,1,0:T(8,128)(2,1)S(1)}, bf16[2,256,128]{2,1,0:T(8,128)(2,1)S(1)}, u32[]{:S(2)}, u32[]{:S(2)}) collective-permute-start(bf16[2,256,128]{2,1,0:T(8,128)(2,1)S(1)} %slice.17), channel_id=1, source_target_pairs={{0,32},{1,33},{2,34},{3,35},{4,36},{5,37},{6,38},{7,39},{8,40},{9,... | collective-permute-start | bytes 393224 | tf_op jit(solution)/shard_map/ppermute | solution.py:287
  91.9 4.4 %collective-permute-start.10 = (bf16[2048,128]{1,0:T(8,128)(2,1)S(1)}, bf16[2048,128]{1,0:T(8,128)(2,1)S(1)}, u32[]{:S(2)}, u32[]{:S(2)}) collective-permute-start(bf16[2048,128]{1,0:T(8,128)(2,1)S(1)} %bitcast.19), channel_id=1, source_target_pairs={{0,1},{1,0},{2,3},{3,2},{4,5},{5,4},{6,7},{7,6},{8,9},{9,8},{10,11... | collective-permute-start | bytes 1572872 | tf_op jit(solution)/shard_map/ppermute | solution.py:287
